TPU v7x, 32 devices: a whole 2x2x4 slice. The times are simulated.
32 devices in a mesh: role: 2 (over core), exp: 4 (over z), tp: 4 (over y, x).
Axes of the slice: x: 2, y: 2, z: 4, core: 2. Of those that a mesh axis runs over, the one named last changes fastest.
Arguments:
- residual_in: bfloat16 [256, 8192], P(('role', 'exp', 'tp')), may hold values from -64 to 64
- context: bfloat16 [256, 8192], P(('role', 'exp'), 'tp'), may hold values from -6 to 6
- out_weight: bfloat16 [8192, 8192], P('tp', ('role', 'exp')), may hold values from -0.0625 to 0.0625
- norm_gain: bfloat16 [8192], replicated, may hold values from 0.5 to 1.5
- router: bfloat16 [2, 4, 8192], replicated, may hold values from -0.125 to 0.125
- up_weight: bfloat16 [2, 4, 8192, 12288], P('role', 'exp', None, 'tp'), may hold values from -0.0625 to 0.0625
- down_weight: bfloat16 [2, 4, 12288, 8192], P('role', 'exp', 'tp'), may hold values from -0.109375 to 0.109375
- modality: int32 [256], P(('role', 'exp', 'tp')), may hold values from 0 to 1
- expert: int32 [256], P(('role', 'exp', 'tp')), may hold values from 0 to 3, as said below
Outputs:
- mixed: bfloat16 [256, 8192], P(('role', 'exp', 'tp'))
Inputs may be any that keep to these rules, and one draw needn't show every extreme that they name: Among the 8 tokens of one device at most 2 choose one expert of one modality, and in every device's tokens some expert of some modality is chosen by exactly 2.
All inputs are finite; a program needn't handle non-finite values.
Results may differ from a plain program's by a relative error of at most 0.0052.
Values may be sent and summed in bfloat16 or wider, within the bound.
No kernel may reach another device: no remote copies, remote signals or barrier semaphores. Data moves between devices by JAX's collectives and lax.ppermute only.
A program may use at most 192 MiB of HBM per device.

v0:
```python
import jax
import jax.numpy as jnp
from jax import lax
from jax.sharding import PartitionSpec as P

EXPERTS = 4
CAP = 2


EPSILON = 1e-05


def per_device(
    residual_in, context, out_weight, norm_gain, router, up_weight, down_weight, modality, expert
):
    tok_rows, width = residual_in.shape
    head_cols = context.shape[1]
    tp_count = lax.axis_size("tp")
    group_count = lax.axis_size("role") * lax.axis_size("exp")
    exp_count = lax.axis_size("exp")
    halves = exp_count // EXPERTS
    grouped = context.reshape(tp_count, tok_rows, head_cols)
    all_rows = lax.all_gather(grouped, ("role", "exp"), axis=1, tiled=True)
    all_rows = all_rows.reshape(tp_count * group_count * tok_rows, head_cols)
    partial_cols = lax.psum_scatter(
        jnp.dot(all_rows, out_weight, preferred_element_type=jnp.float32),
        "tp",
        scatter_dimension=0,
        tiled=True,
    )
    projected = lax.all_to_all(
        partial_cols.reshape(group_count, tok_rows, out_weight.shape[1]),
        ("role", "exp"),
        split_axis=0,
        concat_axis=2,
        tiled=True,
    ).reshape(tok_rows, width)
    resid = (residual_in.astype(jnp.float32) + projected).astype(jnp.bfloat16)
    resid = lax.optimization_barrier(resid)
    widened = resid.astype(jnp.float32)
    inverse_rms = lax.rsqrt(jnp.mean(widened * widened, axis=-1, keepdims=True) + EPSILON)
    normed = (widened * inverse_rms * norm_gain.astype(jnp.float32)).astype(jnp.bfloat16)
    routes = modality * EXPERTS + expert
    choices_hot = routes[:, None] == jnp.arange(2 * EXPERTS, dtype=jnp.int32)[None, :]
    hot_ints = choices_hot.astype(jnp.int32)
    earlier = jnp.cumsum(hot_ints, axis=0) - hot_ints
    position = jnp.sum(earlier * hot_ints, axis=1)
    target = routes * CAP + position
    placed = (jnp.arange(2 * EXPERTS * CAP, dtype=jnp.int32)[:, None] == target[None, :]).astype(
        jnp.bfloat16
    )
    placed = placed.reshape(2, EXPERTS, CAP, tok_rows)
    logits = lax.dot_general(
        normed,
        router.reshape(2 * EXPERTS, width),
        (((1,), (1,)), ((), ())),
        preferred_element_type=jnp.float32,
    )
    gating = jax.nn.sigmoid(jnp.sum(jnp.where(choices_hot, logits, 0.0), axis=1))
    slotted = jnp.einsum("mecq,qd->mecd", placed, normed, preferred_element_type=jnp.float32)
    slotted = slotted.astype(jnp.bfloat16)
    outgoing = jnp.broadcast_to(slotted[:, :, None], (2, EXPERTS, halves, CAP, width))
    outgoing = outgoing.reshape(2, exp_count, CAP, width)
    incoming = lax.all_to_all(
        lax.all_to_all(outgoing, "role", split_axis=0, concat_axis=0, tiled=True),
        "exp",
        split_axis=1,
        concat_axis=1,
        tiled=True,
    )
    local_slots = incoming.reshape(2 * exp_count * CAP, width)
    up_matrix = up_weight[0, 0]
    down_matrix = down_weight[0, 0]
    up_sums = jnp.dot(
        lax.all_gather(local_slots, "tp", axis=0, tiled=True),
        up_matrix,
        preferred_element_type=jnp.float32,
    )
    hidden = jax.nn.gelu(up_sums).astype(jnp.bfloat16)
    results = lax.psum_scatter(
        jnp.dot(hidden, down_matrix, preferred_element_type=jnp.float32),
        "tp",
        scatter_dimension=0,
        tiled=True,
    )
    returned = lax.all_to_all(
        lax.all_to_all(
            results.reshape(2, exp_count, CAP, width).astype(jnp.bfloat16),
            "role",
            split_axis=0,
            concat_axis=0,
            tiled=True,
        ),
        "exp",
        split_axis=1,
        concat_axis=1,
        tiled=True,
    ).astype(jnp.float32)
    expert_out = jnp.einsum(
        "mecq,mescd->qd",
        placed.astype(jnp.float32),
        returned.reshape(2, EXPERTS, halves, CAP, width),
        precision=lax.Precision.HIGHEST,
    )
    return (widened + gating[:, None] * expert_out).astype(jnp.bfloat16)


def solution(mesh):
    in_specs = (
        P(("role", "exp", "tp"), None),
        P(("role", "exp"), "tp"),
        P("tp", ("role", "exp")),
        P(),
        P(),
        P("role", "exp", None, "tp"),
        P("role", "exp", "tp", None),
        P(("role", "exp", "tp")),
        P(("role", "exp", "tp")),
    )
    out_specs = P(("role", "exp", "tp"), None)
    return jax.shard_map(
        per_device, mesh=mesh, in_specs=in_specs, out_specs=out_specs, check_vma=False
    )
```

profile of v0, /device:TPU:0, one launch (start us, length us, event | category | flops | bytes accessed | tf_op | source)
XLA Modules:
  0.0 223.4 jit_solution(17879303161969493802)
XLA Ops:
  6.5 0.0 all-gather.3.cloned.1.call-start
  6.5 0.7 all-gather.3.cloned.1.call-update
  7.3 0.0 reduce-scatter.3.cloned.1.call-start
  7.3 26.5 %all-gather.3.cloned.1.call-done = bf16[4,64,2048]{2,1,0:T(8,128)(2,1)} async-done(((bf16[4,8,2048]{2,1,0:T(8,128)(2,1)}), bf16[4,64,2048]{2,1,0:T(8,128)(2,1)}) %all-gather.3.cloned.1.call-update) | async-done | bytes 1048592 | tf_op jit(solution)/shard_map/all_gather | solution.py:23
  33.8 4.8 %fusion.39 = f32[256,1024]{1,0:T(8,128)} fusion(bf16[256,2048]{1,0:T(8,128)(2,1)} %bitcast.43, bf16[2048,1024]{1,0:T(8,128)(2,1)} %param.11), kind=kOutput, calls=%fused_computation.46 | convolution fusion | flops 1073741824 | bytes 6291456 | tf_op jit(solution)/shard_map/dot_general | solution.py:26
  38.5 0.0 reduce-scatter.3.cloned.1.call-update
  38.6 0.7 multiply_add_fusion.2
  39.2 26.8 %reduce-scatter.3.cloned.1.call-done = f32[64,1024]{1,0:T(8,128)} async-done(((f32[256,1024]{1,0:T(8,128)}), f32[64,1024]{1,0:T(8,128)}) %reduce-scatter.3.cloned.1.call-update) | async-done | bytes 262160 | tf_op jit(solution)/shard_map/reduce_scatter | solution.py:25
  66.1 4.6 %all-to-all-start = ((f32[8,8,1024]{2,1,0:T(8,128)}), f32[8,8,1024]{2,1,0:T(8,128)S(1)}, u32[]{:S(2)}, u32[]{:S(2)}) async-start(f32[8,8,1024]{2,1,0:T(8,128)} %bitcast.41), calls=%async_computation.1 | async-start | bytes 524288 | tf_op jit(solution)/shard_map/all_to_all | solution.py:31
  70.7 0.0 all-gather.5.cloned.1.call-start
  70.7 0.7 convert_element_type.39
  71.5 0.2 reduce_window_sum.11
  71.7 8.4 %all-to-all-done = f32[8,8,1024]{2,1,0:T(8,128)S(1)} async-done(((f32[8,8,1024]{2,1,0:T(8,128)}), f32[8,8,1024]{2,1,0:T(8,128)S(1)}, u32[]{:S(2)}, u32[]{:S(2)}) %all-to-all-start) | async-done | bytes 262176 | tf_op jit(solution)/shard_map/all_to_all | solution.py:31
  80.1 0.9 add_convert_fusion
  81.0 0.2 fusion.26
  81.2 0.3 convolution_convert_fusion
  81.5 3.9 %all_to_all.35 = bf16[2,4,2,8192]{3,1,2,0:T(4,128)(2,1)S(1)} all-to-all(bf16[2,4,2,8192]{3,1,2,0:T(4,128)(2,1)S(1)} %convolution_convert_fusion), channel_id=1, replica_groups=mesh['role'=2,'exp'=4,'tp'=4] {'role'}, dimensions={0} | all-to-all | bytes 524288 | tf_op jit(solution)/shard_map/all_to_all | solution.py:65
  85.5 0.3 copy.16
  85.7 11.9 %all_to_all.36 = bf16[2,4,2,8192]{3,2,0,1:T(2,128)(2,1)S(1)} all-to-all(bf16[2,4,2,8192]{3,2,0,1:T(2,128)(2,1)S(1)} %copy.16), channel_id=1, replica_groups=mesh['role'=2,'exp'=4,'tp'=4] {'exp'}, dimensions={1} | all-to-all | bytes 524288 | tf_op jit(solution)/shard_map/all_to_all | solution.py:64
  97.6 0.2 copy.17
  97.8 0.8 reshape.65
  98.6 0.0 all-gather.5.cloned.1.call-update
  98.6 0.0 copy-start
  98.6 0.0 reduce-scatter.5.cloned.1.call-start
  98.6 24.8 %all-gather.5.cloned.1.call-done = bf16[64,8192]{1,0:T(8,128)(2,1)} async-done(((bf16[16,8192]{1,0:T(8,128)(2,1)}), bf16[64,8192]{1,0:T(8,128)(2,1)}) %all-gather.5.cloned.1.call-update) | async-done | bytes 1048592 | tf_op jit(solution)/shard_map/all_gather | solution.py:75
  123.5 36.7 %fusion = f32[64,8192]{1,0:T(8,128)} fusion(bf16[1,1,3072,8192]{3,2,1,0:T(8,128)(2,1)} %param.15, bf16[64,8192]{1,0:T(8,128)(2,1)} %all-gather.5.cloned.1.call-done, bf16[1,1,8192,3072]{3,2,1,0:T(8,128)(2,1)} %param.14), kind=kOutput, calls=%fused_computation | convolution fusion | flops 6444220416 | bytes 103809024 | tf_op jit(solution)/shard_map/dot_general | solution.py:81
  160.2 0.0 reduce-scatter.5.cloned.1.call-update
  160.2 35.4 %reduce-scatter.5.cloned.1.call-done = f32[16,8192]{1,0:T(8,128)} async-done(((f32[64,8192]{1,0:T(8,128)}), f32[16,8192]{1,0:T(8,128)}) %reduce-scatter.5.cloned.1.call-update) | async-done | bytes 524304 | tf_op jit(solution)/shard_map/reduce_scatter | solution.py:80
  195.6 1.1 convert_element_type.44
  196.6 0.2 convert_element_type.45
  196.8 0.2 copy.18
  197.0 3.9 %all_to_all.37 = bf16[2,4,2,8192]{3,1,2,0:T(4,128)(2,1)S(1)} all-to-all(bf16[2,4,2,8192]{3,1,2,0:T(4,128)(2,1)S(1)} %copy.18), channel_id=1, replica_groups=mesh['role'=2,'exp'=4,'tp'=4] {'role'}, dimensions={0} | all-to-all | bytes 524288 | tf_op jit(solution)/shard_map/all_to_all | solution.py:87
  201.0 1.0 copy.19
  201.9 4.6 %all-to-all-start.4 = ((bf16[2,4,2,8192]{3,0,2,1:T(2,128)(2,1)}), bf16[2,4,2,8192]{3,0,2,1:T(2,128)(2,1)S(1)}, u32[]{:S(2)}, u32[]{:S(2)}) async-start(bf16[2,4,2,8192]{3,0,2,1:T(2,128)(2,1)} %copy.19), calls=%async_computation.6 | async-start | bytes 524288 | tf_op jit(solution)/shard_map/all_to_all | solution.py:86
  206.5 0.0 copy-done
  206.6 0.3 fusion.7
  206.8 8.9 %all-to-all-done.4 = bf16[2,4,2,8192]{3,0,2,1:T(2,128)(2,1)S(1)} async-done(((bf16[2,4,2,8192]{3,0,2,1:T(2,128)(2,1)}), bf16[2,4,2,8192]{3,0,2,1:T(2,128)(2,1)S(1)}, u32[]{:S(2)}, u32[]{:S(2)}) %all-to-all-start.4) | async-done | bytes 262176 | tf_op jit(solution)/shard_map/all_to_all | solution.py:86
  215.7 1.1 fusion.6
  (7 shorter events, 0.1 us)
Async XLA Ops:
  6.5 27.3 %all-gather.3.cloned.1.call-start = ((), (), s32[]{:S(2)}) async-start(), calls=%async_computation.7 | async-start | bytes 1179648 | tf_op jit(solution)/shard_map/all_gather | solution.py:23
  7.3 58.8 %reduce-scatter.3.cloned.1.call-start = ((), (), s32[]{:S(2)}) async-start(), calls=%async_computation.8 | async-start | bytes 1310720 | tf_op jit(solution)/shard_map/reduce_scatter | solution.py:25
  66.1 14.0 %all-to-all-start = ((f32[8,8,1024]{2,1,0:T(8,128)}), f32[8,8,1024]{2,1,0:T(8,128)S(1)}, u32[]{:S(2)}, u32[]{:S(2)}) async-start(f32[8,8,1024]{2,1,0:T(8,128)} %bitcast.41), calls=%async_computation.1 | async-start | bytes 524288 | tf_op jit(solution)/shard_map/all_to_all | solution.py:31
  70.7 52.8 %all-gather.5.cloned.1.call-start = ((), (), s32[]{:S(2)}) async-start(), calls=%async_computation.9 | async-start | bytes 1310720 | tf_op jit(solution)/shard_map/all_gather | solution.py:75
  98.6 107.9 %copy-start = (bf16[2,4,8192]{2,1,0:T(4,128)(2,1)S(1)}, bf16[2,4,8192]{2,1,0:T(4,128)(2,1)}, u32[]{:S(2)}) copy-start(bf16[2,4,8192]{2,1,0:T(4,128)(2,1)} %param.13) | copy-start | bytes 393220
  98.6 97.0 %reduce-scatter.5.cloned.1.call-start = ((), (), s32[]{:S(2)}) async-start(), calls=%async_computation.10 | async-start | bytes 2621440 | tf_op jit(solution)/shard_map/reduce_scatter | solution.py:80
  201.9 13.8 %all-to-all-start.4 = ((bf16[2,4,2,8192]{3,0,2,1:T(2,128)(2,1)}), bf16[2,4,2,8192]{3,0,2,1:T(2,128)(2,1)S(1)}, u32[]{:S(2)}, u32[]{:S(2)}) async-start(bf16[2,4,2,8192]{3,0,2,1:T(2,128)(2,1)} %copy.19), calls=%async_computation.6 | async-start | bytes 524288 | tf_op jit(solution)/shard_map/all_to_all | solution.py:86
Sparse Core Ops, SparseCore 0:
  9.0 24.7 all-gather.2
  38.7 27.3 reduce-scatter.2
  98.7 24.7 all-gather.4
  160.3 35.1 reduce-scatter.4
where the time goes:
time: 224 us; the launch traced here: 223 us
  waiting for transfers between devices  132 us (59%)
  matrix products  43.2 us (19%)
  blocking collectives  19.7 us (9%)
  between operations  13.2 us (6%)
  starting transfers between devices  9.32 us (4%)
  other arithmetic  3.8 us (2%)
  local copies, waits for them, and re-layouts  2.64 us (1%)
    dot_general x1, matrix products, per_device(): jnp.dot(hidden, down_matrix, preferred_element_type=jnp.float32)  36.7 us
    reduce_scatter x1, waiting for transfers between devices, per_device(): lax.psum_scatter(jnp.dot(hidden, down_matrix, preferred_element_type=jnp....  35.4 us
    reduce_scatter x1, waiting for transfers between devices, per_device(): lax.psum_scatter(jnp.dot(all_rows, out_weight, preferred_element_type=jnp...  26.8 us
    all_gather x1, waiting for transfers between devices, per_device(): all_rows = lax.all_gather(grouped, ('role', 'exp'), axis=1, tiled=True)  26.5 us
    all_gather x1, waiting for transfers between devices, per_device(): lax.all_gather(local_slots, 'tp', axis=0, tiled=True)  24.8 us
    all_to_all x1, blocking collectives, per_device(): lax.all_to_all(lax.all_to_all(outgoing, 'role', split_axis=0, concat_axis...  11.9 us
    all_to_all x1, waiting for transfers between devices, per_device(): lax.all_to_all(lax.all_to_all(results.reshape(2, exp_count, CAP, width).a...  8.9 us
    all_to_all x1, waiting for transfers between devices, per_device(): lax.all_to_all(partial_cols.reshape(group_count, tok_rows, out_weight.sha...  8.41 us
  transfers between devices with their start and end apart: 6, of which 6 were waited for; matrix products, arithmetic and copies ran while one was open for 1% of the time, Pallas kernels for 0%

commit v1 on v0

v1 whole, which is shorter than its diff:
```python
import functools

import jax
import jax.numpy as jnp
from jax import lax
from jax.experimental import pallas as pl
from jax.experimental.pallas import tpu as pltpu
from jax.sharding import PartitionSpec as P

EXPERTS = 4
CAP = 2
EPSILON = 1e-05
MIB = 1 << 20
BF16 = jnp.bfloat16
F32 = jnp.float32

VMEM = pl.BlockSpec(memory_space=pltpu.VMEM)
SMEM = pl.BlockSpec(memory_space=pltpu.SMEM)
ANY = pl.BlockSpec(memory_space=pl.ANY)
HBM = pl.BlockSpec(memory_space=pltpu.HBM)


def swap(value, axis, distance):
    size = lax.axis_size(axis)
    return lax.ppermute(value, axis, [(i, i ^ distance) for i in range(size)])


def up_copies(step, exp_count, cols, place_ref, source_ref, out_ref, sems):
    copies = []
    for side in range(2):
        role = place_ref[0] if side == 0 else 1 - place_ref[0]
        start = pl.multiple_of((role * exp_count + (place_ref[1] ^ step)) * cols, cols)
        for part in range(4):
            size = cols // 4
            copies.append(
                pltpu.make_async_copy(
                    source_ref.at[pl.ds(pl.multiple_of(start + part * size, size), size)],
                    out_ref.at[pl.ds(side * cols + part * size, size)],
                    sems.at[4 * side + part],
                )
            )
    return copies


def fetch_kernel(step, exp_count, cols, place_ref, source_ref, *refs):
    out_ref, done_ref, sems = refs[-3:]
    copies = up_copies(step, exp_count, cols, place_ref, source_ref, out_ref, sems)
    for copy in copies:
        copy.start()
    done_ref[...] = jnp.zeros_like(done_ref)
    for copy in copies:
        copy.wait()


def fetch_up(step, exp_count, cols, lanes, place, matrix, after):
    units = matrix.shape[1]
    return pl.pallas_call(
        functools.partial(fetch_kernel, step, exp_count, cols),
        out_shape=[
            pltpu.VMEM((2 * cols, units), BF16),
            jax.ShapeDtypeStruct((8, lanes), BF16),
        ],
        in_specs=[SMEM, HBM] + [ANY] * len(after),
        out_specs=[VMEM] * 2,
        scratch_shapes=[pltpu.SemaphoreType.DMA((8,))],
        compiler_params=pltpu.CompilerParams(vmem_limit_bytes=MIB),
        cost_estimate=pl.CostEstimate(
            flops=0, bytes_accessed=4 * cols * units, transcendentals=0
        ),
        name="fetch_up",
    )(place, matrix, *after)


def project_kernel(tp_count, groups, place_ref, *refs):
    blocks, weight_ref = refs[:groups], refs[groups]
    outs, done_ref = refs[groups + 1 : -1], refs[-1]
    done_ref[...] = jnp.zeros_like(done_ref)
    tp_at = place_ref[2]
    tok_rows = blocks[0].shape[0] // tp_count
    cols = weight_ref.shape[1]
    rows = jnp.concatenate([block[...] for block in blocks], axis=0)
    tile = 256 if cols % 256 == 0 else cols
    for start in range(0, cols, tile):
        at_cols = slice(start, start + tile)
        sums = jnp.dot(rows, weight_ref[:, at_cols], preferred_element_type=F32)
        sums = sums.reshape(groups, tp_count, tok_rows, tile)
        for j in range(tp_count):
            wanted = tp_at ^ j
            block = sums[:, 0]
            for at in range(1, tp_count):
                block = jnp.where(wanted == at, sums[:, at], block)
            outs[j][:, at_cols] = block.reshape(groups * tok_rows, tile).astype(BF16)


def slot_kernel(tp_count, exp_count, split, place_ref, code_ref, residual_ref, *refs):
    parts, outs = refs[:tp_count], refs[tp_count:]
    role_at, exp_at = place_ref[0], place_ref[1]
    total = parts[0][...].astype(F32)
    for part in parts[1:]:
        total = total + part[...].astype(F32)
    resid = (residual_ref[...].astype(F32) + total).astype(BF16)
    count = resid.shape[0]
    slots = 2 * exp_count * CAP
    codes = code_ref[...]
    for out, role in zip(outs, (role_at, 1 - role_at)):
        for q in range(exp_count):
            route = role * EXPERTS + (exp_at ^ q) // split
            ids = lax.broadcasted_iota(jnp.int32, (slots, count), 0) + route * slots
            hot = (ids == codes).astype(F32).astype(BF16)
            picked = jnp.dot(hot, resid, preferred_element_type=F32)
            out[q] = picked.astype(BF16)


def lift(refs, first, place_ref, gain_ref, router_ref, split, exp_count, scaled, squares, logits):
    steps, _, slots, cols = refs[0].shape
    chosen = place_ref[1] // split
    for q in range(steps):
        for side in range(2):
            at = 2 * q + side
            role = place_ref[0] if side == 0 else 1 - place_ref[0]
            group = role * exp_count + (place_ref[1] ^ (first + q))
            at_cols = pl.ds(pl.multiple_of(group * cols, cols), cols)
            gain = gain_ref[:, at_cols]
            for j, ref in enumerate(refs):
                values = ref[q, side].astype(F32)
                squares[j] = squares[j] + jnp.sum(values * values, axis=1, keepdims=True)
                lifted = (values * gain).astype(BF16)
                scaled[j * slots : (j + 1) * slots, at * cols : (at + 1) * cols] = lifted
                if j == 0:
                    rows = router_ref[place_ref[0], :, at_cols].astype(F32)
                    rows_at = lax.broadcasted_iota(jnp.int32, rows.shape, 0)
                    weights = jnp.sum(jnp.where(rows_at == chosen, rows, 0.0), axis=0, keepdims=True)
                    logits = logits + jnp.sum(lifted.astype(F32) * weights, axis=1, keepdims=True)
    return squares, logits


def up_tile(units):
    return 256 if units % 256 == 0 else 128


def up_sums(scaled, up_refs, at_cols):
    total = None
    for at, ref in enumerate(up_refs):
        depth = ref.shape[0]
        term = jnp.dot(
            scaled[:, at * depth : (at + 1) * depth],
            ref[:, at_cols],
            preferred_element_type=F32,
        )
        total = term if total is None else total + term
    return total


def multiply(scaled, up_refs, last, copies, totals_ref, base, finish):
    units = totals_ref.shape[1]
    step = up_tile(units)
    cut = sum(ref.shape[0] for ref in up_refs)
    extra = scaled.shape[1] - cut

    @pl.loop(0, units // step)
    def _(at):
        at_cols = pl.ds(pl.multiple_of(at * step, step), step)
        sums = up_sums(scaled, up_refs, at_cols)
        totals_ref[:, at_cols] = sums if base is None else base[:, at_cols] + sums

    for copy in copies:
        copy.wait()
    if finish is not None:
        finish[0]()

    @pl.loop(0, units // step)
    def _(at):
        at_cols = pl.ds(pl.multiple_of(at * step, step), step)
        sums = totals_ref[:, at_cols]
        if extra:
            sums = sums + jnp.dot(scaled[:, cut:], last[:, at_cols], preferred_element_type=F32)
        if finish is None or finish[1] is None:
            totals_ref[:, at_cols] = sums
        else:
            finish[1](at_cols, sums)


def last_copies(first, count, exp_count, cols, place_ref, source_ref, last, sems):
    copies = []
    for at in range(count):
        copies += up_copies(
            first + at, exp_count, cols, place_ref, source_ref,
            last.at[pl.ds(at * 2 * cols, 2 * cols)], sems.at[at],
        )
    return copies


def first_kernel(sizes, place_ref, gain_ref, router_ref, *refs):
    tp_count, exp_count, split, near, ready = sizes
    rows_in, up_ref, source_ref = refs[:tp_count], refs[tp_count], refs[tp_count + 1]
    sums_ref, squares_ref, logits_ref = refs[tp_count + 2 : tp_count + 5]
    far_refs = refs[tp_count + 5 : tp_count + 5 + ready]
    scaled, last, last_sems, far_sems = refs[tp_count + 5 + ready :]
    slots, cols = rows_in[0].shape[2:]
    copies = last_copies(1, near - 1, exp_count, cols, place_ref, source_ref, last, last_sems)
    for copy in copies:
        copy.start()
    far_copies = []
    for at, far_ref in enumerate(far_refs):
        far_copies += up_copies(
            near + at, exp_count, cols, place_ref, source_ref, far_ref, far_sems.at[at]
        )
    zero = jnp.zeros((slots, 1), F32)
    squares, logits = lift(
        rows_in, 0, place_ref, gain_ref, router_ref, split, exp_count, scaled,
        [zero] * tp_count, zero,
    )
    squares_ref[...] = jnp.broadcast_to(jnp.concatenate(squares, axis=0), squares_ref.shape)
    logits_ref[...] = jnp.broadcast_to(logits, logits_ref.shape)

    def begin():
        for copy in far_copies:
            copy.start()

    multiply(scaled, [up_ref], last, copies, sums_ref, None, (begin, None))
    for copy in far_copies:
        copy.wait()


def down_loop(hidden, down_ref, outs, ring, sems, first, prime):
    depth, _, tile = ring.shape
    slots, width = outs[0].shape
    tiles = width // tile

    def fetch(at, slot):
        return pltpu.make_async_copy(
            down_ref.at[:, pl.ds(pl.multiple_of(first + at * tile, tile), tile)],
            ring.at[slot],
            sems.at[slot],
        )

    if prime:
        for at in range(min(depth, tiles)):
            fetch(at, at).start()
        return

    @pl.loop(0, tiles)
    def _(at):
        slot = lax.rem(at, depth)
        fetch(at, slot).wait()
        sums = jnp.dot(hidden[...], ring[slot], preferred_element_type=F32)
        at_cols = pl.ds(pl.multiple_of(at * tile, tile), tile)
        for j, out in enumerate(outs):
            out[:, at_cols] = sums[j * slots : (j + 1) * slots].astype(BF16)

        @pl.when(at + depth < tiles)
        def _():
            fetch(at + depth, slot).start()


def second_kernel(
    sizes, place_ref, gain_ref, router_ref, sums_ref, squares_ref, logits_ref, *refs
):
    tp_count, exp_count, split, near, far, width, early = sizes
    ready = far - far // 2
    rows_in, up_refs = refs[:tp_count], refs[tp_count : tp_count + ready]
    source_ref, down_ref = refs[tp_count + ready : tp_count + ready + 2]
    outs = refs[tp_count + ready + 2 : 2 * tp_count + ready + 2]
    hidden, gate_ref, held_ref, scaled, totals, last, last_sems, ring, sems, held_sem = refs[
        2 * tp_count + ready + 2 :
    ]
    slots, cols = rows_in[0].shape[2:]
    copies = last_copies(
        near + ready, far - ready, exp_count, cols, place_ref, source_ref, last, last_sems
    )
    for copy in copies:
        copy.start()
    held = pltpu.make_async_copy(
        down_ref.at[:, pl.ds(early, held_ref.shape[1])], held_ref, held_sem
    )
    squares = [squares_ref[j * slots : (j + 1) * slots, :1] for j in range(tp_count)]
    squares, logits = lift(
        rows_in, near, place_ref, gain_ref, router_ref, split, exp_count, scaled,
        squares, logits_ref[:, :1],
    )
    inverse = lax.rsqrt(jnp.concatenate(squares, axis=0) / width + EPSILON)
    gate_ref[...] = jnp.broadcast_to(jax.nn.sigmoid(logits * inverse[:slots]), gate_ref.shape)

    def begin():
        down_loop(hidden, down_ref, outs, ring, sems, 0, True)
        held.start()

    def end(at_cols, sums):
        hidden[:, at_cols] = jax.nn.gelu(sums * inverse).astype(BF16)

    multiply(scaled, up_refs, last, copies, totals, sums_ref, (begin, end))
    down_loop(hidden, down_ref, outs, ring, sems, 0, False)
    held.wait()


def third_kernel(tp_count, first, hidden, held_ref, down_ref, *refs):
    outs, (ring, sems) = refs[:tp_count], refs[tp_count:]
    slots = outs[0].shape[0]
    held = held_ref.shape[1]
    rest = [out.at[:, pl.ds(held, out.shape[1] - held)] for out in outs]
    down_loop(hidden, down_ref, rest, ring, sems, first + held, True)
    tile = ring.shape[2]

    @pl.loop(0, held // tile)
    def _(at):
        at_cols = pl.ds(pl.multiple_of(at * tile, tile), tile)
        sums = jnp.dot(hidden[...], held_ref[:, at_cols], preferred_element_type=F32)
        for j, out in enumerate(outs):
            out[:, at_cols] = sums[j * slots : (j + 1) * slots].astype(BF16)

    down_loop(hidden, down_ref, rest, ring, sems, first + held, False)


def combine_kernel(tp_count, exp_count, split, first, size, place_ref, rows_ref, gate_ref, *refs):
    summands, (stay_ref, leave_ref) = refs[:tp_count], refs[-2:]
    role_at, exp_at = place_ref[0], place_ref[1]
    cols = rows_ref.shape[3]
    count = stay_ref.shape[0]
    gate = gate_ref[:, :1]
    weight = jnp.where(exp_at % split == 0, 1.0, 0.0).astype(F32)
    for at in range(size // cols):
        group = first + at
        own = rows_ref[(group % exp_count) ^ exp_at, (group // exp_count) ^ role_at].astype(F32)
        at_cols = slice(at * cols, (at + 1) * cols)
        to_cols = slice(group * cols, (group + 1) * cols)
        total = summands[0][:, at_cols].astype(F32)
        for part in summands[1:]:
            total = total + part[:, at_cols].astype(F32)
        answers = own * weight + gate * total
        low, high = answers[:count], answers[count:]
        stay_ref[:, to_cols] = jnp.where(role_at == 0, low, high).astype(BF16)
        leave_ref[:, to_cols] = jnp.where(role_at == 0, high, low).astype(BF16)


def per_device(
    residual_in, context, out_weight, norm_gain, router, up_weight, down_weight, modality, expert
):
    tok_rows, width = residual_in.shape
    role_count, exp_count = lax.axis_size("role"), lax.axis_size("exp")
    tp_count = lax.axis_size("tp")
    role_at, exp_at, tp_at = (lax.axis_index(name) for name in ("role", "exp", "tp"))
    groups = role_count * exp_count
    split = exp_count // EXPERTS
    cols = out_weight.shape[1]
    slots = groups * CAP
    place = jnp.stack([role_at, exp_at, tp_at]).astype(jnp.int32)
    up_matrix, down_matrix = up_weight[0, 0], down_weight[0, 0]
    units = up_matrix.shape[1]
    in_hbm = lambda array: pltpu.with_memory_space_constraint(array, pltpu.HBM)
    up_matrix, down_matrix, out_weight = (in_hbm(a) for a in (up_matrix, down_matrix, out_weight))
    near_steps = exp_count // 2
    far_steps = exp_count - near_steps
    gains = norm_gain.astype(F32)[None, :]

    near = [context] + [swap(context, "exp", k) for k in range(1, exp_count)]

    routes = modality * EXPERTS + expert
    hot = (routes[:, None] == jnp.arange(2 * EXPERTS, dtype=jnp.int32)[None, :]).astype(jnp.int32)
    earlier = jnp.cumsum(hot, axis=0) - hot
    position = jnp.sum(earlier * hot, axis=1)
    code = routes * slots + (role_at * exp_count + exp_at) * CAP + position

    from_exp = (jnp.arange(exp_count) ^ exp_at) // split
    from_role = jnp.arange(2) ^ role_at
    row_route = (from_role[None, :] * EXPERTS + from_exp[:, None])[:, :, None]
    row_target = (row_route * CAP + jnp.arange(CAP)).reshape(-1)
    picks = ((routes * CAP + position)[:, None] == row_target[None, :]).astype(BF16)

    lanes = 128
    pieces = residual_in.reshape(tok_rows, role_count, exp_count, cols).transpose(1, 2, 0, 3)
    marks = jnp.broadcast_to(code.astype(BF16)[:, None], (role_count, exp_count, tok_rows, lanes))
    pieces = jnp.concatenate([pieces, marks], axis=3)
    mine = lax.dynamic_index_in_dim(pieces, role_at, 0, keepdims=False)
    other = lax.dynamic_index_in_dim(pieces, 1 - role_at, 0, keepdims=False)
    pair = jnp.stack([mine, swap(other, "role", 1)], axis=1)
    parted = [
        lax.dynamic_index_in_dim(pair, exp_at ^ k, 0, keepdims=False) for k in range(exp_count)
    ]

    up_block, done = fetch_up(
        0, exp_count, cols, context.shape[1], place, up_matrix, [*parted, gains, picks]
    )
    near[1:] = [
        (value.reshape(-1, *done.shape) + done).reshape(value.shape) for value in near[1:]
    ]
    blocks = []
    for value in near:
        blocks += [value, swap(value, "role", 1)]

    *partial_sums, done = pl.pallas_call(
        functools.partial(project_kernel, tp_count, groups),
        out_shape=[jax.ShapeDtypeStruct((groups * tok_rows, cols), BF16)] * tp_count
        + [jax.ShapeDtypeStruct((tok_rows, cols + lanes), BF16)],
        in_specs=[SMEM] + [VMEM] * (groups + 1),
        out_specs=[VMEM] * (tp_count + 1),
        compiler_params=pltpu.CompilerParams(vmem_limit_bytes=(8 if groups <= 8 else 24) * MIB),
        name="project",
    )(place, *blocks, out_weight)
    summands = [partial_sums[0]] + [swap(partial_sums[j], "tp", j) for j in range(1, tp_count)]

    gathered = [parted[0]] + [swap(parted[k] + done, "exp", k) for k in range(1, exp_count)]
    gathered = jnp.stack(gathered).reshape(groups * tok_rows, cols + lanes)
    residual_cols = gathered[:, :cols]
    codes = gathered[:, cols].astype(jnp.int32)[None, :]

    kept, leaving = pl.pallas_call(
        functools.partial(slot_kernel, tp_count, exp_count, split),
        out_shape=[jax.ShapeDtypeStruct((exp_count, slots, cols), BF16)] * 2,
        in_specs=[SMEM] + [VMEM] * (tp_count + 2),
        out_specs=[VMEM] * 2,
        compiler_params=pltpu.CompilerParams(vmem_limit_bytes=(6 if groups <= 8 else 24) * MIB),
        name="slot",
    )(place, codes, residual_cols, *summands)
    arrived = swap(leaving, "role", 1)
    routed = []
    for q in range(exp_count):
        both = jnp.stack([kept[q], arrived[q]])
        routed.append(swap(both, "exp", q) if q else both)
    near_rows = jnp.stack(routed[:near_steps])
    far_rows = jnp.stack(routed[near_steps:])
    near_all = [near_rows] + [swap(near_rows, "tp", j) for j in range(1, tp_count)]
    far_all = [far_rows] + [swap(far_rows, "tp", j) for j in range(1, tp_count)]

    rows = tp_count * slots
    small = rows <= 64
    half = near_steps * 2 * cols
    ready = far_steps - far_steps // 2
    in_vmem = lambda blocks: [pltpu.with_memory_space_constraint(b, pltpu.VMEM) for b in blocks]
    sums, squares, logits, *far_blocks = pl.pallas_call(
        functools.partial(first_kernel, (tp_count, exp_count, split, near_steps, ready)),
        out_shape=[
            pltpu.VMEM((rows, units), F32),
            pltpu.VMEM((rows, 128), F32),
            pltpu.VMEM((slots, 128), F32),
        ]
        + [pltpu.VMEM((2 * cols, units), BF16)] * ready,
        in_specs=[SMEM] + [VMEM] * (3 + tp_count) + [HBM],
        out_specs=[VMEM] * (3 + ready),
        scratch_shapes=[
            pltpu.VMEM((rows, half), BF16),
            pltpu.VMEM(((near_steps - 1) * 2 * cols, units), BF16),
            pltpu.SemaphoreType.DMA((near_steps - 1, 8)),
            pltpu.SemaphoreType.DMA((ready, 8)),
        ],
        compiler_params=pltpu.CompilerParams(vmem_limit_bytes=(21 if small else 36) * MIB),
        cost_estimate=pl.CostEstimate(
            flops=2 * rows * half * units, bytes_accessed=2 * half * units, transcendentals=0
        ),
        name="first",
    )(place, gains, router, *near_all, *in_vmem([up_block]), up_matrix)
    tile, depth = 256, 5
    early = width // 2
    held = early // tile // 4 * tile
    sizes = (tp_count, exp_count, split, near_steps, far_steps, width, early)
    *early_outs, hidden, gate, held_block = pl.pallas_call(
        functools.partial(second_kernel, sizes),
        out_shape=[jax.ShapeDtypeStruct((slots, early), BF16)] * tp_count
        + [jax.ShapeDtypeStruct((rows, units), BF16), jax.ShapeDtypeStruct((slots, 128), F32)]
        + [pltpu.VMEM((units, held), BF16)],
        in_specs=[SMEM] + [VMEM] * (5 + tp_count + ready) + [HBM] * 2,
        out_specs=[VMEM] * (tp_count + 3),
        scratch_shapes=[
            pltpu.VMEM((rows, width - half), BF16),
            pltpu.VMEM((rows, units), F32),
            pltpu.VMEM(((far_steps - ready) * 2 * cols, units), BF16),
            pltpu.SemaphoreType.DMA((far_steps - ready, 8)),
            pltpu.VMEM((depth, units, tile), BF16),
            pltpu.SemaphoreType.DMA((depth,)),
            pltpu.SemaphoreType.DMA,
        ],
        compiler_params=pltpu.CompilerParams(vmem_limit_bytes=(21 if small else 40) * MIB),
        cost_estimate=pl.CostEstimate(
            flops=4 * rows * half * units, bytes_accessed=4 * half * units, transcendentals=0
        ),
        name="second",
    )(
        place, gains, router, *in_vmem([sums, squares, logits]), *far_all, *in_vmem(far_blocks),
        up_matrix, down_matrix,
    )
    late_outs = pl.pallas_call(
        functools.partial(third_kernel, tp_count, early),
        out_shape=[jax.ShapeDtypeStruct((slots, width - early), BF16)] * tp_count,
        in_specs=[VMEM, VMEM, HBM],
        out_specs=[VMEM] * tp_count,
        scratch_shapes=[
            pltpu.VMEM((depth, units, tile), BF16),
            pltpu.SemaphoreType.DMA((depth,)),
        ],
        compiler_params=pltpu.CompilerParams(vmem_limit_bytes=(12 if small else 24) * MIB),
        cost_estimate=pl.CostEstimate(
            flops=2 * rows * half * units, bytes_accessed=2 * half * units, transcendentals=0
        ),
        name="third",
    )(hidden, *in_vmem([held_block]), down_matrix)

    early_sums = [early_outs[0]] + [swap(early_outs[j], "tp", j) for j in range(1, tp_count)]
    late_sums = [late_outs[0]] + [
        swap(late_outs[j] + 0 * early_sums[j], "tp", j) for j in range(1, tp_count)
    ]
    all_rows = jnp.concatenate([near_rows, far_rows])
    home = ()
    for start, summands in ((0, early_sums), (early, late_sums)):
        size = summands[0].shape[1]
        home = pl.pallas_call(
            functools.partial(
                combine_kernel, tp_count, exp_count, split, start // cols, size
            ),
            out_shape=[jax.ShapeDtypeStruct((exp_count * CAP, width), BF16)] * 2,
            in_specs=[SMEM] + [VMEM] * (tp_count + 2 + len(home)),
            out_specs=[VMEM] * 2,
            input_output_aliases={tp_count + 3 + at: at for at in range(len(home))},
            compiler_params=pltpu.CompilerParams(vmem_limit_bytes=(8 if small else 40) * MIB),
            name="combine",
        )(place, all_rows, gate, *summands, *home)
    stay, leave = home
    home = jnp.stack([stay, swap(leave, "role", 1)]).reshape(2, exp_count, CAP, width)
    returned = []
    for q in range(exp_count):
        piece = lax.dynamic_index_in_dim(home, exp_at ^ q, 1, keepdims=False)
        returned.append(swap(piece, "exp", q) if q else piece)
    returned = jnp.stack(returned).reshape(groups * CAP, width)
    return jnp.dot(picks, returned, preferred_element_type=F32).astype(BF16)


def solution(mesh):
    in_specs = (
        P(("role", "exp", "tp"), None),
        P(("role", "exp"), "tp"),
        P("tp", ("role", "exp")),
        P(),
        P(),
        P("role", "exp", None, "tp"),
        P("role", "exp", "tp", None),
        P(("role", "exp", "tp")),
        P(("role", "exp", "tp")),
    )
    out_specs = P(("role", "exp", "tp"), None)
    return jax.shard_map(
        per_device, mesh=mesh, in_specs=in_specs, out_specs=out_specs, check_vma=False
    )
```

time: 224 us -> 116 us (0.52)
  waiting for transfers between devices: 132 us -> 27.6 us
  Pallas kernels: 0 us -> 44.9 us
  matrix products: 43.2 us -> 0.89 us
  starting transfers between devices: 9.32 us -> 37.5 us
  blocking collectives: 19.7 us -> 0 us
  between operations: 13.2 us -> 0.35 us
    reduce_scatter x2 -> x0, waiting for transfers between devices: 62.2 us -> none  [the longest x1 35.4 us: per_device(): lax.psum_scatter(jnp.dot(hidden, down_matrix, preferred_element_type=jnp....]
    all_gather x2 -> x0, waiting for transfers between devices: 51.3 us -> none  [the longest x1 26.5 us: per_device(): all_rows = lax.all_gather(grouped, ('role', 'exp'), axis=1, tiled=True)]
    pallas_call x0 -> x8, Pallas kernels: none -> 44.9 us  [the longest x1 16.7 us: per_device(): pl.pallas_call(functools.partial(second_kernel, sizes), out_shape=[jax.Sh...]
    dot_general x5 -> x1, matrix products: 43.2 us -> 0.89 us  [per_device(): return jnp.dot(picks, returned, preferred_element_type=F32).astype(BF16)]
    ppermute x0 -> x34, starting transfers between devices: none -> 37.5 us  [swap(): return lax.ppermute(value, axis, [(i, i ^ distance) for i in range(size)])]
    ppermute x0 -> x34, waiting for transfers between devices: none -> 27.6 us  [swap(): return lax.ppermute(value, axis, [(i, i ^ distance) for i in range(size)])]
    all_to_all x3 -> x0, blocking collectives: 19.7 us -> none  [the longest x1 11.9 us: per_device(): lax.all_to_all(lax.all_to_all(outgoing, 'role', split_axis=0, concat_axis...]
    all_to_all x2 -> x0, waiting for transfers between devices: 17.3 us -> none  [the longest x1 8.9 us: per_device(): lax.all_to_all(lax.all_to_all(results.reshape(2, exp_count, CAP, width).a...]
  transfers between devices with their start and end apart: 6 -> 34, of which waited for: 6 -> 18; matrix products, arithmetic and copies ran while one was open for 1% -> 3% of each run, Pallas kernels for 0% -> 20%
where the time goes in v1:
time: 116 us
  Pallas kernels  44.9 us (39%)
  starting transfers between devices  37.5 us (32%)
  waiting for transfers between devices  27.6 us (24%)
  other arithmetic  3.7 us (3%)
    ppermute x34, starting transfers between devices, swap(): return lax.ppermute(value, axis, [(i, i ^ distance) for i in range(size)])  37.5 us
    ppermute x34, waiting for transfers between devices, swap(): return lax.ppermute(value, axis, [(i, i ^ distance) for i in range(size)])  27.6 us
    pallas_call x1, Pallas kernels, per_device(): pl.pallas_call(functools.partial(second_kernel, sizes), out_shape=[jax.Sh...  16.7 us
    pallas_call x1, Pallas kernels, per_device(): pl.pallas_call(functools.partial(first_kernel, (tp_count, exp_count, spli...  10.1 us
    pallas_call x1, Pallas kernels, per_device(): pl.pallas_call(functools.partial(third_kernel, tp_count, early), out_shap...  7.25 us
    pallas_call x1, Pallas kernels, fetch_up(): pl.pallas_call(functools.partial(fetch_kernel, step, exp_count, cols), ou...  5.25 us
    pallas_call x1, Pallas kernels, per_device(): pl.pallas_call(functools.partial(project_kernel, tp_count, groups), out_s...  3.46 us
  transfers between devices with their start and end apart: 34, of which 18 were waited for; matrix products, arithmetic and copies ran while one was open for 3% of the time, Pallas kernels for 20%

profile of v1, /device:TPU:0, one launch (start us, length us, event | category | flops | bytes accessed | tf_op | source)
XLA Modules:
  0.0 115.9 jit_solution(3175217223579877446)
XLA Ops:
  0.0 0.5 collective-permute-start.1
  0.5 4.6 %collective-permute-start.6 = (bf16[32,2048]{1,0:T(8,128)(2,1)}, bf16[32,2048]{1,0:T(8,128)(2,1)S(1)}, u32[]{:S(2)}, u32[]{:S(2)}) collective-permute-start(bf16[32,2048]{1,0:T(8,128)(2,1)} %refs_0_.1), channel_id=1, source_target_pairs={{0,12},{4,8},{8,4},{12,0},{1,13},{5,9},{9,5},{13,1},{2,14},{6,10},... | collective-permute-start | bytes 393224 | tf_op jit(solution)/shard_map/ppermute | solution.py:25
  5.1 0.6 collective-permute-start.2
  5.7 0.7 multiply_add_fusion.4
  6.5 0.2 select_reduce_fusion
  6.7 0.9 fusion.1
  7.7 0.7 broadcast_in_dim.9
  8.8 0.1 collective-permute-done
  9.0 5.3 %fetch_up.1 = (bf16[2048,3072]{1,0:T(8,128)(2,1)S(1)}, bf16[8,2048]{1,0:T(8,128)(2,1)S(1)}) custom-call(s32[3]{0:T(128)S(1)} %pad_add_fusion.place_ref, bf16[8192,3072]{1,0:T(8,128)(2,1)} %bitcast.52, bf16[2,8,1152]{2,1,0:T(8,128)(2,1)S(1)} %bitcast.50, bf16[2,8,1152]{2,1,0:T(8,128)(2,1)S(1)} %get-tuple-element.67.refs_1_, ...), custom_call_target="tpu_custom_call" | custom-call | bytes 12582912 | tf_op jit(solution)/shard_map/fetch_up/pallas_call | solution.py:57
  14.3 2.7 %collective-permute-done.4 = bf16[32,2048]{1,0:T(8,128)(2,1)S(1)} collective-permute-done((bf16[32,2048]{1,0:T(8,128)(2,1)}, bf16[32,2048]{1,0:T(8,128)(2,1)S(1)}, u32[]{:S(2)}, u32[]{:S(2)}) %collective-permute-start.4) | collective-permute-done | bytes 131104 | tf_op jit(solution)/shard_map/ppermute | solution.py:25
  17.1 0.5 collective-permute-start.5
  17.7 0.8 collective-permute-done.3.refs_3_
  18.5 0.2 collective-permute-done.5.refs_5_
  18.6 0.3 collective-permute-done.7.refs_7_
  19.0 3.5 %project.1 = (bf16[64,1024]{1,0:T(8,128)(2,1)S(1)}, bf16[64,1024]{1,0:T(8,128)(2,1)S(1)}, bf16[64,1024]{1,0:T(8,128)(2,1)S(1)}, bf16[64,1024]{1,0:T(8,128)(2,1)S(1)}, bf16[8,1152]{1,0:T(8,128)(2,1)S(1)}) custom-call(s32[3]{0:T(128)S(1)} %pad_add_fusion.place_ref, bf16[32,2048]{1,0:T(8,128)(2,1)S(1)} %copy-done.1, ...), custom_call_target="tpu_custom_call" | custom-call | tf_op jit(solution)/shard_map/project/pallas_call | solution.py:390
  22.5 2.5 %collective-permute-start.10 = (bf16[2,8,1152]{2,1,0:T(8,128)(2,1)S(1)}, bf16[2,8,1152]{2,1,0:T(8,128)(2,1)S(1)}, u32[]{:S(2)}, u32[]{:S(2)}) collective-permute-start(bf16[2,8,1152]{2,1,0:T(8,128)(2,1)S(1)} %get-tuple-element.84), channel_id=1, source_target_pairs={{0,12},{4,8},{8,4},{12,0},{1,13},{5,9},{9,5},{13,1},{2,14},{6,10},... | collective-permute-start | bytes 110600 | tf_op jit(solution)/shard_map/ppermute | solution.py:25
  25.0 1.9 %collective-permute-start.8 = (bf16[2,8,1152]{2,1,0:T(8,128)(2,1)S(1)}, bf16[2,8,1152]{2,1,0:T(8,128)(2,1)S(1)}, u32[]{:S(2)}, u32[]{:S(2)}) collective-permute-start(bf16[2,8,1152]{2,1,0:T(8,128)(2,1)S(1)} %get-tuple-element.82), channel_id=1, source_target_pairs={{0,4},{4,0},{8,12},{12,8},{1,5},{5,1},{9,13},{13,9},{2,6},{6,2},{1... | collective-permute-start | bytes 110600 | tf_op jit(solution)/shard_map/ppermute | solution.py:25
  26.9 1.5 %collective-permute-start.11 = (bf16[64,1024]{1,0:T(8,128)(2,1)S(1)}, bf16[64,1024]{1,0:T(8,128)(2,1)S(1)}, u32[]{:S(2)}, u32[]{:S(2)}) collective-permute-start(bf16[64,1024]{1,0:T(8,128)(2,1)S(1)} %get-tuple-element.36), channel_id=1, source_target_pairs={{0,1},{1,0},{2,3},{3,2},{4,5},{5,4},{6,7},{7,6},{8,9},{9,8},{10,11... | collective-permute-start | bytes 393224 | tf_op jit(solution)/shard_map/ppermute | solution.py:25
  28.4 1.5 %collective-permute-start.12 = (bf16[64,1024]{1,0:T(8,128)(2,1)S(1)}, bf16[64,1024]{1,0:T(8,128)(2,1)S(1)}, u32[]{:S(2)}, u32[]{:S(2)}) collective-permute-start(bf16[64,1024]{1,0:T(8,128)(2,1)S(1)} %get-tuple-element.37), channel_id=1, source_target_pairs={{0,2},{1,3},{2,0},{3,1},{4,6},{5,7},{6,4},{7,5},{8,10},{9,11},{10,... | collective-permute-start | bytes 393224 | tf_op jit(solution)/shard_map/ppermute | solution.py:25
  29.9 0.8 collective-permute-start.13
  30.8 0.1 convert_reduce_fusion
  30.9 1.6 %collective-permute-done.11.refs_1_ = bf16[64,1024]{1,0:T(8,128)(2,1)S(1)} collective-permute-done((bf16[64,1024]{1,0:T(8,128)(2,1)S(1)}, bf16[64,1024]{1,0:T(8,128)(2,1)S(1)}, u32[]{:S(2)}, u32[]{:S(2)}) %collective-permute-start.11) | collective-permute-done | bytes 131104 | tf_op jit(solution)/shard_map/ppermute | solution.py:25
  32.6 3.6 %collective-permute-done.12.refs_2_ = bf16[64,1024]{1,0:T(8,128)(2,1)S(1)} collective-permute-done((bf16[64,1024]{1,0:T(8,128)(2,1)S(1)}, bf16[64,1024]{1,0:T(8,128)(2,1)S(1)}, u32[]{:S(2)}, u32[]{:S(2)}) %collective-permute-start.12) | collective-permute-done | bytes 131104 | tf_op jit(solution)/shard_map/ppermute | solution.py:25
  36.2 0.9 slot.1
  37.2 1.3 %collective-permute-done.14 = bf16[4,16,1024]{2,1,0:T(8,128)(2,1)S(1)} collective-permute-done((bf16[4,16,1024]{2,1,0:T(8,128)(2,1)S(1)}, bf16[4,16,1024]{2,1,0:T(8,128)(2,1)S(1)}, u32[]{:S(2)}, u32[]{:S(2)}) %collective-permute-start.14) | collective-permute-done | bytes 131104 | tf_op jit(solution)/shard_map/ppermute | solution.py:25
  38.5 2.5 %collective-permute-start.17 = (bf16[2,16,1024]{2,1,0:T(8,128)(2,1)S(1)}, bf16[2,16,1024]{2,1,0:T(8,128)(2,1)S(1)}, u32[]{:S(2)}, u32[]{:S(2)}) collective-permute-start(bf16[2,16,1024]{2,1,0:T(8,128)(2,1)S(1)} %pad_maximum_fusion.7), channel_id=1, source_target_pairs={{0,12},{4,8},{8,4},{12,0},{1,13},{5,9},{9,5},{13,1},{2,14},{6,10},... | collective-permute-start | bytes 196616 | tf_op jit(solution)/shard_map/ppermute | solution.py:25
  41.2 2.0 %collective-permute-start.15 = (bf16[2,16,1024]{2,1,0:T(8,128)(2,1)S(1)}, bf16[2,16,1024]{2,1,0:T(8,128)(2,1)S(1)}, u32[]{:S(2)}, u32[]{:S(2)}) collective-permute-start(bf16[2,16,1024]{2,1,0:T(8,128)(2,1)S(1)} %pad_maximum_fusion.5), channel_id=1, source_target_pairs={{0,4},{4,0},{8,12},{12,8},{1,5},{5,1},{9,13},{13,9},{2,6},{6,2},{1... | collective-permute-start | bytes 196616 | tf_op jit(solution)/shard_map/ppermute | solution.py:25
  43.1 2.9 %collective-permute-done.15 = bf16[2,16,1024]{2,1,0:T(8,128)(2,1)S(1)} collective-permute-done((bf16[2,16,1024]{2,1,0:T(8,128)(2,1)S(1)}, bf16[2,16,1024]{2,1,0:T(8,128)(2,1)S(1)}, u32[]{:S(2)}, u32[]{:S(2)}) %collective-permute-start.15) | collective-permute-done | bytes 65568 | tf_op jit(solution)/shard_map/ppermute | solution.py:25
  46.1 0.8 collective-permute-start.18
  46.9 1.1 collective-permute-start.19
  48.0 1.6 %collective-permute-start.20 = (bf16[2,2,16,1024]{3,2,1,0:T(8,128)(2,1)S(1)}, bf16[2,2,16,1024]{3,2,1,0:T(8,128)(2,1)S(1)}, u32[]{:S(2)}, u32[]{:S(2)}) collective-permute-start(bf16[2,2,16,1024]{3,2,1,0:T(8,128)(2,1)S(1)} %pad_maximum_fusion.3.refs_0_), channel_id=1, source_target_pairs={{0,3},{1,2},{2,1},{3,0},{4,7},{5,6},{6,5},{7,4},{8,11},{9,10},{10,... | collective-permute-start | bytes 393224 | tf_op jit(solution)/shard_map/ppermute | solution.py:25
  49.7 0.8 collective-permute-start.21
  50.5 1.1 collective-permute-start.22
  51.6 0.6 collective-permute-done.18.refs_1_
  52.2 1.0 collective-permute-start.23
  53.2 2.2 %collective-permute-done.19.refs_2_ = bf16[2,2,16,1024]{3,2,1,0:T(8,128)(2,1)S(1)} collective-permute-done((bf16[2,2,16,1024]{3,2,1,0:T(8,128)(2,1)S(1)}, bf16[2,2,16,1024]{3,2,1,0:T(8,128)(2,1)S(1)}, u32[]{:S(2)}, u32[]{:S(2)}) %collective-permute-start.19) | collective-permute-done | bytes 131104 | tf_op jit(solution)/shard_map/ppermute | solution.py:25
  55.4 0.1 collective-permute-done.20.refs_3_
  55.6 10.1 %first.1 = (f32[64,3072]{1,0:T(8,128)S(1)}, f32[64,128]{1,0:T(8,128)S(1)}, f32[16,128]{1,0:T(8,128)S(1)}, bf16[2048,3072]{1,0:T(8,128)(2,1)S(1)}) custom-call(s32[3]{0:T(128)S(1)} %pad_add_fusion.place_ref, f32[1,8192]{1,0:T(1,128)S(1)} %bitcast.48, bf16[2,4,8192]{2,1,0:T(4,128)(2,1)S(1)} %copy-done, bf16[2,2,16,1024]{3,2,1,0:T(8,128)(2,1)S(1)} %pad_maximum_fusion.3.refs_0_, ...), custom_call_target="tpu_custom_call" | custom-call | flops 1610612736 | bytes 25165824 | tf_op jit(solution)/shard_map/first/pallas_call | solution.py:429
  65.8 16.7 %second.1 = (bf16[16,4096]{1,0:T(8,128)(2,1)S(1)}, bf16[16,4096]{1,0:T(8,128)(2,1)S(1)}, bf16[16,4096]{1,0:T(8,128)(2,1)S(1)}, bf16[16,4096]{1,0:T(8,128)(2,1)S(...) custom-call(s32[3]{0:T(128)S(1)} %pad_add_fusion.place_ref, ...), custom_call_target="tpu_custom_call" | custom-call | flops 3221225472 | bytes 50331648 | tf_op jit(solution)/shard_map/second/pallas_call | solution.py:455
  82.4 1.4 %collective-permute-start.24 = (bf16[16,4096]{1,0:T(8,128)(2,1)S(1)}, bf16[16,4096]{1,0:T(8,128)(2,1)S(1)}, u32[]{:S(2)}, u32[]{:S(2)}) collective-permute-start(bf16[16,4096]{1,0:T(8,128)(2,1)S(1)} %get-tuple-element.51), channel_id=1, source_target_pairs={{0,1},{1,0},{2,3},{3,2},{4,5},{5,4},{6,7},{7,6},{8,9},{9,8},{10,11... | collective-permute-start | bytes 393224 | tf_op jit(solution)/shard_map/ppermute | solution.py:25
  83.8 1.2 %collective-permute-start.26 = (bf16[16,4096]{1,0:T(8,128)(2,1)S(1)}, bf16[16,4096]{1,0:T(8,128)(2,1)S(1)}, u32[]{:S(2)}, u32[]{:S(2)}) collective-permute-start(bf16[16,4096]{1,0:T(8,128)(2,1)S(1)} %get-tuple-element.53), channel_id=1, source_target_pairs={{0,2},{1,3},{2,0},{3,1},{4,6},{5,7},{6,4},{7,5},{8,10},{9,11},{10,... | collective-permute-start | bytes 393224 | tf_op jit(solution)/shard_map/ppermute | solution.py:25
  85.0 1.0 collective-permute-start.28
  86.0 7.3 %third.1 = (bf16[16,4096]{1,0:T(8,128)(2,1)S(1)}, bf16[16,4096]{1,0:T(8,128)(2,1)S(1)}, bf16[16,4096]{1,0:T(8,128)(2,1)S(1)}, bf16[16,4096]{1,0:T(8,128)(2,1)S(1)}) custom-call(bf16[64,3072]{1,0:T(8,128)(2,1)S(1)} %get-tuple-element.47.hidden, bf16[3072,1024]{1,0:T(8,128)(2,1)S(1)} %get-tuple-element.48.held_ref, bf16[3072,8192]{1,0:T(8,128)(2,1)} %bitcast.56), custom_call_target="tpu_custom_call" | custom-call | flops 1610612736 | bytes 25165824 | tf_op jit(solution)/shard_map/third/pallas_call | solution.py:480
  93.3 1.4 %collective-permute-start.25 = (bf16[16,4096]{1,0:T(8,128)(2,1)S(1)}, bf16[16,4096]{1,0:T(8,128)(2,1)S(1)}, u32[]{:S(2)}, u32[]{:S(2)}) collective-permute-start(bf16[16,4096]{1,0:T(8,128)(2,1)S(1)} %multiply_add_fusion.2), channel_id=1, source_target_pairs={{0,1},{1,0},{2,3},{3,2},{4,5},{5,4},{6,7},{7,6},{8,9},{9,8},{10,11... | collective-permute-start | bytes 393224 | tf_op jit(solution)/shard_map/ppermute | solution.py:25
  94.7 1.2 %collective-permute-start.27 = (bf16[16,4096]{1,0:T(8,128)(2,1)S(1)}, bf16[16,4096]{1,0:T(8,128)(2,1)S(1)}, u32[]{:S(2)}, u32[]{:S(2)}) collective-permute-start(bf16[16,4096]{1,0:T(8,128)(2,1)S(1)} %multiply_add_fusion.1), channel_id=1, source_target_pairs={{0,2},{1,3},{2,0},{3,1},{4,6},{5,7},{6,4},{7,5},{8,10},{9,11},{10,... | collective-permute-start | bytes 393224 | tf_op jit(solution)/shard_map/ppermute | solution.py:25
  96.0 1.0 collective-permute-start.29
  97.1 0.7 combine.2
  97.7 0.6 collective-permute-done.25.refs_1_
  98.3 1.4 %collective-permute-done.27.refs_2_ = bf16[16,4096]{1,0:T(8,128)(2,1)S(1)} collective-permute-done((bf16[16,4096]{1,0:T(8,128)(2,1)S(1)}, bf16[16,4096]{1,0:T(8,128)(2,1)S(1)}, u32[]{:S(2)}, u32[]{:S(2)}) %collective-permute-start.27) | collective-permute-done | bytes 131104 | tf_op jit(solution)/shard_map/ppermute | solution.py:25
  99.8 2.2 %collective-permute-done.29.refs_3_ = bf16[16,4096]{1,0:T(8,128)(2,1)S(1)} collective-permute-done((bf16[16,4096]{1,0:T(8,128)(2,1)S(1)}, bf16[16,4096]{1,0:T(8,128)(2,1)S(1)}, u32[]{:S(2)}, u32[]{:S(2)}) %collective-permute-start.29) | collective-permute-done | bytes 131104 | tf_op jit(solution)/shard_map/ppermute | solution.py:25
  101.9 0.6 combine.3
  102.6 0.1 stack.109
  102.8 1.2 %collective-permute-done.30 = bf16[8,8192]{1,0:T(8,128)(2,1)S(1)} collective-permute-done((bf16[8,8192]{1,0:T(8,128)(2,1)S(1)}, bf16[8,8192]{1,0:T(8,128)(2,1)S(1)}, u32[]{:S(2)}, u32[]{:S(2)}) %collective-permute-start.30) | collective-permute-done | bytes 131104 | tf_op jit(solution)/shard_map/ppermute | solution.py:25
  104.1 0.1 stack.110
  104.2 0.1 constant_dynamic-update-slice_fusion
  104.3 0.2 dynamic-slice_bitcast_fusion.3
  104.5 3.2 %collective-permute-start.33 = (bf16[2,2,8192]{2,1,0:T(2,128)(2,1)S(1)}, bf16[2,2,8192]{2,1,0:T(2,128)(2,1)S(1)}, u32[]{:S(2)}, u32[]{:S(2)}) collective-permute-start(bf16[2,2,8192]{2,1,0:T(2,128)(2,1)S(1)} %get-tuple-element.62), channel_id=1, source_target_pairs={{0,12},{4,8},{8,4},{12,0},{1,13},{5,9},{9,5},{13,1},{2,14},{6,10},... | collective-permute-start | bytes 196616 | tf_op jit(solution)/shard_map/ppermute | solution.py:25
  107.7 0.4 collective-permute-start.32
  108.1 0.9 collective-permute-start.31
  109.0 2.1 %collective-permute-done.33 = bf16[2,2,8192]{2,1,0:T(2,128)(2,1)S(1)} collective-permute-done((bf16[2,2,8192]{2,1,0:T(2,128)(2,1)S(1)}, bf16[2,2,8192]{2,1,0:T(2,128)(2,1)S(1)}, u32[]{:S(2)}, u32[]{:S(2)}) %collective-permute-start.33) | collective-permute-done | bytes 65568 | tf_op jit(solution)/shard_map/ppermute | solution.py:25
  111.1 3.3 %collective-permute-done.32 = bf16[2,2,8192]{2,1,0:T(2,128)(2,1)S(1)} collective-permute-done((bf16[2,2,8192]{2,1,0:T(2,128)(2,1)S(1)}, bf16[2,2,8192]{2,1,0:T(2,128)(2,1)S(1)}, u32[]{:S(2)}, u32[]{:S(2)}) %collective-permute-start.32) | collective-permute-done | bytes 65568 | tf_op jit(solution)/shard_map/ppermute | solution.py:25
  114.4 0.5 pad_maximum_fusion.1
  114.9 0.1 reshape.96
  115.0 0.9 convolution_convert_fusion
  (57 shorter events, 1.4 us)
Async XLA Ops:
  0.0 17.7 %collective-permute-start.1 = (bf16[32,2048]{1,0:T(8,128)(2,1)}, bf16[32,2048]{1,0:T(8,128)(2,1)S(1)}, u32[]{:S(2)}, u32[]{:S(2)}) collective-permute-start(bf16[32,2048]{1,0:T(8,128)(2,1)} %refs_0_.1), channel_id=1, source_target_pairs={{0,16},{16,0},{1,17},{17,1},{2,18},{18,2},{3,19},{19,3},{4,20},{20... | collective-permute-start | bytes 393224 | tf_op jit(solution)/shard_map/ppermute | solution.py:25
  0.5 13.8 %collective-permute-start.6 = (bf16[32,2048]{1,0:T(8,128)(2,1)}, bf16[32,2048]{1,0:T(8,128)(2,1)S(1)}, u32[]{:S(2)}, u32[]{:S(2)}) collective-permute-start(bf16[32,2048]{1,0:T(8,128)(2,1)} %refs_0_.1), channel_id=1, source_target_pairs={{0,12},{4,8},{8,4},{12,0},{1,13},{5,9},{9,5},{13,1},{2,14},{6,10},... | collective-permute-start | bytes 393224 | tf_op jit(solution)/shard_map/ppermute | solution.py:25
  5.1 12.0 %collective-permute-start.4 = (bf16[32,2048]{1,0:T(8,128)(2,1)}, bf16[32,2048]{1,0:T(8,128)(2,1)S(1)}, u32[]{:S(2)}, u32[]{:S(2)}) collective-permute-start(bf16[32,2048]{1,0:T(8,128)(2,1)} %refs_0_.1), channel_id=1, source_target_pairs={{0,8},{4,12},{8,0},{12,4},{1,9},{5,13},{9,1},{13,5},{2,10},{6,14},... | collective-permute-start | bytes 393224 | tf_op jit(solution)/shard_map/ppermute | solution.py:25
  5.1 12.0 %collective-permute-start.2 = (bf16[32,2048]{1,0:T(8,128)(2,1)}, bf16[32,2048]{1,0:T(8,128)(2,1)S(1)}, u32[]{:S(2)}, u32[]{:S(2)}) collective-permute-start(bf16[32,2048]{1,0:T(8,128)(2,1)} %refs_0_.1), channel_id=1, source_target_pairs={{0,4},{4,0},{8,12},{12,8},{1,5},{5,1},{9,13},{13,9},{2,6},{6,2},{1... | collective-permute-start | bytes 393224 | tf_op jit(solution)/shard_map/ppermute | solution.py:25
  7.6 1.3 %collective-permute-start = (bf16[4,8,1152]{2,1,0:T(8,128)(2,1)S(1)}, bf16[4,8,1152]{2,1,0:T(8,128)(2,1)S(1)}, u32[]{:S(2)}, u32[]{:S(2)}) collective-permute-start(bf16[4,8,1152]{2,1,0:T(8,128)(2,1)S(1)} %get-tuple-element.69), channel_id=1, source_target_pairs={{0,16},{16,0},{1,17},{17,1},{2,18},{18,2},{3,19},{19,3},{4,20},{20... | collective-permute-start | bytes 221192 | tf_op jit(solution)/shard_map/ppermute | solution.py:25
  9.0 10.0 %copy-start.1 = (bf16[32,2048]{1,0:T(8,128)(2,1)S(1)}, bf16[32,2048]{1,0:T(8,128)(2,1)}, u32[]{:S(2)}) copy-start(bf16[32,2048]{1,0:T(8,128)(2,1)} %refs_0_.1) | copy-start | bytes 393220
  9.0 46.6 %copy-start = (bf16[2,4,8192]{2,1,0:T(4,128)(2,1)S(1)}, bf16[2,4,8192]{2,1,0:T(4,128)(2,1)}, u32[]{:S(2)}) copy-start(bf16[2,4,8192]{2,1,0:T(4,128)(2,1)} %router_ref.3) | copy-start | bytes 393220
  17.0 1.4 %collective-permute-start.3 = (bf16[32,2048]{1,0:T(8,128)(2,1)S(1)}, bf16[32,2048]{1,0:T(8,128)(2,1)S(1)}, u32[]{:S(2)}, u32[]{:S(2)}) collective-permute-start(bf16[32,2048]{1,0:T(8,128)(2,1)S(1)} %get-tuple-element.81.refs_2_), channel_id=1, source_target_pairs={{0,16},{16,0},{1,17},{17,1},{2,18},{18,2},{3,19},{19,3},{4,20},{20... | collective-permute-start | bytes 393224 | tf_op jit(solution)/shard_map/ppermute | solution.py:25
  17.1 1.5 %collective-permute-start.5 = (bf16[32,2048]{1,0:T(8,128)(2,1)S(1)}, bf16[32,2048]{1,0:T(8,128)(2,1)S(1)}, u32[]{:S(2)}, u32[]{:S(2)}) collective-permute-start(bf16[32,2048]{1,0:T(8,128)(2,1)S(1)} %get-tuple-element.80.refs_4_), channel_id=1, source_target_pairs={{0,16},{16,0},{1,17},{17,1},{2,18},{18,2},{3,19},{19,3},{4,20},{20... | collective-permute-start | bytes 393224 | tf_op jit(solution)/shard_map/ppermute | solution.py:25
  17.6 1.3 %collective-permute-start.7 = (bf16[32,2048]{1,0:T(8,128)(2,1)S(1)}, bf16[32,2048]{1,0:T(8,128)(2,1)S(1)}, u32[]{:S(2)}, u32[]{:S(2)}) collective-permute-start(bf16[32,2048]{1,0:T(8,128)(2,1)S(1)} %get-tuple-element.79.refs_6_), channel_id=1, source_target_pairs={{0,16},{16,0},{1,17},{17,1},{2,18},{18,2},{3,19},{19,3},{4,20},{20... | collective-permute-start | bytes 393224 | tf_op jit(solution)/shard_map/ppermute | solution.py:25
  22.5 7.5 %collective-permute-start.10 = (bf16[2,8,1152]{2,1,0:T(8,128)(2,1)S(1)}, bf16[2,8,1152]{2,1,0:T(8,128)(2,1)S(1)}, u32[]{:S(2)}, u32[]{:S(2)}) collective-permute-start(bf16[2,8,1152]{2,1,0:T(8,128)(2,1)S(1)} %get-tuple-element.84), channel_id=1, source_target_pairs={{0,12},{4,8},{8,4},{12,0},{1,13},{5,9},{9,5},{13,1},{2,14},{6,10},... | collective-permute-start | bytes 110600 | tf_op jit(solution)/shard_map/ppermute | solution.py:25
  25.0 5.7 %collective-permute-start.9 = (bf16[2,8,1152]{2,1,0:T(8,128)(2,1)S(1)}, bf16[2,8,1152]{2,1,0:T(8,128)(2,1)S(1)}, u32[]{:S(2)}, u32[]{:S(2)}) collective-permute-start(bf16[2,8,1152]{2,1,0:T(8,128)(2,1)S(1)} %get-tuple-element.83), channel_id=1, source_target_pairs={{0,8},{4,12},{8,0},{12,4},{1,9},{5,13},{9,1},{13,5},{2,10},{6,14},... | collective-permute-start | bytes 110600 | tf_op jit(solution)/shard_map/ppermute | solution.py:25
  25.0 5.7 %collective-permute-start.8 = (bf16[2,8,1152]{2,1,0:T(8,128)(2,1)S(1)}, bf16[2,8,1152]{2,1,0:T(8,128)(2,1)S(1)}, u32[]{:S(2)}, u32[]{:S(2)}) collective-permute-start(bf16[2,8,1152]{2,1,0:T(8,128)(2,1)S(1)} %get-tuple-element.82), channel_id=1, source_target_pairs={{0,4},{4,0},{8,12},{12,8},{1,5},{5,1},{9,13},{13,9},{2,6},{6,2},{1... | collective-permute-start | bytes 110600 | tf_op jit(solution)/shard_map/ppermute | solution.py:25
  26.9 5.6 %collective-permute-start.11 = (bf16[64,1024]{1,0:T(8,128)(2,1)S(1)}, bf16[64,1024]{1,0:T(8,128)(2,1)S(1)}, u32[]{:S(2)}, u32[]{:S(2)}) collective-permute-start(bf16[64,1024]{1,0:T(8,128)(2,1)S(1)} %get-tuple-element.36), channel_id=1, source_target_pairs={{0,1},{1,0},{2,3},{3,2},{4,5},{5,4},{6,7},{7,6},{8,9},{9,8},{10,11... | collective-permute-start | bytes 393224 | tf_op jit(solution)/shard_map/ppermute | solution.py:25
  28.4 7.8 %collective-permute-start.12 = (bf16[64,1024]{1,0:T(8,128)(2,1)S(1)}, bf16[64,1024]{1,0:T(8,128)(2,1)S(1)}, u32[]{:S(2)}, u32[]{:S(2)}) collective-permute-start(bf16[64,1024]{1,0:T(8,128)(2,1)S(1)} %get-tuple-element.37), channel_id=1, source_target_pairs={{0,2},{1,3},{2,0},{3,1},{4,6},{5,7},{6,4},{7,5},{8,10},{9,11},{10,... | collective-permute-start | bytes 393224 | tf_op jit(solution)/shard_map/ppermute | solution.py:25
  29.9 6.3 %collective-permute-start.13 = (bf16[64,1024]{1,0:T(8,128)(2,1)S(1)}, bf16[64,1024]{1,0:T(8,128)(2,1)S(1)}, u32[]{:S(2)}, u32[]{:S(2)}) collective-permute-start(bf16[64,1024]{1,0:T(8,128)(2,1)S(1)} %get-tuple-element.38), channel_id=1, source_target_pairs={{0,3},{1,2},{2,1},{3,0},{4,7},{5,6},{6,5},{7,4},{8,11},{9,10},{10,... | collective-permute-start | bytes 393224 | tf_op jit(solution)/shard_map/ppermute | solution.py:25
  37.1 1.4 %collective-permute-start.14 = (bf16[4,16,1024]{2,1,0:T(8,128)(2,1)S(1)}, bf16[4,16,1024]{2,1,0:T(8,128)(2,1)S(1)}, u32[]{:S(2)}, u32[]{:S(2)}) collective-permute-start(bf16[4,16,1024]{2,1,0:T(8,128)(2,1)S(1)} %get-tuple-element.40), channel_id=1, source_target_pairs={{0,16},{16,0},{1,17},{17,1},{2,18},{18,2},{3,19},{19,3},{4,20},{20... | collective-permute-start | bytes 393224 | tf_op jit(solution)/shard_map/ppermute | solution.py:25
  38.5 11.1 %collective-permute-start.17 = (bf16[2,16,1024]{2,1,0:T(8,128)(2,1)S(1)}, bf16[2,16,1024]{2,1,0:T(8,128)(2,1)S(1)}, u32[]{:S(2)}, u32[]{:S(2)}) collective-permute-start(bf16[2,16,1024]{2,1,0:T(8,128)(2,1)S(1)} %pad_maximum_fusion.7), channel_id=1, source_target_pairs={{0,12},{4,8},{8,4},{12,0},{1,13},{5,9},{9,5},{13,1},{2,14},{6,10},... | collective-permute-start | bytes 196616 | tf_op jit(solution)/shard_map/ppermute | solution.py:25
  41.1 8.6 %collective-permute-start.16 = (bf16[2,16,1024]{2,1,0:T(8,128)(2,1)S(1)}, bf16[2,16,1024]{2,1,0:T(8,128)(2,1)S(1)}, u32[]{:S(2)}, u32[]{:S(2)}) collective-permute-start(bf16[2,16,1024]{2,1,0:T(8,128)(2,1)S(1)} %pad_maximum_fusion.6), channel_id=1, source_target_pairs={{0,8},{4,12},{8,0},{12,4},{1,9},{5,13},{9,1},{13,5},{2,10},{6,14},... | collective-permute-start | bytes 196616 | tf_op jit(solution)/shard_map/ppermute | solution.py:25
  41.2 4.9 %collective-permute-start.15 = (bf16[2,16,1024]{2,1,0:T(8,128)(2,1)S(1)}, bf16[2,16,1024]{2,1,0:T(8,128)(2,1)S(1)}, u32[]{:S(2)}, u32[]{:S(2)}) collective-permute-start(bf16[2,16,1024]{2,1,0:T(8,128)(2,1)S(1)} %pad_maximum_fusion.5), channel_id=1, source_target_pairs={{0,4},{4,0},{8,12},{12,8},{1,5},{5,1},{9,13},{13,9},{2,6},{6,2},{1... | collective-permute-start | bytes 196616 | tf_op jit(solution)/shard_map/ppermute | solution.py:25
  46.1 6.2 %collective-permute-start.18 = (bf16[2,2,16,1024]{3,2,1,0:T(8,128)(2,1)S(1)}, bf16[2,2,16,1024]{3,2,1,0:T(8,128)(2,1)S(1)}, u32[]{:S(2)}, u32[]{:S(2)}) collective-permute-start(bf16[2,2,16,1024]{3,2,1,0:T(8,128)(2,1)S(1)} %pad_maximum_fusion.3.refs_0_), channel_id=1, source_target_pairs={{0,1},{1,0},{2,3},{3,2},{4,5},{5,4},{6,7},{7,6},{8,9},{9,8},{10,11... | collective-permute-start | bytes 393224 | tf_op jit(solution)/shard_map/ppermute | solution.py:25
  46.9 8.5 %collective-permute-start.19 = (bf16[2,2,16,1024]{3,2,1,0:T(8,128)(2,1)S(1)}, bf16[2,2,16,1024]{3,2,1,0:T(8,128)(2,1)S(1)}, u32[]{:S(2)}, u32[]{:S(2)}) collective-permute-start(bf16[2,2,16,1024]{3,2,1,0:T(8,128)(2,1)S(1)} %pad_maximum_fusion.3.refs_0_), channel_id=1, source_target_pairs={{0,2},{1,3},{2,0},{3,1},{4,6},{5,7},{6,4},{7,5},{8,10},{9,11},{10,... | collective-permute-start | bytes 393224 | tf_op jit(solution)/shard_map/ppermute | solution.py:25
  48.0 7.6 %collective-permute-start.20 = (bf16[2,2,16,1024]{3,2,1,0:T(8,128)(2,1)S(1)}, bf16[2,2,16,1024]{3,2,1,0:T(8,128)(2,1)S(1)}, u32[]{:S(2)}, u32[]{:S(2)}) collective-permute-start(bf16[2,2,16,1024]{3,2,1,0:T(8,128)(2,1)S(1)} %pad_maximum_fusion.3.refs_0_), channel_id=1, source_target_pairs={{0,3},{1,2},{2,1},{3,0},{4,7},{5,6},{6,5},{7,4},{8,11},{9,10},{10,... | collective-permute-start | bytes 393224 | tf_op jit(solution)/shard_map/ppermute | solution.py:25
  49.7 16.1 %collective-permute-start.21 = (bf16[2,2,16,1024]{3,2,1,0:T(8,128)(2,1)S(1)}, bf16[2,2,16,1024]{3,2,1,0:T(8,128)(2,1)S(1)}, u32[]{:S(2)}, u32[]{:S(2)}) collective-permute-start(bf16[2,2,16,1024]{3,2,1,0:T(8,128)(2,1)S(1)} %pad_maximum_fusion.4.refs_0_), channel_id=1, source_target_pairs={{0,1},{1,0},{2,3},{3,2},{4,5},{5,4},{6,7},{7,6},{8,9},{9,8},{10,11... | collective-permute-start | bytes 393224 | tf_op jit(solution)/shard_map/ppermute | solution.py:25
  50.5 15.3 %collective-permute-start.22 = (bf16[2,2,16,1024]{3,2,1,0:T(8,128)(2,1)S(1)}, bf16[2,2,16,1024]{3,2,1,0:T(8,128)(2,1)S(1)}, u32[]{:S(2)}, u32[]{:S(2)}) collective-permute-start(bf16[2,2,16,1024]{3,2,1,0:T(8,128)(2,1)S(1)} %pad_maximum_fusion.4.refs_0_), channel_id=1, source_target_pairs={{0,2},{1,3},{2,0},{3,1},{4,6},{5,7},{6,4},{7,5},{8,10},{9,11},{10,... | collective-permute-start | bytes 393224 | tf_op jit(solution)/shard_map/ppermute | solution.py:25
  52.2 13.5 %collective-permute-start.23 = (bf16[2,2,16,1024]{3,2,1,0:T(8,128)(2,1)S(1)}, bf16[2,2,16,1024]{3,2,1,0:T(8,128)(2,1)S(1)}, u32[]{:S(2)}, u32[]{:S(2)}) collective-permute-start(bf16[2,2,16,1024]{3,2,1,0:T(8,128)(2,1)S(1)} %pad_maximum_fusion.4.refs_0_), channel_id=1, source_target_pairs={{0,3},{1,2},{2,1},{3,0},{4,7},{5,6},{6,5},{7,4},{8,11},{9,10},{10,... | collective-permute-start | bytes 393224 | tf_op jit(solution)/shard_map/ppermute | solution.py:25
  82.4 10.8 %collective-permute-start.24 = (bf16[16,4096]{1,0:T(8,128)(2,1)S(1)}, bf16[16,4096]{1,0:T(8,128)(2,1)S(1)}, u32[]{:S(2)}, u32[]{:S(2)}) collective-permute-start(bf16[16,4096]{1,0:T(8,128)(2,1)S(1)} %get-tuple-element.51), channel_id=1, source_target_pairs={{0,1},{1,0},{2,3},{3,2},{4,5},{5,4},{6,7},{7,6},{8,9},{9,8},{10,11... | collective-permute-start | bytes 393224 | tf_op jit(solution)/shard_map/ppermute | solution.py:25
  83.8 10.9 %collective-permute-start.26 = (bf16[16,4096]{1,0:T(8,128)(2,1)S(1)}, bf16[16,4096]{1,0:T(8,128)(2,1)S(1)}, u32[]{:S(2)}, u32[]{:S(2)}) collective-permute-start(bf16[16,4096]{1,0:T(8,128)(2,1)S(1)} %get-tuple-element.53), channel_id=1, source_target_pairs={{0,2},{1,3},{2,0},{3,1},{4,6},{5,7},{6,4},{7,5},{8,10},{9,11},{10,... | collective-permute-start | bytes 393224 | tf_op jit(solution)/shard_map/ppermute | solution.py:25
  85.0 10.9 %collective-permute-start.28 = (bf16[16,4096]{1,0:T(8,128)(2,1)S(1)}, bf16[16,4096]{1,0:T(8,128)(2,1)S(1)}, u32[]{:S(2)}, u32[]{:S(2)}) collective-permute-start(bf16[16,4096]{1,0:T(8,128)(2,1)S(1)} %get-tuple-element.55), channel_id=1, source_target_pairs={{0,3},{1,2},{2,1},{3,0},{4,7},{5,6},{6,5},{7,4},{8,11},{9,10},{10,... | collective-permute-start | bytes 393224 | tf_op jit(solution)/shard_map/ppermute | solution.py:25
  93.3 5.0 %collective-permute-start.25 = (bf16[16,4096]{1,0:T(8,128)(2,1)S(1)}, bf16[16,4096]{1,0:T(8,128)(2,1)S(1)}, u32[]{:S(2)}, u32[]{:S(2)}) collective-permute-start(bf16[16,4096]{1,0:T(8,128)(2,1)S(1)} %multiply_add_fusion.2), channel_id=1, source_target_pairs={{0,1},{1,0},{2,3},{3,2},{4,5},{5,4},{6,7},{7,6},{8,9},{9,8},{10,11... | collective-permute-start | bytes 393224 | tf_op jit(solution)/shard_map/ppermute | solution.py:25
  94.7 5.0 %collective-permute-start.27 = (bf16[16,4096]{1,0:T(8,128)(2,1)S(1)}, bf16[16,4096]{1,0:T(8,128)(2,1)S(1)}, u32[]{:S(2)}, u32[]{:S(2)}) collective-permute-start(bf16[16,4096]{1,0:T(8,128)(2,1)S(1)} %multiply_add_fusion.1), channel_id=1, source_target_pairs={{0,2},{1,3},{2,0},{3,1},{4,6},{5,7},{6,4},{7,5},{8,10},{9,11},{10,... | collective-permute-start | bytes 393224 | tf_op jit(solution)/shard_map/ppermute | solution.py:25
  96.0 5.9 %collective-permute-start.29 = (bf16[16,4096]{1,0:T(8,128)(2,1)S(1)}, bf16[16,4096]{1,0:T(8,128)(2,1)S(1)}, u32[]{:S(2)}, u32[]{:S(2)}) collective-permute-start(bf16[16,4096]{1,0:T(8,128)(2,1)S(1)} %multiply_add_fusion), channel_id=1, source_target_pairs={{0,3},{1,2},{2,1},{3,0},{4,7},{5,6},{6,5},{7,4},{8,11},{9,10},{10,... | collective-permute-start | bytes 393224 | tf_op jit(solution)/shard_map/ppermute | solution.py:25
  102.7 1.4 %collective-permute-start.30 = (bf16[8,8192]{1,0:T(8,128)(2,1)S(1)}, bf16[8,8192]{1,0:T(8,128)(2,1)S(1)}, u32[]{:S(2)}, u32[]{:S(2)}) collective-permute-start(bf16[8,8192]{1,0:T(8,128)(2,1)S(1)} %get-tuple-element.60), channel_id=1, source_target_pairs={{0,16},{16,0},{1,17},{17,1},{2,18},{18,2},{3,19},{19,3},{4,20},{20... | collective-permute-start | bytes 393224 | tf_op jit(solution)/shard_map/ppermute | solution.py:25
  104.5 6.6 %collective-permute-start.33 = (bf16[2,2,8192]{2,1,0:T(2,128)(2,1)S(1)}, bf16[2,2,8192]{2,1,0:T(2,128)(2,1)S(1)}, u32[]{:S(2)}, u32[]{:S(2)}) collective-permute-start(bf16[2,2,8192]{2,1,0:T(2,128)(2,1)S(1)} %get-tuple-element.62), channel_id=1, source_target_pairs={{0,12},{4,8},{8,4},{12,0},{1,13},{5,9},{9,5},{13,1},{2,14},{6,10},... | collective-permute-start | bytes 196616 | tf_op jit(solution)/shard_map/ppermute | solution.py:25
  107.7 6.7 %collective-permute-start.32 = (bf16[2,2,8192]{2,1,0:T(2,128)(2,1)S(1)}, bf16[2,2,8192]{2,1,0:T(2,128)(2,1)S(1)}, u32[]{:S(2)}, u32[]{:S(2)}) collective-permute-start(bf16[2,2,8192]{2,1,0:T(2,128)(2,1)S(1)} %get-tuple-element.63), channel_id=1, source_target_pairs={{0,8},{4,12},{8,0},{12,4},{1,9},{5,13},{9,1},{13,5},{2,10},{6,14},... | collective-permute-start | bytes 196616 | tf_op jit(solution)/shard_map/ppermute | solution.py:25
  108.1 6.3 %collective-permute-start.31 = (bf16[2,2,8192]{2,1,0:T(2,128)(2,1)S(1)}, bf16[2,2,8192]{2,1,0:T(2,128)(2,1)S(1)}, u32[]{:S(2)}, u32[]{:S(2)}) collective-permute-start(bf16[2,2,8192]{2,1,0:T(2,128)(2,1)S(1)} %get-tuple-element.64), channel_id=1, source_target_pairs={{0,4},{4,0},{8,12},{12,8},{1,5},{5,1},{9,13},{13,9},{2,6},{6,2},{1... | collective-permute-start | bytes 196616 | tf_op jit(solution)/shard_map/ppermute | solution.py:25

commit v2 on v1

v2 whole, which is shorter than its diff:
```python
import functools

import jax
import jax.numpy as jnp
from jax import lax
from jax.experimental import pallas as pl
from jax.experimental.pallas import tpu as pltpu
from jax.sharding import PartitionSpec as P

EXPERTS = 4
CAP = 2
EPSILON = 1e-05
MIB = 1 << 20
BF16 = jnp.bfloat16
F32 = jnp.float32

VMEM = pl.BlockSpec(memory_space=pltpu.VMEM)
SMEM = pl.BlockSpec(memory_space=pltpu.SMEM)
ANY = pl.BlockSpec(memory_space=pl.ANY)
HBM = pl.BlockSpec(memory_space=pltpu.HBM)


def swap(value, axis, distance):
    size = lax.axis_size(axis)
    return lax.ppermute(value, axis, [(i, i ^ distance) for i in range(size)])


def up_copies(places, exp_count, cols, place_ref, source_ref, out_ref, sems):
    copies = []
    for at, (step, side) in enumerate(places):
        role = place_ref[0] if side == 0 else 1 - place_ref[0]
        start = pl.multiple_of((role * exp_count + (place_ref[1] ^ step)) * cols, cols)
        size = cols // 4
        for part in range(4):
            copies.append(
                pltpu.make_async_copy(
                    source_ref.at[pl.ds(pl.multiple_of(start + part * size, size), size)],
                    out_ref.at[pl.ds(at * cols + part * size, size)],
                    sems.at[4 * at + part],
                )
            )
    return copies


def fetch_kernel(places, exp_count, cols, place_ref, source_ref, *refs):
    out_ref, sems = refs[-2:]
    copies = up_copies(places, exp_count, cols, place_ref, source_ref, out_ref, sems)
    for copy in copies:
        copy.start()
    for copy in copies:
        copy.wait()


def fetch_up(places, exp_count, cols, place, matrix, after):
    units = matrix.shape[1]
    count = len(places)
    return pl.pallas_call(
        functools.partial(fetch_kernel, places, exp_count, cols),
        out_shape=pltpu.VMEM((count * cols, units), BF16),
        in_specs=[SMEM, HBM] + [ANY] * len(after),
        out_specs=VMEM,
        scratch_shapes=[pltpu.SemaphoreType.DMA((4 * count,))],
        compiler_params=pltpu.CompilerParams(vmem_limit_bytes=MIB),
        cost_estimate=pl.CostEstimate(
            flops=0, bytes_accessed=2 * count * cols * units, transcendentals=0
        ),
        name="fetch_up",
    )(place, matrix, *after)


def piece_kernel(exp_count, place_ref, residual_ref, codes_ref, *outs):
    role_at, exp_at = place_ref[0], place_ref[1]
    cols = outs[0].shape[2] - codes_ref.shape[1]
    for out, role in zip(outs, (role_at, 1 - role_at)):
        for q in range(exp_count):
            start = pl.multiple_of((role * exp_count + (exp_at ^ q)) * cols, cols)
            out[q, :, :cols] = residual_ref[:, pl.ds(start, cols)]
            out[q, :, cols:] = codes_ref[...]


def weight_kernel(source_ref, *refs):
    out_ref, done_ref, sems = refs[-3:]
    parts = sems.shape[0]
    size = source_ref.shape[0] // parts
    copies = [
        pltpu.make_async_copy(
            source_ref.at[pl.ds(at * size, size)], out_ref.at[pl.ds(at * size, size)], sems.at[at]
        )
        for at in range(parts)
    ]
    for copy in copies:
        copy.start()
    done_ref[...] = jnp.zeros_like(done_ref)
    for copy in copies:
        copy.wait()


def fetch_weight(matrix, after, lanes):
    return pl.pallas_call(
        weight_kernel,
        out_shape=[
            pltpu.VMEM(matrix.shape, matrix.dtype),
            jax.ShapeDtypeStruct((8, lanes), BF16),
        ],
        in_specs=[HBM] + [ANY] * len(after),
        out_specs=[VMEM] * 2,
        scratch_shapes=[pltpu.SemaphoreType.DMA((4,))],
        compiler_params=pltpu.CompilerParams(vmem_limit_bytes=MIB),
        cost_estimate=pl.CostEstimate(
            flops=0, bytes_accessed=2 * matrix.size, transcendentals=0
        ),
        name="fetch_weight",
    )(matrix, *after)


def project_kernel(tp_count, groups, place_ref, *refs):
    blocks, weight_ref = refs[:groups], refs[groups]
    outs = refs[groups + 1 :]
    tp_at = place_ref[2]
    tok_rows = blocks[0].shape[0] // tp_count
    cols = weight_ref.shape[1]
    rows = jnp.concatenate([block[...] for block in blocks], axis=0)
    tile = 256 if cols % 256 == 0 else cols
    for start in range(0, cols, tile):
        at_cols = slice(start, start + tile)
        sums = jnp.dot(rows, weight_ref[:, at_cols], preferred_element_type=F32)
        sums = sums.reshape(groups, tp_count, tok_rows, tile)
        for j in range(tp_count):
            wanted = tp_at ^ j
            block = sums[:, 0]
            for at in range(1, tp_count):
                block = jnp.where(wanted == at, sums[:, at], block)
            outs[j][:, at_cols] = block.reshape(groups * tok_rows, tile).astype(BF16)


def slot_kernel(tp_count, exp_count, split, steps, place_ref, code_ref, residual_ref, *refs):
    parts, outs = refs[:tp_count], refs[-2:]
    role_at, exp_at = place_ref[0], place_ref[1]
    total = parts[0][...].astype(F32)
    for part in parts[1:]:
        total = total + part[...].astype(F32)
    resid = (residual_ref[...].astype(F32) + total).astype(BF16)
    count = resid.shape[0]
    slots = 2 * exp_count * CAP
    codes = code_ref[...]
    at = lax.broadcasted_iota(jnp.int32, (slots, count), 0)
    side, away, place = at // (exp_count * CAP), at // CAP % exp_count, at % CAP
    for out, role in zip(outs, (role_at, 1 - role_at)):
        for to, q in enumerate(steps):
            exp_to = exp_at ^ q
            route = role * EXPERTS + exp_to // split
            group = (side ^ role) * exp_count + (away ^ exp_to)
            ids = route * slots + group * CAP + place
            hot = (ids == codes).astype(F32).astype(BF16)
            picked = jnp.dot(hot, resid, preferred_element_type=F32)
            out[to] = picked.astype(BF16)


def lift(refs, first, place_ref, gain_ref, router_ref, split, exp_count, scaled, squares, logits):
    steps, _, slots, cols = refs[0].shape
    chosen = place_ref[1] // split
    for q in range(steps):
        for side in range(2):
            at = 2 * q + side
            role = place_ref[0] if side == 0 else 1 - place_ref[0]
            group = role * exp_count + (place_ref[1] ^ (first + q))
            at_cols = pl.ds(pl.multiple_of(group * cols, cols), cols)
            gain = gain_ref[:, at_cols]
            for j, ref in enumerate(refs):
                values = ref[q, side].astype(F32)
                squares[j] = squares[j] + jnp.sum(values * values, axis=1, keepdims=True)
                lifted = (values * gain).astype(BF16)
                scaled[j * slots : (j + 1) * slots, at * cols : (at + 1) * cols] = lifted
                if j == 0:
                    rows = router_ref[place_ref[0], :, at_cols].astype(F32)
                    rows_at = lax.broadcasted_iota(jnp.int32, rows.shape, 0)
                    weights = jnp.sum(jnp.where(rows_at == chosen, rows, 0.0), axis=0, keepdims=True)
                    logits = logits + jnp.sum(lifted.astype(F32) * weights, axis=1, keepdims=True)
    return squares, logits


def up_tile(units, depth):
    step = units
    while step % 256 == 0 and step * depth > MIB * 3 // 2:
        step //= 2
    return step


def up_sums(scaled, up_refs, at_cols):
    total = None
    for at, ref in enumerate(up_refs):
        depth = ref.shape[0]
        term = jnp.dot(
            scaled[:, at * depth : (at + 1) * depth],
            ref[:, at_cols],
            preferred_element_type=F32,
        )
        total = term if total is None else total + term
    return total


def add_blocks(scaled, blocks, totals_ref, base, finish):
    units = totals_ref.shape[1]
    first = 0
    for number, (waits, block) in enumerate(blocks):
        for wait in waits:
            wait()
        depth = block.shape[0]
        step = up_tile(units, depth)
        rows = slice(first, first + depth)
        last = number == len(blocks) - 1

        @pl.loop(0, units // step)
        def _(at, number=number, block=block, rows=rows, last=last, step=step):
            at_cols = pl.ds(pl.multiple_of(at * step, step), step)
            sums = jnp.dot(scaled[:, rows], block[:, at_cols], preferred_element_type=F32)
            if number:
                sums = totals_ref[:, at_cols] + sums
            elif base is not None:
                sums = base[:, at_cols] + sums
            if last and finish is not None:
                finish(at_cols, sums)
            else:
                totals_ref[:, at_cols] = sums

        first += depth


def stream(places, exp_count, cols, place_ref, source_ref, blocks, sems):
    count, size, _ = blocks.shape
    copies = []
    for step, side in places:
        role = place_ref[0] if side == 0 else 1 - place_ref[0]
        start = (role * exp_count + (place_ref[1] ^ step)) * cols
        for part in range(cols // size):
            slot = len(copies) % count
            copies.append(
                pltpu.make_async_copy(
                    source_ref.at[pl.ds(pl.multiple_of(start + part * size, size), size)],
                    blocks.at[slot],
                    sems.at[slot],
                )
            )
    for copy in copies[:count]:
        copy.start()
    plan = []
    for at, copy in enumerate(copies):
        steps = [copy.wait]
        if 0 < at and at - 1 + count < len(copies):
            steps.insert(0, copies[at - 1 + count].start)
        plan.append((steps, blocks.at[at % count]))
    return plan


def first_kernel(sizes, place_ref, gain_ref, router_ref, up_ref, *refs):
    tp_count, exp_count, split, near = sizes
    rows_in, source_ref = refs[:tp_count], refs[tp_count]
    sums_ref, squares_ref, logits_ref, scaled, blocks, sems = refs[tp_count + 1 :]
    slots, cols = rows_in[0].shape[2:]
    places = [(q, side) for q in range(near) for side in range(2)][up_ref.shape[0] // cols :]
    plan = stream(places, exp_count, cols, place_ref, source_ref, blocks, sems)
    zero = jnp.zeros((slots, 1), F32)
    squares, logits = lift(
        rows_in, 0, place_ref, gain_ref, router_ref, split, exp_count, scaled,
        [zero] * tp_count, zero,
    )
    squares_ref[...] = jnp.broadcast_to(jnp.concatenate(squares, axis=0), squares_ref.shape)
    logits_ref[...] = jnp.broadcast_to(logits, logits_ref.shape)
    add_blocks(scaled, [([], up_ref)] + plan, sums_ref, None, None)


def down_loop(hidden, down_ref, outs, ring, sems, first, prime):
    depth, _, tile = ring.shape
    slots, width = outs[0].shape
    tiles = width // tile

    def fetch(at, slot):
        return pltpu.make_async_copy(
            down_ref.at[:, pl.ds(pl.multiple_of(first + at * tile, tile), tile)],
            ring.at[slot],
            sems.at[slot],
        )

    if prime:
        for at in range(min(depth, tiles)):
            fetch(at, at).start()
        return

    @pl.loop(0, tiles)
    def _(at):
        slot = lax.rem(at, depth)
        fetch(at, slot).wait()
        sums = jnp.dot(hidden[...], ring[slot], preferred_element_type=F32)
        at_cols = pl.ds(pl.multiple_of(at * tile, tile), tile)
        for j, out in enumerate(outs):
            out[:, at_cols] = sums[j * slots : (j + 1) * slots].astype(BF16)

        @pl.when(at + depth < tiles)
        def _():
            fetch(at + depth, slot).start()


def second_kernel(
    sizes, place_ref, gain_ref, router_ref, sums_ref, squares_ref, logits_ref, *refs
):
    tp_count, exp_count, split, near, far, width, early = sizes
    rows_in = refs[:tp_count]
    up_ref, source_ref, down_ref = refs[tp_count : tp_count + 3]
    outs = refs[tp_count + 3 : 2 * tp_count + 3]
    hidden, gate_ref, held_ref, scaled, totals, blocks, block_sems, ring, sems, held_sem = refs[
        2 * tp_count + 3 :
    ]
    slots, cols = rows_in[0].shape[2:]
    places = [(q, side) for q in range(near, near + far) for side in range(2)]
    places = places[up_ref.shape[0] // cols :]
    plan = stream(places, exp_count, cols, place_ref, source_ref, blocks, block_sems)
    last = max(1, len(plan) - blocks.shape[0] + 1)
    plan[min(last, len(plan) - 1)][0].insert(
        -1, lambda: down_loop(hidden, down_ref, outs, ring, sems, 0, True)
    )
    plan[-1][0].insert(-1, lambda: held.start())
    held = pltpu.make_async_copy(
        down_ref.at[:, pl.ds(early, held_ref.shape[1])], held_ref, held_sem
    )
    squares = [squares_ref[j * slots : (j + 1) * slots, :1] for j in range(tp_count)]
    squares, logits = lift(
        rows_in, near, place_ref, gain_ref, router_ref, split, exp_count, scaled,
        squares, logits_ref[:, :1],
    )
    inverse = lax.rsqrt(jnp.concatenate(squares, axis=0) / width + EPSILON)
    gate_ref[...] = jnp.broadcast_to(jax.nn.sigmoid(logits * inverse[:slots]), gate_ref.shape)

    def end(at_cols, sums):
        hidden[:, at_cols] = jax.nn.gelu(sums * inverse).astype(BF16)

    add_blocks(scaled, [([], up_ref)] + plan, totals, sums_ref, end)
    down_loop(hidden, down_ref, outs, ring, sems, 0, False)
    held.wait()


def third_kernel(tp_count, first, hidden, held_ref, down_ref, *refs):
    outs, (ring, sems) = refs[:tp_count], refs[tp_count:]
    slots = outs[0].shape[0]
    held = held_ref.shape[1]
    rest = [out.at[:, pl.ds(held, out.shape[1] - held)] for out in outs]
    down_loop(hidden, down_ref, rest, ring, sems, first + held, True)
    tile = ring.shape[2]

    @pl.loop(0, held // tile)
    def _(at):
        at_cols = pl.ds(pl.multiple_of(at * tile, tile), tile)
        sums = jnp.dot(hidden[...], held_ref[:, at_cols], preferred_element_type=F32)
        for j, out in enumerate(outs):
            out[:, at_cols] = sums[j * slots : (j + 1) * slots].astype(BF16)

    down_loop(hidden, down_ref, rest, ring, sems, first + held, False)


def combine_kernel(tp_count, exp_count, split, first, size, place_ref, rows_ref, gate_ref, *refs):
    summands, (stay_ref, leave_ref) = refs[:tp_count], refs[-2:]
    role_at, exp_at = place_ref[0], place_ref[1]
    cols = rows_ref.shape[3]
    count = stay_ref.shape[0]
    gate = gate_ref[:, :1]
    weight = jnp.where(exp_at % split == 0, 1.0, 0.0).astype(F32)
    for at in range(size // cols):
        group = first + at
        to_cols = slice(group * cols, (group + 1) * cols)
        own = rows_ref[(group % exp_count) ^ exp_at, (group // exp_count) ^ role_at].astype(F32)
        at_cols = slice(at * cols, (at + 1) * cols)
        total = summands[0][:, at_cols].astype(F32)
        for part in summands[1:]:
            total = total + part[:, at_cols].astype(F32)
        answers = own * weight + gate * total
        stay_ref[:, to_cols] = answers[:count].astype(BF16)
        leave_ref[:, to_cols] = answers[count:].astype(BF16)


def final_kernel(parts, picks_ref, *refs):
    pieces, out_ref = refs[:-1], refs[-1]
    picks = picks_ref[...].astype(F32)
    per_part = len(pieces) // parts
    first = 0
    for part in range(parts):
        size = pieces[part * per_part].shape[1]
        tile = 1024 if size % 1024 == 0 else size
        for start in range(0, size, tile):
            total, row_at = None, 0
            for piece in pieces[part * per_part : (part + 1) * per_part]:
                rows = piece[:, start : start + tile].astype(F32)
                for row in range(rows.shape[0]):
                    term = picks[:, row_at : row_at + 1] * rows[row : row + 1]
                    total = term if total is None else total + term
                    row_at += 1
            out_ref[:, first + start : first + start + tile] = total.astype(BF16)
        first += size


def per_device(
    residual_in, context, out_weight, norm_gain, router, up_weight, down_weight, modality, expert
):
    tok_rows, width = residual_in.shape
    role_count, exp_count = lax.axis_size("role"), lax.axis_size("exp")
    tp_count = lax.axis_size("tp")
    role_at, exp_at, tp_at = (lax.axis_index(name) for name in ("role", "exp", "tp"))
    groups = role_count * exp_count
    split = exp_count // EXPERTS
    cols = out_weight.shape[1]
    slots = groups * CAP
    place = jnp.stack([role_at, exp_at, tp_at]).astype(jnp.int32)
    up_matrix, down_matrix = up_weight[0, 0], down_weight[0, 0]
    units = up_matrix.shape[1]
    in_vmem = lambda blocks: [pltpu.with_memory_space_constraint(b, pltpu.VMEM) for b in blocks]
    in_hbm = lambda array: pltpu.with_memory_space_constraint(array, pltpu.HBM)
    up_matrix, down_matrix, out_weight = (in_hbm(a) for a in (up_matrix, down_matrix, out_weight))
    near_steps = exp_count // 2
    far_steps = exp_count - near_steps
    gains = norm_gain.astype(F32)[None, :]

    near = [context] + [swap(context, "exp", k) for k in range(1, exp_count)]

    routes = modality * EXPERTS + expert
    hot = (routes[:, None] == jnp.arange(2 * EXPERTS, dtype=jnp.int32)[None, :]).astype(jnp.int32)
    earlier = jnp.cumsum(hot, axis=0) - hot
    position = jnp.sum(earlier * hot, axis=1)
    code = routes * slots + (role_at * exp_count + exp_at) * CAP + position

    from_exp = (jnp.arange(exp_count) ^ exp_at) // split
    from_role = jnp.arange(2) ^ role_at
    row_route = (from_role[None, :] * EXPERTS + from_exp[:, None])[:, :, None]
    row_target = (row_route * CAP + jnp.arange(CAP)).reshape(-1)
    picks = ((routes * CAP + position)[:, None] == row_target[None, :]).astype(BF16)

    lanes = 128
    marks = jnp.broadcast_to(code.astype(BF16)[:, None], (tok_rows, lanes))
    mine, other = pl.pallas_call(
        functools.partial(piece_kernel, exp_count),
        out_shape=[jax.ShapeDtypeStruct((exp_count, tok_rows, cols + lanes), BF16)] * 2,
        in_specs=[SMEM] + [VMEM] * 2,
        out_specs=[VMEM] * 2,
        compiler_params=pltpu.CompilerParams(vmem_limit_bytes=4 * MIB),
        name="piece",
    )(place, residual_in, marks)
    head_cols = context.shape[1]
    zeros = max(head_cols, cols + lanes)
    weight, done = fetch_weight(out_weight, [place, other, gains, picks], zeros)
    arrived = swap(other, "role", 1) + done[:, : cols + lanes]
    parted = [jnp.stack([mine[k], arrived[k]]) for k in range(exp_count)]
    near[0] = (context.reshape(-1, 8, head_cols) + done[:, :head_cols]).reshape(context.shape)

    gathered = [parted[0]] + [swap(parted[k], "exp", k) for k in range(1, exp_count)]
    blocks = []
    for value in near:
        blocks += [value, swap(value if blocks else context, "role", 1)]

    partial_sums = pl.pallas_call(
        functools.partial(project_kernel, tp_count, groups),
        out_shape=[jax.ShapeDtypeStruct((groups * tok_rows, cols), BF16)] * tp_count,
        in_specs=[SMEM] + [VMEM] * (groups + 1),
        out_specs=[VMEM] * tp_count,
        compiler_params=pltpu.CompilerParams(vmem_limit_bytes=(8 if groups <= 8 else 24) * MIB),
        name="project",
    )(place, *blocks, in_vmem([weight])[0])
    summands = [partial_sums[0]] + [swap(partial_sums[j], "tp", j) for j in range(1, tp_count)]

    gathered = jnp.stack(gathered).reshape(groups * tok_rows, cols + lanes)
    residual_cols = gathered[:, :cols]
    codes = gathered[:, cols].astype(jnp.int32)[None, :]

    places = [(q, side) for q in range(exp_count) for side in range(2)]
    ahead = near_steps
    up_block = fetch_up(
        places[2 * near_steps : 2 * near_steps + ahead], exp_count, cols, place, up_matrix, [partial_sums[0], gains, picks]
    )

    routed, after = [], up_block
    for steps in (range(near_steps), range(near_steps, exp_count)):
        kept, leaving = pl.pallas_call(
            functools.partial(slot_kernel, tp_count, exp_count, split, steps),
            out_shape=[jax.ShapeDtypeStruct((len(steps), slots, cols), BF16)] * 2,
            in_specs=[SMEM] + [VMEM] * (tp_count + 2) + [ANY],
            out_specs=[VMEM] * 2,
            compiler_params=pltpu.CompilerParams(
                vmem_limit_bytes=(6 if groups <= 8 else 24) * MIB
            ),
            name="slot",
        )(place, codes, residual_cols, *summands, after)
        arrived = swap(leaving, "role", 1)
        for at, q in enumerate(steps):
            both = jnp.stack([kept[at], arrived[at]])
            routed.append(swap(both, "exp", q) if q else both)
            after = both
    near_rows = jnp.stack(routed[:near_steps])
    far_rows = jnp.stack(routed[near_steps:])
    near_block = fetch_up(places[:1], exp_count, cols, place, up_matrix, [near_rows])
    near_all = [near_rows] + [swap(near_rows, "tp", j) for j in range(1, tp_count)]
    far_all = [far_rows] + [swap(far_rows, "tp", j) for j in range(1, tp_count)]

    rows = tp_count * slots
    small = rows <= 64
    half = near_steps * 2 * cols
    sums, squares, logits = pl.pallas_call(
        functools.partial(first_kernel, (tp_count, exp_count, split, near_steps)),
        out_shape=[
            pltpu.VMEM((rows, units), F32),
            pltpu.VMEM((rows, 128), F32),
            pltpu.VMEM((slots, 128), F32),
        ],
        in_specs=[SMEM] + [VMEM] * (3 + tp_count) + [HBM],
        out_specs=[VMEM] * 3,
        scratch_shapes=[
            pltpu.VMEM((rows, half), BF16),
            pltpu.VMEM((4, cols // 2, units), BF16),
            pltpu.SemaphoreType.DMA((4,)),
        ],
        compiler_params=pltpu.CompilerParams(vmem_limit_bytes=(14 if small else 36) * MIB),
        cost_estimate=pl.CostEstimate(
            flops=2 * rows * half * units, bytes_accessed=2 * half * units, transcendentals=0
        ),
        name="first",
    )(place, gains, router, *in_vmem([near_block]), *near_all, up_matrix)
    tile, depth = 256, 4
    early = width // cols * 5 // 8 * cols
    held = width // tile // 8 * tile
    sizes = (tp_count, exp_count, split, near_steps, far_steps, width, early)
    *early_outs, hidden, gate, held_block = pl.pallas_call(
        functools.partial(second_kernel, sizes),
        out_shape=[jax.ShapeDtypeStruct((slots, early), BF16)] * tp_count
        + [jax.ShapeDtypeStruct((rows, units), BF16), jax.ShapeDtypeStruct((slots, 128), F32)]
        + [pltpu.VMEM((units, held), BF16)],
        in_specs=[SMEM] + [VMEM] * (6 + tp_count) + [HBM] * 2,
        out_specs=[VMEM] * (tp_count + 3),
        scratch_shapes=[
            pltpu.VMEM((rows, width - half), BF16),
            pltpu.VMEM((rows, units), F32),
            pltpu.VMEM((4, cols // 2, units), BF16),
            pltpu.SemaphoreType.DMA((4,)),
            pltpu.VMEM((depth, units, tile), BF16),
            pltpu.SemaphoreType.DMA((depth,)),
            pltpu.SemaphoreType.DMA,
        ],
        compiler_params=pltpu.CompilerParams(vmem_limit_bytes=(21 if small else 40) * MIB),
        cost_estimate=pl.CostEstimate(
            flops=4 * rows * half * units, bytes_accessed=4 * half * units, transcendentals=0
        ),
        name="second",
    )(
        place, gains, router, *in_vmem([sums, squares, logits]), *far_all, *in_vmem([up_block]),
        up_matrix, down_matrix,
    )
    late_outs = pl.pallas_call(
        functools.partial(third_kernel, tp_count, early),
        out_shape=[jax.ShapeDtypeStruct((slots, width - early), BF16)] * tp_count,
        in_specs=[VMEM, VMEM, HBM],
        out_specs=[VMEM] * tp_count,
        scratch_shapes=[
            pltpu.VMEM((depth, units, tile), BF16),
            pltpu.SemaphoreType.DMA((depth,)),
        ],
        compiler_params=pltpu.CompilerParams(vmem_limit_bytes=(12 if small else 24) * MIB),
        cost_estimate=pl.CostEstimate(
            flops=2 * rows * half * units, bytes_accessed=2 * half * units, transcendentals=0
        ),
        name="third",
    )(hidden, *in_vmem([held_block]), down_matrix)

    early_sums = [early_outs[0]] + [swap(early_outs[j], "tp", j) for j in range(1, tp_count)]
    late_sums = [late_outs[0]] + [
        swap(late_outs[j] + 0 * early_sums[j][:, : width - early], "tp", j) for j in range(1, tp_count)
    ]
    all_rows = jnp.concatenate([near_rows, far_rows])
    home = ()
    for start, summands in ((0, early_sums), (early, late_sums)):
        size = summands[0].shape[1]
        home = pl.pallas_call(
            functools.partial(
                combine_kernel, tp_count, exp_count, split, start // cols, size
            ),
            out_shape=[jax.ShapeDtypeStruct((exp_count * CAP, width), BF16)] * 2,
            in_specs=[SMEM] + [VMEM] * (tp_count + 2 + len(home)),
            out_specs=[VMEM] * 2,
            input_output_aliases={tp_count + 3 + at: at for at in range(len(home))},
            compiler_params=pltpu.CompilerParams(vmem_limit_bytes=(8 if small else 40) * MIB),
            name="combine",
        )(place, all_rows, gate, *summands, *home)
    stay, leave = home
    back = swap(leave, "role", 1)
    pieces = []
    for q in range(exp_count):
        own = slice(q * CAP, (q + 1) * CAP)
        piece = jnp.concatenate([stay[own], back[own]])
        pieces.append(swap(piece, "exp", q) if q else piece)
    return pl.pallas_call(
        functools.partial(final_kernel, 1),
        out_shape=jax.ShapeDtypeStruct((tok_rows, width), BF16),
        in_specs=[VMEM] * (1 + len(pieces)),
        out_specs=VMEM,
        compiler_params=pltpu.CompilerParams(vmem_limit_bytes=8 * MIB),
        name="final",
    )(picks, *pieces)


def solution(mesh):
    in_specs = (
        P(("role", "exp", "tp"), None),
        P(("role", "exp"), "tp"),
        P("tp", ("role", "exp")),
        P(),
        P(),
        P("role", "exp", None, "tp"),
        P("role", "exp", "tp", None),
        P(("role", "exp", "tp")),
        P(("role", "exp", "tp")),
    )
    out_specs = P(("role", "exp", "tp"), None)
    return jax.shard_map(
        per_device, mesh=mesh, in_specs=in_specs, out_specs=out_specs, check_vma=False
    )
```

time: 116 us -> 106 us (0.914)
  waiting for transfers between devices: 27.6 us -> 14.9 us
  Pallas kernels: 44.9 us -> 48.2 us
    ppermute x34 -> x35, waiting for transfers between devices: 27.6 us -> 14.9 us  [swap(): return lax.ppermute(value, axis, [(i, i ^ distance) for i in range(size)])]
    pallas_call x2 -> x7, Pallas kernels: 6.11 us -> 14.3 us  [the longest x2 8.67 us: fetch_up(): pl.pallas_call(functools.partial(fetch_kernel, places, exp_count, cols),...]
    pallas_call x1, Pallas kernels: 10.1 us -> 8.1 us  [per_device(): pl.pallas_call(functools.partial(first_kernel, (tp_count, exp_count, spli...]
    pallas_call x1, Pallas kernels: 7.25 us -> 5.44 us  [per_device(): pl.pallas_call(functools.partial(third_kernel, tp_count, early), out_shap...]
    pallas_call x1, Pallas kernels: 3.46 us -> 1.82 us  [per_device(): pl.pallas_call(functools.partial(project_kernel, tp_count, groups), out_s...]
    ppermute x34 -> x35, starting transfers between devices: 37.5 us -> 37.6 us  [swap(): return lax.ppermute(value, axis, [(i, i ^ distance) for i in range(size)])]
  transfers between devices with their start and end apart: 34 -> 35, of which waited for: 18 -> 12; matrix products, arithmetic and copies ran while one was open for 3% -> 4% of each run, Pallas kernels for 20% -> 27%
where the time goes in v2:
time: 106 us
  Pallas kernels  48.2 us (45%)
  starting transfers between devices  37.6 us (35%)
  waiting for transfers between devices  14.9 us (14%)
  other arithmetic  3.53 us (3%)
  local copies, waits for them, and re-layouts  1.32 us (1%)
    ppermute x35, starting transfers between devices, swap(): return lax.ppermute(value, axis, [(i, i ^ distance) for i in range(size)])  37.6 us
    pallas_call x1, Pallas kernels, per_device(): pl.pallas_call(functools.partial(second_kernel, sizes), out_shape=[jax.Sh...  17.3 us
    ppermute x35, waiting for transfers between devices, swap(): return lax.ppermute(value, axis, [(i, i ^ distance) for i in range(size)])  14.9 us
    pallas_call x2, Pallas kernels, fetch_up(): pl.pallas_call(functools.partial(fetch_kernel, places, exp_count, cols),...  8.67 us
    pallas_call x1, Pallas kernels, per_device(): pl.pallas_call(functools.partial(first_kernel, (tp_count, exp_count, spli...  8.1 us
    pallas_call x1, Pallas kernels, per_device(): pl.pallas_call(functools.partial(third_kernel, tp_count, early), out_shap...  5.44 us
    pallas_call x1, Pallas kernels, fetch_weight(): pl.pallas_call(weight_kernel, out_shape=[pltpu.VMEM(matrix.shape, matrix....  2.21 us
  transfers between devices with their start and end apart: 35, of which 12 were waited for; matrix products, arithmetic and copies ran while one was open for 4% of the time, Pallas kernels for 27%

profile of v2, /device:TPU:0, one launch (start us, length us, event | category | flops | bytes accessed | tf_op | source)
XLA Modules:
  0.0 105.9 jit_solution(17448687943783605617)
XLA Ops:
  0.0 3.0 %collective-permute-start.5 = (bf16[32,2048]{1,0:T(8,128)(2,1)}, bf16[32,2048]{1,0:T(8,128)(2,1)S(1)}, u32[]{:S(2)}, u32[]{:S(2)}) collective-permute-start(bf16[32,2048]{1,0:T(8,128)(2,1)} %param.10), channel_id=1, source_target_pairs={{0,4},{4,0},{8,12},{12,8},{1,5},{5,1},{9,13},{13,9},{2,6},{6,2},{1... | collective-permute-start | bytes 393224 | tf_op jit(solution)/shard_map/ppermute | solution.py:25
  3.0 2.5 %collective-permute-start.9 = (bf16[32,2048]{1,0:T(8,128)(2,1)}, bf16[32,2048]{1,0:T(8,128)(2,1)S(1)}, u32[]{:S(2)}, u32[]{:S(2)}) collective-permute-start(bf16[32,2048]{1,0:T(8,128)(2,1)} %param.10), channel_id=1, source_target_pairs={{0,12},{4,8},{8,4},{12,0},{1,13},{5,9},{9,5},{13,1},{2,14},{6,10},... | collective-permute-start | bytes 393224 | tf_op jit(solution)/shard_map/ppermute | solution.py:25
  5.5 0.1 collective-permute-start.7
  5.6 0.7 multiply_add_fusion.1
  6.4 0.2 select_reduce_fusion
  6.7 0.9 copy-done.1
  7.7 0.6 piece.1
  8.2 0.3 collective-permute-start
  8.7 0.1 add.93
  8.8 0.7 broadcast_in_dim.9
  9.6 2.2 %fetch_weight.1 = (bf16[2048,1024]{1,0:T(8,128)(2,1)S(1)}, bf16[8,2048]{1,0:T(8,128)(2,1)S(1)}) custom-call(bf16[2048,1024]{1,0:T(8,128)(2,1)} %source_ref.1, s32[3]{0:T(128)S(1)} %pad_add_fusion.place_ref.refs_0_, bf16[4,8,1152]{2,1,0:T(8,128)(2,1)S(1)} %get-tuple-element.36.refs_1_, f32[1,8192]{1,0:T(1,128)S(1)} %bitcast.20, ...), custom_call_target="tpu_custom_call" | custom-call | bytes 4194304 | tf_op jit(solution)/shard_map/fetch_weight/pallas_call | solution.py:99
  11.8 0.9 bitcast_add_fusion.refs_0_
  12.8 1.7 %collective-permute-start.1 = (bf16[2,8,1152]{2,1,0:T(8,128)(2,1)S(1)}, bf16[2,8,1152]{2,1,0:T(8,128)(2,1)S(1)}, u32[]{:S(2)}, u32[]{:S(2)}) collective-permute-start(bf16[2,8,1152]{2,1,0:T(8,128)(2,1)S(1)} %pad_maximum_fusion.11), channel_id=1, source_target_pairs={{0,4},{4,0},{8,12},{12,8},{1,5},{5,1},{9,13},{13,9},{2,6},{6,2},{1... | collective-permute-start | bytes 110600 | tf_op jit(solution)/shard_map/ppermute | solution.py:25
  14.5 0.3 collective-permute-start.6
  14.8 1.8 %collective-permute-start.2 = (bf16[2,8,1152]{2,1,0:T(8,128)(2,1)S(1)}, bf16[2,8,1152]{2,1,0:T(8,128)(2,1)S(1)}, u32[]{:S(2)}, u32[]{:S(2)}) collective-permute-start(bf16[2,8,1152]{2,1,0:T(8,128)(2,1)S(1)} %pad_maximum_fusion.12), channel_id=1, source_target_pairs={{0,8},{4,12},{8,0},{12,4},{1,9},{5,13},{9,1},{13,5},{2,10},{6,14},... | collective-permute-start | bytes 110600 | tf_op jit(solution)/shard_map/ppermute | solution.py:25
  16.5 1.0 collective-permute-start.3
  17.5 1.0 collective-permute-done.7.refs_4_
  18.5 0.5 collective-permute-start.8
  19.1 0.8 collective-permute-done.10.refs_7_
  19.9 0.2 collective-permute-done.8.refs_5_
  20.1 1.8 %project.1 = (bf16[64,1024]{1,0:T(8,128)(2,1)S(1)}, bf16[64,1024]{1,0:T(8,128)(2,1)S(1)}, bf16[64,1024]{1,0:T(8,128)(2,1)S(1)}, bf16[64,1024]{1,0:T(8,128)(2,1)S(1)}) custom-call(s32[3]{0:T(128)S(1)} %pad_add_fusion.place_ref.refs_0_, bf16[32,2048]{1,0:T(8,128)(2,1)S(1)} %bitcast_add_fusion.refs_0_, bf16[32,2048]{1,0:T(8,128)(2,1)S(1)} %collective-permute-done.4.refs_1_, ...), custom_call_target="tpu_custom_call" | custom-call | tf_op jit(solution)/shard_map/project/pallas_call | solution.py:456
  21.9 1.6 %collective-permute-start.11 = (bf16[64,1024]{1,0:T(8,128)(2,1)S(1)}, bf16[64,1024]{1,0:T(8,128)(2,1)S(1)}, u32[]{:S(2)}, u32[]{:S(2)}) collective-permute-start(bf16[64,1024]{1,0:T(8,128)(2,1)S(1)} %get-tuple-element.40), channel_id=1, source_target_pairs={{0,1},{1,0},{2,3},{3,2},{4,5},{5,4},{6,7},{7,6},{8,9},{9,8},{10,11... | collective-permute-start | bytes 393224 | tf_op jit(solution)/shard_map/ppermute | solution.py:25
  23.4 1.5 %collective-permute-start.12 = (bf16[64,1024]{1,0:T(8,128)(2,1)S(1)}, bf16[64,1024]{1,0:T(8,128)(2,1)S(1)}, u32[]{:S(2)}, u32[]{:S(2)}) collective-permute-start(bf16[64,1024]{1,0:T(8,128)(2,1)S(1)} %get-tuple-element.41), channel_id=1, source_target_pairs={{0,2},{1,3},{2,0},{3,1},{4,6},{5,7},{6,4},{7,5},{8,10},{9,11},{10,... | collective-permute-start | bytes 393224 | tf_op jit(solution)/shard_map/ppermute | solution.py:25
  25.0 0.5 collective-permute-start.13
  25.5 0.1 convert_reduce_fusion
  25.6 5.3 %fetch_up.2.refs_4_ = bf16[2048,3072]{1,0:T(8,128)(2,1)S(1)} custom-call(s32[3]{0:T(128)S(1)} %pad_add_fusion.place_ref.refs_0_, bf16[8192,3072]{1,0:T(8,128)(2,1)} %bitcast.26, bf16[64,1024]{1,0:T(8,128)(2,1)S(1)} %get-tuple-element.39.refs_0_, f32[1,8192]{1,0:T(1,128)S(1)} %bitcast.21, bf16[8,16]{1,0:T(8,128)(2,1)S(1)} %compare_convert_fusion.refs_3_.refs_2_.picks_ref), custom_call_target="tpu_custom_call" | custom-call | bytes 12582912 | tf_op jit(solution)/shard_map/fetch_up/pallas_call | solution.py:57
  30.9 0.8 collective-permute-done.12.refs_2_
  31.7 0.8 slot.2
  32.6 1.2 %collective-permute-done.14 = bf16[2,16,1024]{2,1,0:T(8,128)(2,1)S(1)} collective-permute-done((bf16[2,16,1024]{2,1,0:T(8,128)(2,1)S(1)}, bf16[2,16,1024]{2,1,0:T(8,128)(2,1)S(1)}, u32[]{:S(2)}, u32[]{:S(2)}) %collective-permute-start.14) | collective-permute-done | bytes 65568 | tf_op jit(solution)/shard_map/ppermute | solution.py:25
  33.9 0.8 slot.3
  34.8 0.2 collective-permute-start.16
  35.0 1.1 %collective-permute-done.16 = bf16[2,16,1024]{2,1,0:T(8,128)(2,1)S(1)} collective-permute-done((bf16[2,16,1024]{2,1,0:T(8,128)(2,1)S(1)}, bf16[2,16,1024]{2,1,0:T(8,128)(2,1)S(1)}, u32[]{:S(2)}, u32[]{:S(2)}) %collective-permute-start.16) | collective-permute-done | bytes 65568 | tf_op jit(solution)/shard_map/ppermute | solution.py:25
  36.1 2.7 %collective-permute-start.18 = (bf16[2,16,1024]{2,1,0:T(8,128)(2,1)S(1)}, bf16[2,16,1024]{2,1,0:T(8,128)(2,1)S(1)}, u32[]{:S(2)}, u32[]{:S(2)}) collective-permute-start(bf16[2,16,1024]{2,1,0:T(8,128)(2,1)S(1)} %pad_maximum_fusion.6), channel_id=1, source_target_pairs={{0,12},{4,8},{8,4},{12,0},{1,13},{5,9},{9,5},{13,1},{2,14},{6,10},... | collective-permute-start | bytes 196616 | tf_op jit(solution)/shard_map/ppermute | solution.py:25
  38.8 0.9 collective-permute-start.17
  39.7 1.7 %collective-permute-start.21 = (bf16[2,2,16,1024]{3,2,1,0:T(8,128)(2,1)S(1)}, bf16[2,2,16,1024]{3,2,1,0:T(8,128)(2,1)S(1)}, u32[]{:S(2)}, u32[]{:S(2)}) collective-permute-start(bf16[2,2,16,1024]{3,2,1,0:T(8,128)(2,1)S(1)} %pad_maximum_fusion.2.refs_0_), channel_id=1, source_target_pairs={{0,3},{1,2},{2,1},{3,0},{4,7},{5,6},{6,5},{7,4},{8,11},{9,10},{10,... | collective-permute-start | bytes 393224 | tf_op jit(solution)/shard_map/ppermute | solution.py:25
  41.5 1.0 collective-permute-start.20
  42.5 0.8 collective-permute-start.19
  43.3 3.4 %fetch_up.3.up_ref = bf16[1024,3072]{1,0:T(8,128)(2,1)S(1)} custom-call(s32[3]{0:T(128)S(1)} %pad_add_fusion.place_ref.refs_0_, bf16[8192,3072]{1,0:T(8,128)(2,1)} %bitcast.27, bf16[2,2,16,1024]{3,2,1,0:T(8,128)(2,1)S(1)} %pad_maximum_fusion.2.refs_0_), custom_call_target="tpu_custom_call" | custom-call | bytes 6291456 | tf_op jit(solution)/shard_map/fetch_up/pallas_call | solution.py:57
  46.8 1.7 %collective-permute-start.24 = (bf16[2,2,16,1024]{3,2,1,0:T(8,128)(2,1)S(1)}, bf16[2,2,16,1024]{3,2,1,0:T(8,128)(2,1)S(1)}, u32[]{:S(2)}, u32[]{:S(2)}) collective-permute-start(bf16[2,2,16,1024]{3,2,1,0:T(8,128)(2,1)S(1)} %pad_maximum_fusion.3.refs_0_), channel_id=1, source_target_pairs={{0,3},{1,2},{2,1},{3,0},{4,7},{5,6},{6,5},{7,4},{8,11},{9,10},{10,... | collective-permute-start | bytes 393224 | tf_op jit(solution)/shard_map/ppermute | solution.py:25
  48.5 1.0 collective-permute-start.23
  49.5 0.8 collective-permute-start.22
  50.3 8.1 %first.1 = (f32[64,3072]{1,0:T(8,128)S(1)}, f32[64,128]{1,0:T(8,128)S(1)}, f32[16,128]{1,0:T(8,128)S(1)}) custom-call(s32[3]{0:T(128)S(1)} %pad_add_fusion.place_ref.refs_0_, f32[1,8192]{1,0:T(1,128)S(1)} %bitcast.22, bf16[2,4,8192]{2,1,0:T(4,128)(2,1)S(1)} %copy-done, bf16[1024,3072]{1,0:T(8,128)(2,1)S(1)} %fetch_up.3.up_ref, ...), custom_call_target="tpu_custom_call" | custom-call | flops 1610612736 | bytes 25165824 | tf_op jit(solution)/shard_map/first/pallas_call | solution.py:502
  58.5 17.3 %second.1 = (bf16[16,5120]{1,0:T(8,128)(2,1)S(1)}, bf16[16,5120]{1,0:T(8,128)(2,1)S(1)}, bf16[16,5120]{1,0:T(8,128)(2,1)S(1)}, bf16[16,5120]{1,0:T(8,128)(2,1)S(...) custom-call(s32[3]{0:T(128)S(1)} %pad_add_fusion.place_ref.refs_0_, ...), custom_call_target="tpu_custom_call" | custom-call | flops 3221225472 | bytes 50331648 | tf_op jit(solution)/shard_map/second/pallas_call | solution.py:526
  75.7 1.3 %collective-permute-start.25 = (bf16[16,5120]{1,0:T(8,128)(2,1)S(1)}, bf16[16,5120]{1,0:T(8,128)(2,1)S(1)}, u32[]{:S(2)}, u32[]{:S(2)}) collective-permute-start(bf16[16,5120]{1,0:T(8,128)(2,1)S(1)} %get-tuple-element.55), channel_id=1, source_target_pairs={{0,1},{1,0},{2,3},{3,2},{4,5},{5,4},{6,7},{7,6},{8,9},{9,8},{10,11... | collective-permute-start | bytes 491528 | tf_op jit(solution)/shard_map/ppermute | solution.py:25
  77.0 1.0 collective-permute-start.27
  78.0 1.3 %collective-permute-start.29 = (bf16[16,5120]{1,0:T(8,128)(2,1)S(1)}, bf16[16,5120]{1,0:T(8,128)(2,1)S(1)}, u32[]{:S(2)}, u32[]{:S(2)}) collective-permute-start(bf16[16,5120]{1,0:T(8,128)(2,1)S(1)} %get-tuple-element.59), channel_id=1, source_target_pairs={{0,3},{1,2},{2,1},{3,0},{4,7},{5,6},{6,5},{7,4},{8,11},{9,10},{10,... | collective-permute-start | bytes 491528 | tf_op jit(solution)/shard_map/ppermute | solution.py:25
  79.3 5.4 %third.1 = (bf16[16,3072]{1,0:T(8,128)(2,1)S(1)}, bf16[16,3072]{1,0:T(8,128)(2,1)S(1)}, bf16[16,3072]{1,0:T(8,128)(2,1)S(1)}, bf16[16,3072]{1,0:T(8,128)(2,1)S(1)}) custom-call(bf16[64,3072]{1,0:T(8,128)(2,1)S(1)} %get-tuple-element.51.hidden, bf16[3072,1024]{1,0:T(8,128)(2,1)S(1)} %get-tuple-element.52.held_ref, bf16[3072,8192]{1,0:T(8,128)(2,1)} %bitcast.31), custom_call_target="tpu_custom_call" | custom-call | flops 1610612736 | bytes 25165824 | tf_op jit(solution)/shard_map/third/pallas_call | solution.py:551
  84.8 1.3 %collective-permute-start.26 = (bf16[16,3072]{1,0:T(8,128)(2,1)S(1)}, bf16[16,3072]{1,0:T(8,128)(2,1)S(1)}, u32[]{:S(2)}, u32[]{:S(2)}) collective-permute-start(bf16[16,3072]{1,0:T(8,128)(2,1)S(1)} %fusion.2), channel_id=1, source_target_pairs={{0,1},{1,0},{2,3},{3,2},{4,5},{5,4},{6,7},{7,6},{8,9},{9,8},{10,11... | collective-permute-start | bytes 294920 | tf_op jit(solution)/shard_map/ppermute | solution.py:25
  86.1 1.0 collective-permute-start.28
  87.1 1.3 %collective-permute-start.30 = (bf16[16,3072]{1,0:T(8,128)(2,1)S(1)}, bf16[16,3072]{1,0:T(8,128)(2,1)S(1)}, u32[]{:S(2)}, u32[]{:S(2)}) collective-permute-start(bf16[16,3072]{1,0:T(8,128)(2,1)S(1)} %fusion), channel_id=1, source_target_pairs={{0,3},{1,2},{2,1},{3,0},{4,7},{5,6},{6,5},{7,4},{8,11},{9,10},{10,... | collective-permute-start | bytes 294920 | tf_op jit(solution)/shard_map/ppermute | solution.py:25
  88.5 0.7 combine.2
  89.2 0.2 collective-permute-done.26.refs_1_
  89.5 1.3 %collective-permute-done.28.refs_2_ = bf16[16,3072]{1,0:T(8,128)(2,1)S(1)} collective-permute-done((bf16[16,3072]{1,0:T(8,128)(2,1)S(1)}, bf16[16,3072]{1,0:T(8,128)(2,1)S(1)}, u32[]{:S(2)}, u32[]{:S(2)}) %collective-permute-start.28) | collective-permute-done | bytes 98336 | tf_op jit(solution)/shard_map/ppermute | solution.py:25
  90.8 2.0 %collective-permute-done.30.refs_3_ = bf16[16,3072]{1,0:T(8,128)(2,1)S(1)} collective-permute-done((bf16[16,3072]{1,0:T(8,128)(2,1)S(1)}, bf16[16,3072]{1,0:T(8,128)(2,1)S(1)}, u32[]{:S(2)}, u32[]{:S(2)}) %collective-permute-start.30) | collective-permute-done | bytes 98336 | tf_op jit(solution)/shard_map/ppermute | solution.py:25
  92.7 0.6 combine.3
  93.4 0.1 fusion.4
  93.5 1.2 %collective-permute-done.31 = bf16[8,8192]{1,0:T(8,128)(2,1)S(1)} collective-permute-done((bf16[8,8192]{1,0:T(8,128)(2,1)S(1)}, bf16[8,8192]{1,0:T(8,128)(2,1)S(1)}, u32[]{:S(2)}, u32[]{:S(2)}) %collective-permute-start.31) | collective-permute-done | bytes 131104 | tf_op jit(solution)/shard_map/ppermute | solution.py:25
  94.8 0.1 fusion.5
  95.0 1.0 collective-permute-start.32
  96.0 2.3 %collective-permute-start.33 = (bf16[4,8192]{1,0:T(4,128)(2,1)S(1)}, bf16[4,8192]{1,0:T(4,128)(2,1)S(1)}, u32[]{:S(2)}, u32[]{:S(2)}) collective-permute-start(bf16[4,8192]{1,0:T(4,128)(2,1)S(1)} %pad_maximum_fusion.9), channel_id=1, source_target_pairs={{0,8},{4,12},{8,0},{12,4},{1,9},{5,13},{9,1},{13,5},{2,10},{6,14},... | collective-permute-start | bytes 196616 | tf_op jit(solution)/shard_map/ppermute | solution.py:25
  98.4 1.3 %collective-permute-start.34 = (bf16[4,8192]{1,0:T(4,128)(2,1)S(1)}, bf16[4,8192]{1,0:T(4,128)(2,1)S(1)}, u32[]{:S(2)}, u32[]{:S(2)}) collective-permute-start(bf16[4,8192]{1,0:T(4,128)(2,1)S(1)} %pad_maximum_fusion.10), channel_id=1, source_target_pairs={{0,12},{4,8},{8,4},{12,0},{1,13},{5,9},{9,5},{13,1},{2,14},{6,10},... | collective-permute-start | bytes 196616 | tf_op jit(solution)/shard_map/ppermute | solution.py:25
  99.8 3.7 %collective-permute-done.33.refs_2_ = bf16[4,8192]{1,0:T(4,128)(2,1)S(1)} collective-permute-done((bf16[4,8192]{1,0:T(4,128)(2,1)S(1)}, bf16[4,8192]{1,0:T(4,128)(2,1)S(1)}, u32[]{:S(2)}, u32[]{:S(2)}) %collective-permute-start.33) | collective-permute-done | bytes 65568 | tf_op jit(solution)/shard_map/ppermute | solution.py:25
  103.5 1.2 %collective-permute-done.34.refs_3_ = bf16[4,8192]{1,0:T(4,128)(2,1)S(1)} collective-permute-done((bf16[4,8192]{1,0:T(4,128)(2,1)S(1)}, bf16[4,8192]{1,0:T(4,128)(2,1)S(1)}, u32[]{:S(2)}, u32[]{:S(2)}) %collective-permute-start.34) | collective-permute-done | bytes 65568 | tf_op jit(solution)/shard_map/ppermute | solution.py:25
  104.7 1.2 %final.1 = bf16[8,8192]{1,0:T(8,128)(2,1)} custom-call(bf16[8,16]{1,0:T(8,128)(2,1)S(1)} %compare_convert_fusion.refs_3_.refs_2_.picks_ref, bf16[4,8192]{1,0:T(4,128)(2,1)S(1)} %pad_maximum_fusion.7.refs_0_, bf16[4,8192]{1,0:T(4,128)(2,1)S(1)} %collective-permute-done.32.refs_1_, bf16[4,8192]{1,0:T(4,128)(2,1)S(1)} %collective-permute-done.33.refs_2_, ...), custom_call_target="tpu_custom_call" | custom-call | tf_op jit(solution)/shard_map/final/pallas_call | solution.py:593
  (69 shorter events, 1.3 us)
Async XLA Ops:
  0.0 14.5 %collective-permute-start.5 = (bf16[32,2048]{1,0:T(8,128)(2,1)}, bf16[32,2048]{1,0:T(8,128)(2,1)S(1)}, u32[]{:S(2)}, u32[]{:S(2)}) collective-permute-start(bf16[32,2048]{1,0:T(8,128)(2,1)} %param.10), channel_id=1, source_target_pairs={{0,4},{4,0},{8,12},{12,8},{1,5},{5,1},{9,13},{13,9},{2,6},{6,2},{1... | collective-permute-start | bytes 393224 | tf_op jit(solution)/shard_map/ppermute | solution.py:25
  3.0 11.7 %collective-permute-start.4 = (bf16[32,2048]{1,0:T(8,128)(2,1)}, bf16[32,2048]{1,0:T(8,128)(2,1)S(1)}, u32[]{:S(2)}, u32[]{:S(2)}) collective-permute-start(bf16[32,2048]{1,0:T(8,128)(2,1)} %param.10), channel_id=1, source_target_pairs={{0,16},{16,0},{1,17},{17,1},{2,18},{18,2},{3,19},{19,3},{4,20},{20... | collective-permute-start | bytes 393224 | tf_op jit(solution)/shard_map/ppermute | solution.py:25
  3.0 13.5 %collective-permute-start.9 = (bf16[32,2048]{1,0:T(8,128)(2,1)}, bf16[32,2048]{1,0:T(8,128)(2,1)S(1)}, u32[]{:S(2)}, u32[]{:S(2)}) collective-permute-start(bf16[32,2048]{1,0:T(8,128)(2,1)} %param.10), channel_id=1, source_target_pairs={{0,12},{4,8},{8,4},{12,0},{1,13},{5,9},{9,5},{13,1},{2,14},{6,10},... | collective-permute-start | bytes 393224 | tf_op jit(solution)/shard_map/ppermute | solution.py:25
  5.5 13.0 %collective-permute-start.7 = (bf16[32,2048]{1,0:T(8,128)(2,1)}, bf16[32,2048]{1,0:T(8,128)(2,1)S(1)}, u32[]{:S(2)}, u32[]{:S(2)}) collective-permute-start(bf16[32,2048]{1,0:T(8,128)(2,1)} %param.10), channel_id=1, source_target_pairs={{0,8},{4,12},{8,0},{12,4},{1,9},{5,13},{9,1},{13,5},{2,10},{6,14},... | collective-permute-start | bytes 393224 | tf_op jit(solution)/shard_map/ppermute | solution.py:25
  6.7 0.9 copy-start.1
  8.2 4.5 %collective-permute-start = (bf16[4,8,1152]{2,1,0:T(8,128)(2,1)S(1)}, bf16[4,8,1152]{2,1,0:T(8,128)(2,1)S(1)}, u32[]{:S(2)}, u32[]{:S(2)}) collective-permute-start(bf16[4,8,1152]{2,1,0:T(8,128)(2,1)S(1)} %get-tuple-element.36.refs_1_), channel_id=1, source_target_pairs={{0,16},{16,0},{1,17},{17,1},{2,18},{18,2},{3,19},{19,3},{4,20},{20... | collective-permute-start | bytes 221192 | tf_op jit(solution)/shard_map/ppermute | solution.py:25
  12.8 12.2 %collective-permute-start.1 = (bf16[2,8,1152]{2,1,0:T(8,128)(2,1)S(1)}, bf16[2,8,1152]{2,1,0:T(8,128)(2,1)S(1)}, u32[]{:S(2)}, u32[]{:S(2)}) collective-permute-start(bf16[2,8,1152]{2,1,0:T(8,128)(2,1)S(1)} %pad_maximum_fusion.11), channel_id=1, source_target_pairs={{0,4},{4,0},{8,12},{12,8},{1,5},{5,1},{9,13},{13,9},{2,6},{6,2},{1... | collective-permute-start | bytes 110600 | tf_op jit(solution)/shard_map/ppermute | solution.py:25
  14.5 4.1 %collective-permute-start.6 = (bf16[32,2048]{1,0:T(8,128)(2,1)S(1)}, bf16[32,2048]{1,0:T(8,128)(2,1)S(1)}, u32[]{:S(2)}, u32[]{:S(2)}) collective-permute-start(bf16[32,2048]{1,0:T(8,128)(2,1)S(1)} %collective-permute-done.5.refs_2_), channel_id=1, source_target_pairs={{0,16},{16,0},{1,17},{17,1},{2,18},{18,2},{3,19},{19,3},{4,20},{20... | collective-permute-start | bytes 393224 | tf_op jit(solution)/shard_map/ppermute | solution.py:25
  14.8 10.7 %collective-permute-start.2 = (bf16[2,8,1152]{2,1,0:T(8,128)(2,1)S(1)}, bf16[2,8,1152]{2,1,0:T(8,128)(2,1)S(1)}, u32[]{:S(2)}, u32[]{:S(2)}) collective-permute-start(bf16[2,8,1152]{2,1,0:T(8,128)(2,1)S(1)} %pad_maximum_fusion.12), channel_id=1, source_target_pairs={{0,8},{4,12},{8,0},{12,4},{1,9},{5,13},{9,1},{13,5},{2,10},{6,14},... | collective-permute-start | bytes 110600 | tf_op jit(solution)/shard_map/ppermute | solution.py:25
  16.5 8.9 %collective-permute-start.3 = (bf16[2,8,1152]{2,1,0:T(8,128)(2,1)S(1)}, bf16[2,8,1152]{2,1,0:T(8,128)(2,1)S(1)}, u32[]{:S(2)}, u32[]{:S(2)}) collective-permute-start(bf16[2,8,1152]{2,1,0:T(8,128)(2,1)S(1)} %pad_maximum_fusion.13), channel_id=1, source_target_pairs={{0,12},{4,8},{8,4},{12,0},{1,13},{5,9},{9,5},{13,1},{2,14},{6,10},... | collective-permute-start | bytes 110600 | tf_op jit(solution)/shard_map/ppermute | solution.py:25
  18.5 1.3 %collective-permute-start.10 = (bf16[32,2048]{1,0:T(8,128)(2,1)S(1)}, bf16[32,2048]{1,0:T(8,128)(2,1)S(1)}, u32[]{:S(2)}, u32[]{:S(2)}) collective-permute-start(bf16[32,2048]{1,0:T(8,128)(2,1)S(1)} %collective-permute-done.9.refs_6_), channel_id=1, source_target_pairs={{0,16},{16,0},{1,17},{17,1},{2,18},{18,2},{3,19},{19,3},{4,20},{20... | collective-permute-start | bytes 393224 | tf_op jit(solution)/shard_map/ppermute | solution.py:25
  18.5 1.5 %collective-permute-start.8 = (bf16[32,2048]{1,0:T(8,128)(2,1)S(1)}, bf16[32,2048]{1,0:T(8,128)(2,1)S(1)}, u32[]{:S(2)}, u32[]{:S(2)}) collective-permute-start(bf16[32,2048]{1,0:T(8,128)(2,1)S(1)} %collective-permute-done.7.refs_4_), channel_id=1, source_target_pairs={{0,16},{16,0},{1,17},{17,1},{2,18},{18,2},{3,19},{19,3},{4,20},{20... | collective-permute-start | bytes 393224 | tf_op jit(solution)/shard_map/ppermute | solution.py:25
  21.9 9.0 %collective-permute-start.11 = (bf16[64,1024]{1,0:T(8,128)(2,1)S(1)}, bf16[64,1024]{1,0:T(8,128)(2,1)S(1)}, u32[]{:S(2)}, u32[]{:S(2)}) collective-permute-start(bf16[64,1024]{1,0:T(8,128)(2,1)S(1)} %get-tuple-element.40), channel_id=1, source_target_pairs={{0,1},{1,0},{2,3},{3,2},{4,5},{5,4},{6,7},{7,6},{8,9},{9,8},{10,11... | collective-permute-start | bytes 393224 | tf_op jit(solution)/shard_map/ppermute | solution.py:25
  23.4 8.3 %collective-permute-start.12 = (bf16[64,1024]{1,0:T(8,128)(2,1)S(1)}, bf16[64,1024]{1,0:T(8,128)(2,1)S(1)}, u32[]{:S(2)}, u32[]{:S(2)}) collective-permute-start(bf16[64,1024]{1,0:T(8,128)(2,1)S(1)} %get-tuple-element.41), channel_id=1, source_target_pairs={{0,2},{1,3},{2,0},{3,1},{4,6},{5,7},{6,4},{7,5},{8,10},{9,11},{10,... | collective-permute-start | bytes 393224 | tf_op jit(solution)/shard_map/ppermute | solution.py:25
  25.0 6.7 %collective-permute-start.13 = (bf16[64,1024]{1,0:T(8,128)(2,1)S(1)}, bf16[64,1024]{1,0:T(8,128)(2,1)S(1)}, u32[]{:S(2)}, u32[]{:S(2)}) collective-permute-start(bf16[64,1024]{1,0:T(8,128)(2,1)S(1)} %get-tuple-element.42), channel_id=1, source_target_pairs={{0,3},{1,2},{2,1},{3,0},{4,7},{5,6},{6,5},{7,4},{8,11},{9,10},{10,... | collective-permute-start | bytes 393224 | tf_op jit(solution)/shard_map/ppermute | solution.py:25
  32.5 1.3 %collective-permute-start.14 = (bf16[2,16,1024]{2,1,0:T(8,128)(2,1)S(1)}, bf16[2,16,1024]{2,1,0:T(8,128)(2,1)S(1)}, u32[]{:S(2)}, u32[]{:S(2)}) collective-permute-start(bf16[2,16,1024]{2,1,0:T(8,128)(2,1)S(1)} %get-tuple-element.44), channel_id=1, source_target_pairs={{0,16},{16,0},{1,17},{17,1},{2,18},{18,2},{3,19},{19,3},{4,20},{20... | collective-permute-start | bytes 196616 | tf_op jit(solution)/shard_map/ppermute | solution.py:25
  33.9 5.9 %collective-permute-start.15 = (bf16[2,16,1024]{2,1,0:T(8,128)(2,1)S(1)}, bf16[2,16,1024]{2,1,0:T(8,128)(2,1)S(1)}, u32[]{:S(2)}, u32[]{:S(2)}) collective-permute-start(bf16[2,16,1024]{2,1,0:T(8,128)(2,1)S(1)} %pad_maximum_fusion.4.refs_4_), channel_id=1, source_target_pairs={{0,4},{4,0},{8,12},{12,8},{1,5},{5,1},{9,13},{13,9},{2,6},{6,2},{1... | collective-permute-start | bytes 196616 | tf_op jit(solution)/shard_map/ppermute | solution.py:25
  34.8 1.3 %collective-permute-start.16 = (bf16[2,16,1024]{2,1,0:T(8,128)(2,1)S(1)}, bf16[2,16,1024]{2,1,0:T(8,128)(2,1)S(1)}, u32[]{:S(2)}, u32[]{:S(2)}) collective-permute-start(bf16[2,16,1024]{2,1,0:T(8,128)(2,1)S(1)} %get-tuple-element.46), channel_id=1, source_target_pairs={{0,16},{16,0},{1,17},{17,1},{2,18},{18,2},{3,19},{19,3},{4,20},{20... | collective-permute-start | bytes 196616 | tf_op jit(solution)/shard_map/ppermute | solution.py:25
  36.1 10.6 %collective-permute-start.18 = (bf16[2,16,1024]{2,1,0:T(8,128)(2,1)S(1)}, bf16[2,16,1024]{2,1,0:T(8,128)(2,1)S(1)}, u32[]{:S(2)}, u32[]{:S(2)}) collective-permute-start(bf16[2,16,1024]{2,1,0:T(8,128)(2,1)S(1)} %pad_maximum_fusion.6), channel_id=1, source_target_pairs={{0,12},{4,8},{8,4},{12,0},{1,13},{5,9},{9,5},{13,1},{2,14},{6,10},... | collective-permute-start | bytes 196616 | tf_op jit(solution)/shard_map/ppermute | solution.py:25
  38.8 7.9 %collective-permute-start.17 = (bf16[2,16,1024]{2,1,0:T(8,128)(2,1)S(1)}, bf16[2,16,1024]{2,1,0:T(8,128)(2,1)S(1)}, u32[]{:S(2)}, u32[]{:S(2)}) collective-permute-start(bf16[2,16,1024]{2,1,0:T(8,128)(2,1)S(1)} %pad_maximum_fusion.5), channel_id=1, source_target_pairs={{0,8},{4,12},{8,0},{12,4},{1,9},{5,13},{9,1},{13,5},{2,10},{6,14},... | collective-permute-start | bytes 196616 | tf_op jit(solution)/shard_map/ppermute | solution.py:25
  39.7 10.6 %copy-start = (bf16[2,4,8192]{2,1,0:T(4,128)(2,1)S(1)}, bf16[2,4,8192]{2,1,0:T(4,128)(2,1)}, u32[]{:S(2)}) copy-start(bf16[2,4,8192]{2,1,0:T(4,128)(2,1)} %router_ref.3) | copy-start | bytes 393220
  39.7 9.8 %collective-permute-start.21 = (bf16[2,2,16,1024]{3,2,1,0:T(8,128)(2,1)S(1)}, bf16[2,2,16,1024]{3,2,1,0:T(8,128)(2,1)S(1)}, u32[]{:S(2)}, u32[]{:S(2)}) collective-permute-start(bf16[2,2,16,1024]{3,2,1,0:T(8,128)(2,1)S(1)} %pad_maximum_fusion.2.refs_0_), channel_id=1, source_target_pairs={{0,3},{1,2},{2,1},{3,0},{4,7},{5,6},{6,5},{7,4},{8,11},{9,10},{10,... | collective-permute-start | bytes 393224 | tf_op jit(solution)/shard_map/ppermute | solution.py:25
  41.5 8.9 %collective-permute-start.20 = (bf16[2,2,16,1024]{3,2,1,0:T(8,128)(2,1)S(1)}, bf16[2,2,16,1024]{3,2,1,0:T(8,128)(2,1)S(1)}, u32[]{:S(2)}, u32[]{:S(2)}) collective-permute-start(bf16[2,2,16,1024]{3,2,1,0:T(8,128)(2,1)S(1)} %pad_maximum_fusion.2.refs_0_), channel_id=1, source_target_pairs={{0,2},{1,3},{2,0},{3,1},{4,6},{5,7},{6,4},{7,5},{8,10},{9,11},{10,... | collective-permute-start | bytes 393224 | tf_op jit(solution)/shard_map/ppermute | solution.py:25
  42.5 7.8 %collective-permute-start.19 = (bf16[2,2,16,1024]{3,2,1,0:T(8,128)(2,1)S(1)}, bf16[2,2,16,1024]{3,2,1,0:T(8,128)(2,1)S(1)}, u32[]{:S(2)}, u32[]{:S(2)}) collective-permute-start(bf16[2,2,16,1024]{3,2,1,0:T(8,128)(2,1)S(1)} %pad_maximum_fusion.2.refs_0_), channel_id=1, source_target_pairs={{0,1},{1,0},{2,3},{3,2},{4,5},{5,4},{6,7},{7,6},{8,9},{9,8},{10,11... | collective-permute-start | bytes 393224 | tf_op jit(solution)/shard_map/ppermute | solution.py:25
  46.8 11.7 %collective-permute-start.24 = (bf16[2,2,16,1024]{3,2,1,0:T(8,128)(2,1)S(1)}, bf16[2,2,16,1024]{3,2,1,0:T(8,128)(2,1)S(1)}, u32[]{:S(2)}, u32[]{:S(2)}) collective-permute-start(bf16[2,2,16,1024]{3,2,1,0:T(8,128)(2,1)S(1)} %pad_maximum_fusion.3.refs_0_), channel_id=1, source_target_pairs={{0,3},{1,2},{2,1},{3,0},{4,7},{5,6},{6,5},{7,4},{8,11},{9,10},{10,... | collective-permute-start | bytes 393224 | tf_op jit(solution)/shard_map/ppermute | solution.py:25
  48.5 10.0 %collective-permute-start.23 = (bf16[2,2,16,1024]{3,2,1,0:T(8,128)(2,1)S(1)}, bf16[2,2,16,1024]{3,2,1,0:T(8,128)(2,1)S(1)}, u32[]{:S(2)}, u32[]{:S(2)}) collective-permute-start(bf16[2,2,16,1024]{3,2,1,0:T(8,128)(2,1)S(1)} %pad_maximum_fusion.3.refs_0_), channel_id=1, source_target_pairs={{0,2},{1,3},{2,0},{3,1},{4,6},{5,7},{6,4},{7,5},{8,10},{9,11},{10,... | collective-permute-start | bytes 393224 | tf_op jit(solution)/shard_map/ppermute | solution.py:25
  49.5 8.9 %collective-permute-start.22 = (bf16[2,2,16,1024]{3,2,1,0:T(8,128)(2,1)S(1)}, bf16[2,2,16,1024]{3,2,1,0:T(8,128)(2,1)S(1)}, u32[]{:S(2)}, u32[]{:S(2)}) collective-permute-start(bf16[2,2,16,1024]{3,2,1,0:T(8,128)(2,1)S(1)} %pad_maximum_fusion.3.refs_0_), channel_id=1, source_target_pairs={{0,1},{1,0},{2,3},{3,2},{4,5},{5,4},{6,7},{7,6},{8,9},{9,8},{10,11... | collective-permute-start | bytes 393224 | tf_op jit(solution)/shard_map/ppermute | solution.py:25
  75.7 9.0 %collective-permute-start.25 = (bf16[16,5120]{1,0:T(8,128)(2,1)S(1)}, bf16[16,5120]{1,0:T(8,128)(2,1)S(1)}, u32[]{:S(2)}, u32[]{:S(2)}) collective-permute-start(bf16[16,5120]{1,0:T(8,128)(2,1)S(1)} %get-tuple-element.55), channel_id=1, source_target_pairs={{0,1},{1,0},{2,3},{3,2},{4,5},{5,4},{6,7},{7,6},{8,9},{9,8},{10,11... | collective-permute-start | bytes 491528 | tf_op jit(solution)/shard_map/ppermute | solution.py:25
  77.0 9.0 %collective-permute-start.27 = (bf16[16,5120]{1,0:T(8,128)(2,1)S(1)}, bf16[16,5120]{1,0:T(8,128)(2,1)S(1)}, u32[]{:S(2)}, u32[]{:S(2)}) collective-permute-start(bf16[16,5120]{1,0:T(8,128)(2,1)S(1)} %get-tuple-element.57), channel_id=1, source_target_pairs={{0,2},{1,3},{2,0},{3,1},{4,6},{5,7},{6,4},{7,5},{8,10},{9,11},{10,... | collective-permute-start | bytes 491528 | tf_op jit(solution)/shard_map/ppermute | solution.py:25
  78.0 9.1 %collective-permute-start.29 = (bf16[16,5120]{1,0:T(8,128)(2,1)S(1)}, bf16[16,5120]{1,0:T(8,128)(2,1)S(1)}, u32[]{:S(2)}, u32[]{:S(2)}) collective-permute-start(bf16[16,5120]{1,0:T(8,128)(2,1)S(1)} %get-tuple-element.59), channel_id=1, source_target_pairs={{0,3},{1,2},{2,1},{3,0},{4,7},{5,6},{6,5},{7,4},{8,11},{9,10},{10,... | collective-permute-start | bytes 491528 | tf_op jit(solution)/shard_map/ppermute | solution.py:25
  84.8 4.7 %collective-permute-start.26 = (bf16[16,3072]{1,0:T(8,128)(2,1)S(1)}, bf16[16,3072]{1,0:T(8,128)(2,1)S(1)}, u32[]{:S(2)}, u32[]{:S(2)}) collective-permute-start(bf16[16,3072]{1,0:T(8,128)(2,1)S(1)} %fusion.2), channel_id=1, source_target_pairs={{0,1},{1,0},{2,3},{3,2},{4,5},{5,4},{6,7},{7,6},{8,9},{9,8},{10,11... | collective-permute-start | bytes 294920 | tf_op jit(solution)/shard_map/ppermute | solution.py:25
  86.1 4.7 %collective-permute-start.28 = (bf16[16,3072]{1,0:T(8,128)(2,1)S(1)}, bf16[16,3072]{1,0:T(8,128)(2,1)S(1)}, u32[]{:S(2)}, u32[]{:S(2)}) collective-permute-start(bf16[16,3072]{1,0:T(8,128)(2,1)S(1)} %fusion.1), channel_id=1, source_target_pairs={{0,2},{1,3},{2,0},{3,1},{4,6},{5,7},{6,4},{7,5},{8,10},{9,11},{10,... | collective-permute-start | bytes 294920 | tf_op jit(solution)/shard_map/ppermute | solution.py:25
  87.1 5.6 %collective-permute-start.30 = (bf16[16,3072]{1,0:T(8,128)(2,1)S(1)}, bf16[16,3072]{1,0:T(8,128)(2,1)S(1)}, u32[]{:S(2)}, u32[]{:S(2)}) collective-permute-start(bf16[16,3072]{1,0:T(8,128)(2,1)S(1)} %fusion), channel_id=1, source_target_pairs={{0,3},{1,2},{2,1},{3,0},{4,7},{5,6},{6,5},{7,4},{8,11},{9,10},{10,... | collective-permute-start | bytes 294920 | tf_op jit(solution)/shard_map/ppermute | solution.py:25
  93.4 1.4 %collective-permute-start.31 = (bf16[8,8192]{1,0:T(8,128)(2,1)S(1)}, bf16[8,8192]{1,0:T(8,128)(2,1)S(1)}, u32[]{:S(2)}, u32[]{:S(2)}) collective-permute-start(bf16[8,8192]{1,0:T(8,128)(2,1)S(1)} %get-tuple-element.64), channel_id=1, source_target_pairs={{0,16},{16,0},{1,17},{17,1},{2,18},{18,2},{3,19},{19,3},{4,20},{20... | collective-permute-start | bytes 393224 | tf_op jit(solution)/shard_map/ppermute | solution.py:25
  95.0 4.8 %collective-permute-start.32 = (bf16[4,8192]{1,0:T(4,128)(2,1)S(1)}, bf16[4,8192]{1,0:T(4,128)(2,1)S(1)}, u32[]{:S(2)}, u32[]{:S(2)}) collective-permute-start(bf16[4,8192]{1,0:T(4,128)(2,1)S(1)} %pad_maximum_fusion.8), channel_id=1, source_target_pairs={{0,4},{4,0},{8,12},{12,8},{1,5},{5,1},{9,13},{13,9},{2,6},{6,2},{1... | collective-permute-start | bytes 196616 | tf_op jit(solution)/shard_map/ppermute | solution.py:25
  96.0 7.5 %collective-permute-start.33 = (bf16[4,8192]{1,0:T(4,128)(2,1)S(1)}, bf16[4,8192]{1,0:T(4,128)(2,1)S(1)}, u32[]{:S(2)}, u32[]{:S(2)}) collective-permute-start(bf16[4,8192]{1,0:T(4,128)(2,1)S(1)} %pad_maximum_fusion.9), channel_id=1, source_target_pairs={{0,8},{4,12},{8,0},{12,4},{1,9},{5,13},{9,1},{13,5},{2,10},{6,14},... | collective-permute-start | bytes 196616 | tf_op jit(solution)/shard_map/ppermute | solution.py:25
  98.4 6.2 %collective-permute-start.34 = (bf16[4,8192]{1,0:T(4,128)(2,1)S(1)}, bf16[4,8192]{1,0:T(4,128)(2,1)S(1)}, u32[]{:S(2)}, u32[]{:S(2)}) collective-permute-start(bf16[4,8192]{1,0:T(4,128)(2,1)S(1)} %pad_maximum_fusion.10), channel_id=1, source_target_pairs={{0,12},{4,8},{8,4},{12,0},{1,13},{5,9},{9,5},{13,1},{2,14},{6,10},... | collective-permute-start | bytes 196616 | tf_op jit(solution)/shard_map/ppermute | solution.py:25

commit v3 on v2

--- a/solution.py
+++ b/solution.py
@@ -180,10 +180,8 @@
 
 
 def up_tile(units, depth):
-    step = units
-    while step % 256 == 0 and step * depth > MIB * 3 // 2:
-        step //= 2
-    return step
+    widths = [n for n in range(256, units + 1, 256) if units % n == 0 and n * depth <= MIB * 3 // 2]
+    return max(widths, default=128)
 
 
 def up_sums(scaled, up_refs, at_cols):
@@ -376,24 +374,17 @@
         leave_ref[:, to_cols] = answers[count:].astype(BF16)
 
 
-def final_kernel(parts, picks_ref, *refs):
+def final_kernel(picks_ref, *refs):
     pieces, out_ref = refs[:-1], refs[-1]
-    picks = picks_ref[...].astype(F32)
-    per_part = len(pieces) // parts
-    first = 0
-    for part in range(parts):
-        size = pieces[part * per_part].shape[1]
-        tile = 1024 if size % 1024 == 0 else size
-        for start in range(0, size, tile):
-            total, row_at = None, 0
-            for piece in pieces[part * per_part : (part + 1) * per_part]:
-                rows = piece[:, start : start + tile].astype(F32)
-                for row in range(rows.shape[0]):
-                    term = picks[:, row_at : row_at + 1] * rows[row : row + 1]
-                    total = term if total is None else total + term
-                    row_at += 1
-            out_ref[:, first + start : first + start + tile] = total.astype(BF16)
-        first += size
+    picks = picks_ref[...]
+    size = out_ref.shape[1]
+    tile = 1024 if size % 1024 == 0 else size
+    for start in range(0, size, tile):
+        rows = jnp.concatenate(
+            [piece[:, start : start + tile].astype(F32) for piece in pieces], axis=0
+        )
+        total = jnp.dot(picks, rows.astype(BF16), preferred_element_type=F32)
+        out_ref[:, start : start + tile] = total.astype(BF16)
 
 
 def per_device(
@@ -591,7 +582,7 @@
         piece = jnp.concatenate([stay[own], back[own]])
         pieces.append(swap(piece, "exp", q) if q else piece)
     return pl.pallas_call(
-        functools.partial(final_kernel, 1),
+        final_kernel,
         out_shape=jax.ShapeDtypeStruct((tok_rows, width), BF16),
         in_specs=[VMEM] * (1 + len(pieces)),
         out_specs=VMEM,

time: 106 us -> 106 us (level)
  no operation moved by 1% of the time
where the time goes in v3:
time: 106 us
  Pallas kernels  47.8 us (45%)
  starting transfers between devices  37.6 us (35%)
  waiting for transfers between devices  14.9 us (14%)
  other arithmetic  3.53 us (3%)
  local copies, waits for them, and re-layouts  1.32 us (1%)
    ppermute x35, starting transfers between devices, swap(): return lax.ppermute(value, axis, [(i, i ^ distance) for i in range(size)])  37.6 us
    pallas_call x1, Pallas kernels, per_device(): pl.pallas_call(functools.partial(second_kernel, sizes), out_shape=[jax.Sh...  17.3 us
    ppermute x35, waiting for transfers between devices, swap(): return lax.ppermute(value, axis, [(i, i ^ distance) for i in range(size)])  14.9 us
    pallas_call x2, Pallas kernels, fetch_up(): pl.pallas_call(functools.partial(fetch_kernel, places, exp_count, cols),...  8.67 us
    pallas_call x1, Pallas kernels, per_device(): pl.pallas_call(functools.partial(first_kernel, (tp_count, exp_count, spli...  8.1 us
    pallas_call x1, Pallas kernels, per_device(): pl.pallas_call(functools.partial(third_kernel, tp_count, early), out_shap...  5.44 us
    pallas_call x1, Pallas kernels, fetch_weight(): pl.pallas_call(weight_kernel, out_shape=[pltpu.VMEM(matrix.shape, matrix....  2.21 us
  transfers between devices with their start and end apart: 35, of which 12 were waited for; matrix products, arithmetic and copies ran while one was open for 4% of the time, Pallas kernels for 27%

profile of v3, /device:TPU:0, one launch (start us, length us, event | category | flops | bytes accessed | tf_op | source)
XLA Modules:
  0.0 105.5 jit_solution(11031201268331893876)
XLA Ops:
  0.0 3.0 %collective-permute-start.5 = (bf16[32,2048]{1,0:T(8,128)(2,1)}, bf16[32,2048]{1,0:T(8,128)(2,1)S(1)}, u32[]{:S(2)}, u32[]{:S(2)}) collective-permute-start(bf16[32,2048]{1,0:T(8,128)(2,1)} %param.10), channel_id=1, source_target_pairs={{0,4},{4,0},{8,12},{12,8},{1,5},{5,1},{9,13},{13,9},{2,6},{6,2},{1... | collective-permute-start | bytes 393224 | tf_op jit(solution)/shard_map/ppermute | solution.py:25
  3.0 2.5 %collective-permute-start.9 = (bf16[32,2048]{1,0:T(8,128)(2,1)}, bf16[32,2048]{1,0:T(8,128)(2,1)S(1)}, u32[]{:S(2)}, u32[]{:S(2)}) collective-permute-start(bf16[32,2048]{1,0:T(8,128)(2,1)} %param.10), channel_id=1, source_target_pairs={{0,12},{4,8},{8,4},{12,0},{1,13},{5,9},{9,5},{13,1},{2,14},{6,10},... | collective-permute-start | bytes 393224 | tf_op jit(solution)/shard_map/ppermute | solution.py:25
  5.5 0.1 collective-permute-start.7
  5.6 0.7 multiply_add_fusion.1
  6.4 0.2 select_reduce_fusion
  6.7 0.9 copy-done.1
  7.7 0.6 piece.1
  8.2 0.3 collective-permute-start
  8.7 0.1 add.93
  8.8 0.7 broadcast_in_dim.9
  9.6 2.2 %fetch_weight.1 = (bf16[2048,1024]{1,0:T(8,128)(2,1)S(1)}, bf16[8,2048]{1,0:T(8,128)(2,1)S(1)}) custom-call(bf16[2048,1024]{1,0:T(8,128)(2,1)} %source_ref.1, s32[3]{0:T(128)S(1)} %pad_add_fusion.place_ref.refs_0_, bf16[4,8,1152]{2,1,0:T(8,128)(2,1)S(1)} %get-tuple-element.36.refs_1_, f32[1,8192]{1,0:T(1,128)S(1)} %bitcast.20, ...), custom_call_target="tpu_custom_call" | custom-call | bytes 4194304 | tf_op jit(solution)/shard_map/fetch_weight/pallas_call | solution.py:99
  11.8 0.9 bitcast_add_fusion.refs_0_
  12.8 1.7 %collective-permute-start.1 = (bf16[2,8,1152]{2,1,0:T(8,128)(2,1)S(1)}, bf16[2,8,1152]{2,1,0:T(8,128)(2,1)S(1)}, u32[]{:S(2)}, u32[]{:S(2)}) collective-permute-start(bf16[2,8,1152]{2,1,0:T(8,128)(2,1)S(1)} %pad_maximum_fusion.11), channel_id=1, source_target_pairs={{0,4},{4,0},{8,12},{12,8},{1,5},{5,1},{9,13},{13,9},{2,6},{6,2},{1... | collective-permute-start | bytes 110600 | tf_op jit(solution)/shard_map/ppermute | solution.py:25
  14.5 0.3 collective-permute-start.6
  14.8 1.8 %collective-permute-start.2 = (bf16[2,8,1152]{2,1,0:T(8,128)(2,1)S(1)}, bf16[2,8,1152]{2,1,0:T(8,128)(2,1)S(1)}, u32[]{:S(2)}, u32[]{:S(2)}) collective-permute-start(bf16[2,8,1152]{2,1,0:T(8,128)(2,1)S(1)} %pad_maximum_fusion.12), channel_id=1, source_target_pairs={{0,8},{4,12},{8,0},{12,4},{1,9},{5,13},{9,1},{13,5},{2,10},{6,14},... | collective-permute-start | bytes 110600 | tf_op jit(solution)/shard_map/ppermute | solution.py:25
  16.5 1.0 collective-permute-start.3
  17.5 1.0 collective-permute-done.7.refs_4_
  18.5 0.5 collective-permute-start.8
  19.1 0.8 collective-permute-done.10.refs_7_
  19.9 0.2 collective-permute-done.8.refs_5_
  20.1 1.8 %project.1 = (bf16[64,1024]{1,0:T(8,128)(2,1)S(1)}, bf16[64,1024]{1,0:T(8,128)(2,1)S(1)}, bf16[64,1024]{1,0:T(8,128)(2,1)S(1)}, bf16[64,1024]{1,0:T(8,128)(2,1)S(1)}) custom-call(s32[3]{0:T(128)S(1)} %pad_add_fusion.place_ref.refs_0_, bf16[32,2048]{1,0:T(8,128)(2,1)S(1)} %bitcast_add_fusion.refs_0_, bf16[32,2048]{1,0:T(8,128)(2,1)S(1)} %collective-permute-done.4.refs_1_, ...), custom_call_target="tpu_custom_call" | custom-call | tf_op jit(solution)/shard_map/project/pallas_call | solution.py:447
  21.9 1.6 %collective-permute-start.11 = (bf16[64,1024]{1,0:T(8,128)(2,1)S(1)}, bf16[64,1024]{1,0:T(8,128)(2,1)S(1)}, u32[]{:S(2)}, u32[]{:S(2)}) collective-permute-start(bf16[64,1024]{1,0:T(8,128)(2,1)S(1)} %get-tuple-element.40), channel_id=1, source_target_pairs={{0,1},{1,0},{2,3},{3,2},{4,5},{5,4},{6,7},{7,6},{8,9},{9,8},{10,11... | collective-permute-start | bytes 393224 | tf_op jit(solution)/shard_map/ppermute | solution.py:25
  23.4 1.5 %collective-permute-start.12 = (bf16[64,1024]{1,0:T(8,128)(2,1)S(1)}, bf16[64,1024]{1,0:T(8,128)(2,1)S(1)}, u32[]{:S(2)}, u32[]{:S(2)}) collective-permute-start(bf16[64,1024]{1,0:T(8,128)(2,1)S(1)} %get-tuple-element.41), channel_id=1, source_target_pairs={{0,2},{1,3},{2,0},{3,1},{4,6},{5,7},{6,4},{7,5},{8,10},{9,11},{10,... | collective-permute-start | bytes 393224 | tf_op jit(solution)/shard_map/ppermute | solution.py:25
  25.0 0.5 collective-permute-start.13
  25.5 0.1 convert_reduce_fusion
  25.6 5.3 %fetch_up.2.refs_4_ = bf16[2048,3072]{1,0:T(8,128)(2,1)S(1)} custom-call(s32[3]{0:T(128)S(1)} %pad_add_fusion.place_ref.refs_0_, bf16[8192,3072]{1,0:T(8,128)(2,1)} %bitcast.26, bf16[64,1024]{1,0:T(8,128)(2,1)S(1)} %get-tuple-element.39.refs_0_, f32[1,8192]{1,0:T(1,128)S(1)} %bitcast.21, bf16[8,16]{1,0:T(8,128)(2,1)S(1)} %compare_convert_fusion.refs_3_.refs_2_.picks_ref), custom_call_target="tpu_custom_call" | custom-call | bytes 12582912 | tf_op jit(solution)/shard_map/fetch_up/pallas_call | solution.py:57
  30.9 0.8 collective-permute-done.12.refs_2_
  31.7 0.8 slot.2
  32.6 1.2 %collective-permute-done.14 = bf16[2,16,1024]{2,1,0:T(8,128)(2,1)S(1)} collective-permute-done((bf16[2,16,1024]{2,1,0:T(8,128)(2,1)S(1)}, bf16[2,16,1024]{2,1,0:T(8,128)(2,1)S(1)}, u32[]{:S(2)}, u32[]{:S(2)}) %collective-permute-start.14) | collective-permute-done | bytes 65568 | tf_op jit(solution)/shard_map/ppermute | solution.py:25
  33.9 0.8 slot.3
  34.8 0.2 collective-permute-start.16
  35.0 1.1 %collective-permute-done.16 = bf16[2,16,1024]{2,1,0:T(8,128)(2,1)S(1)} collective-permute-done((bf16[2,16,1024]{2,1,0:T(8,128)(2,1)S(1)}, bf16[2,16,1024]{2,1,0:T(8,128)(2,1)S(1)}, u32[]{:S(2)}, u32[]{:S(2)}) %collective-permute-start.16) | collective-permute-done | bytes 65568 | tf_op jit(solution)/shard_map/ppermute | solution.py:25
  36.1 2.7 %collective-permute-start.18 = (bf16[2,16,1024]{2,1,0:T(8,128)(2,1)S(1)}, bf16[2,16,1024]{2,1,0:T(8,128)(2,1)S(1)}, u32[]{:S(2)}, u32[]{:S(2)}) collective-permute-start(bf16[2,16,1024]{2,1,0:T(8,128)(2,1)S(1)} %pad_maximum_fusion.6), channel_id=1, source_target_pairs={{0,12},{4,8},{8,4},{12,0},{1,13},{5,9},{9,5},{13,1},{2,14},{6,10},... | collective-permute-start | bytes 196616 | tf_op jit(solution)/shard_map/ppermute | solution.py:25
  38.8 0.9 collective-permute-start.17
  39.7 1.7 %collective-permute-start.21 = (bf16[2,2,16,1024]{3,2,1,0:T(8,128)(2,1)S(1)}, bf16[2,2,16,1024]{3,2,1,0:T(8,128)(2,1)S(1)}, u32[]{:S(2)}, u32[]{:S(2)}) collective-permute-start(bf16[2,2,16,1024]{3,2,1,0:T(8,128)(2,1)S(1)} %pad_maximum_fusion.2.refs_0_), channel_id=1, source_target_pairs={{0,3},{1,2},{2,1},{3,0},{4,7},{5,6},{6,5},{7,4},{8,11},{9,10},{10,... | collective-permute-start | bytes 393224 | tf_op jit(solution)/shard_map/ppermute | solution.py:25
  41.5 1.0 collective-permute-start.20
  42.5 0.8 collective-permute-start.19
  43.3 3.4 %fetch_up.3.up_ref = bf16[1024,3072]{1,0:T(8,128)(2,1)S(1)} custom-call(s32[3]{0:T(128)S(1)} %pad_add_fusion.place_ref.refs_0_, bf16[8192,3072]{1,0:T(8,128)(2,1)} %bitcast.27, bf16[2,2,16,1024]{3,2,1,0:T(8,128)(2,1)S(1)} %pad_maximum_fusion.2.refs_0_), custom_call_target="tpu_custom_call" | custom-call | bytes 6291456 | tf_op jit(solution)/shard_map/fetch_up/pallas_call | solution.py:57
  46.8 1.7 %collective-permute-start.24 = (bf16[2,2,16,1024]{3,2,1,0:T(8,128)(2,1)S(1)}, bf16[2,2,16,1024]{3,2,1,0:T(8,128)(2,1)S(1)}, u32[]{:S(2)}, u32[]{:S(2)}) collective-permute-start(bf16[2,2,16,1024]{3,2,1,0:T(8,128)(2,1)S(1)} %pad_maximum_fusion.3.refs_0_), channel_id=1, source_target_pairs={{0,3},{1,2},{2,1},{3,0},{4,7},{5,6},{6,5},{7,4},{8,11},{9,10},{10,... | collective-permute-start | bytes 393224 | tf_op jit(solution)/shard_map/ppermute | solution.py:25
  48.5 1.0 collective-permute-start.23
  49.5 0.8 collective-permute-start.22
  50.3 8.1 %first.1 = (f32[64,3072]{1,0:T(8,128)S(1)}, f32[64,128]{1,0:T(8,128)S(1)}, f32[16,128]{1,0:T(8,128)S(1)}) custom-call(s32[3]{0:T(128)S(1)} %pad_add_fusion.place_ref.refs_0_, f32[1,8192]{1,0:T(1,128)S(1)} %bitcast.22, bf16[2,4,8192]{2,1,0:T(4,128)(2,1)S(1)} %copy-done, bf16[1024,3072]{1,0:T(8,128)(2,1)S(1)} %fetch_up.3.up_ref, ...), custom_call_target="tpu_custom_call" | custom-call | flops 1610612736 | bytes 25165824 | tf_op jit(solution)/shard_map/first/pallas_call | solution.py:493
  58.5 17.3 %second.1 = (bf16[16,5120]{1,0:T(8,128)(2,1)S(1)}, bf16[16,5120]{1,0:T(8,128)(2,1)S(1)}, bf16[16,5120]{1,0:T(8,128)(2,1)S(1)}, bf16[16,5120]{1,0:T(8,128)(2,1)S(...) custom-call(s32[3]{0:T(128)S(1)} %pad_add_fusion.place_ref.refs_0_, ...), custom_call_target="tpu_custom_call" | custom-call | flops 3221225472 | bytes 50331648 | tf_op jit(solution)/shard_map/second/pallas_call | solution.py:517
  75.7 1.3 %collective-permute-start.25 = (bf16[16,5120]{1,0:T(8,128)(2,1)S(1)}, bf16[16,5120]{1,0:T(8,128)(2,1)S(1)}, u32[]{:S(2)}, u32[]{:S(2)}) collective-permute-start(bf16[16,5120]{1,0:T(8,128)(2,1)S(1)} %get-tuple-element.55), channel_id=1, source_target_pairs={{0,1},{1,0},{2,3},{3,2},{4,5},{5,4},{6,7},{7,6},{8,9},{9,8},{10,11... | collective-permute-start | bytes 491528 | tf_op jit(solution)/shard_map/ppermute | solution.py:25
  77.0 1.0 collective-permute-start.27
  78.0 1.3 %collective-permute-start.29 = (bf16[16,5120]{1,0:T(8,128)(2,1)S(1)}, bf16[16,5120]{1,0:T(8,128)(2,1)S(1)}, u32[]{:S(2)}, u32[]{:S(2)}) collective-permute-start(bf16[16,5120]{1,0:T(8,128)(2,1)S(1)} %get-tuple-element.59), channel_id=1, source_target_pairs={{0,3},{1,2},{2,1},{3,0},{4,7},{5,6},{6,5},{7,4},{8,11},{9,10},{10,... | collective-permute-start | bytes 491528 | tf_op jit(solution)/shard_map/ppermute | solution.py:25
  79.3 5.4 %third.1 = (bf16[16,3072]{1,0:T(8,128)(2,1)S(1)}, bf16[16,3072]{1,0:T(8,128)(2,1)S(1)}, bf16[16,3072]{1,0:T(8,128)(2,1)S(1)}, bf16[16,3072]{1,0:T(8,128)(2,1)S(1)}) custom-call(bf16[64,3072]{1,0:T(8,128)(2,1)S(1)} %get-tuple-element.51.hidden, bf16[3072,1024]{1,0:T(8,128)(2,1)S(1)} %get-tuple-element.52.held_ref, bf16[3072,8192]{1,0:T(8,128)(2,1)} %bitcast.31), custom_call_target="tpu_custom_call" | custom-call | flops 1610612736 | bytes 25165824 | tf_op jit(solution)/shard_map/third/pallas_call | solution.py:542
  84.8 1.3 %collective-permute-start.26 = (bf16[16,3072]{1,0:T(8,128)(2,1)S(1)}, bf16[16,3072]{1,0:T(8,128)(2,1)S(1)}, u32[]{:S(2)}, u32[]{:S(2)}) collective-permute-start(bf16[16,3072]{1,0:T(8,128)(2,1)S(1)} %fusion.2), channel_id=1, source_target_pairs={{0,1},{1,0},{2,3},{3,2},{4,5},{5,4},{6,7},{7,6},{8,9},{9,8},{10,11... | collective-permute-start | bytes 294920 | tf_op jit(solution)/shard_map/ppermute | solution.py:25
  86.1 1.0 collective-permute-start.28
  87.1 1.3 %collective-permute-start.30 = (bf16[16,3072]{1,0:T(8,128)(2,1)S(1)}, bf16[16,3072]{1,0:T(8,128)(2,1)S(1)}, u32[]{:S(2)}, u32[]{:S(2)}) collective-permute-start(bf16[16,3072]{1,0:T(8,128)(2,1)S(1)} %fusion), channel_id=1, source_target_pairs={{0,3},{1,2},{2,1},{3,0},{4,7},{5,6},{6,5},{7,4},{8,11},{9,10},{10,... | collective-permute-start | bytes 294920 | tf_op jit(solution)/shard_map/ppermute | solution.py:25
  88.5 0.7 combine.2
  89.2 0.2 collective-permute-done.26.refs_1_
  89.5 1.3 %collective-permute-done.28.refs_2_ = bf16[16,3072]{1,0:T(8,128)(2,1)S(1)} collective-permute-done((bf16[16,3072]{1,0:T(8,128)(2,1)S(1)}, bf16[16,3072]{1,0:T(8,128)(2,1)S(1)}, u32[]{:S(2)}, u32[]{:S(2)}) %collective-permute-start.28) | collective-permute-done | bytes 98336 | tf_op jit(solution)/shard_map/ppermute | solution.py:25
  90.8 2.0 %collective-permute-done.30.refs_3_ = bf16[16,3072]{1,0:T(8,128)(2,1)S(1)} collective-permute-done((bf16[16,3072]{1,0:T(8,128)(2,1)S(1)}, bf16[16,3072]{1,0:T(8,128)(2,1)S(1)}, u32[]{:S(2)}, u32[]{:S(2)}) %collective-permute-start.30) | collective-permute-done | bytes 98336 | tf_op jit(solution)/shard_map/ppermute | solution.py:25
  92.7 0.6 combine.3
  93.4 0.1 fusion.4
  93.5 1.2 %collective-permute-done.31 = bf16[8,8192]{1,0:T(8,128)(2,1)S(1)} collective-permute-done((bf16[8,8192]{1,0:T(8,128)(2,1)S(1)}, bf16[8,8192]{1,0:T(8,128)(2,1)S(1)}, u32[]{:S(2)}, u32[]{:S(2)}) %collective-permute-start.31) | collective-permute-done | bytes 131104 | tf_op jit(solution)/shard_map/ppermute | solution.py:25
  94.8 0.1 fusion.5
  95.0 1.0 collective-permute-start.32
  96.0 2.3 %collective-permute-start.33 = (bf16[4,8192]{1,0:T(4,128)(2,1)S(1)}, bf16[4,8192]{1,0:T(4,128)(2,1)S(1)}, u32[]{:S(2)}, u32[]{:S(2)}) collective-permute-start(bf16[4,8192]{1,0:T(4,128)(2,1)S(1)} %pad_maximum_fusion.9), channel_id=1, source_target_pairs={{0,8},{4,12},{8,0},{12,4},{1,9},{5,13},{9,1},{13,5},{2,10},{6,14},... | collective-permute-start | bytes 196616 | tf_op jit(solution)/shard_map/ppermute | solution.py:25
  98.4 1.3 %collective-permute-start.34 = (bf16[4,8192]{1,0:T(4,128)(2,1)S(1)}, bf16[4,8192]{1,0:T(4,128)(2,1)S(1)}, u32[]{:S(2)}, u32[]{:S(2)}) collective-permute-start(bf16[4,8192]{1,0:T(4,128)(2,1)S(1)} %pad_maximum_fusion.10), channel_id=1, source_target_pairs={{0,12},{4,8},{8,4},{12,0},{1,13},{5,9},{9,5},{13,1},{2,14},{6,10},... | collective-permute-start | bytes 196616 | tf_op jit(solution)/shard_map/ppermute | solution.py:25
  99.8 3.7 %collective-permute-done.33.refs_2_ = bf16[4,8192]{1,0:T(4,128)(2,1)S(1)} collective-permute-done((bf16[4,8192]{1,0:T(4,128)(2,1)S(1)}, bf16[4,8192]{1,0:T(4,128)(2,1)S(1)}, u32[]{:S(2)}, u32[]{:S(2)}) %collective-permute-start.33) | collective-permute-done | bytes 65568 | tf_op jit(solution)/shard_map/ppermute | solution.py:25
  103.5 1.2 %collective-permute-done.34.refs_3_ = bf16[4,8192]{1,0:T(4,128)(2,1)S(1)} collective-permute-done((bf16[4,8192]{1,0:T(4,128)(2,1)S(1)}, bf16[4,8192]{1,0:T(4,128)(2,1)S(1)}, u32[]{:S(2)}, u32[]{:S(2)}) %collective-permute-start.34) | collective-permute-done | bytes 65568 | tf_op jit(solution)/shard_map/ppermute | solution.py:25
  104.7 0.9 final.1
  (69 shorter events, 1.3 us)
Async XLA Ops:
  0.0 14.5 %collective-permute-start.5 = (bf16[32,2048]{1,0:T(8,128)(2,1)}, bf16[32,2048]{1,0:T(8,128)(2,1)S(1)}, u32[]{:S(2)}, u32[]{:S(2)}) collective-permute-start(bf16[32,2048]{1,0:T(8,128)(2,1)} %param.10), channel_id=1, source_target_pairs={{0,4},{4,0},{8,12},{12,8},{1,5},{5,1},{9,13},{13,9},{2,6},{6,2},{1... | collective-permute-start | bytes 393224 | tf_op jit(solution)/shard_map/ppermute | solution.py:25
  3.0 11.7 %collective-permute-start.4 = (bf16[32,2048]{1,0:T(8,128)(2,1)}, bf16[32,2048]{1,0:T(8,128)(2,1)S(1)}, u32[]{:S(2)}, u32[]{:S(2)}) collective-permute-start(bf16[32,2048]{1,0:T(8,128)(2,1)} %param.10), channel_id=1, source_target_pairs={{0,16},{16,0},{1,17},{17,1},{2,18},{18,2},{3,19},{19,3},{4,20},{20... | collective-permute-start | bytes 393224 | tf_op jit(solution)/shard_map/ppermute | solution.py:25
  3.0 13.5 %collective-permute-start.9 = (bf16[32,2048]{1,0:T(8,128)(2,1)}, bf16[32,2048]{1,0:T(8,128)(2,1)S(1)}, u32[]{:S(2)}, u32[]{:S(2)}) collective-permute-start(bf16[32,2048]{1,0:T(8,128)(2,1)} %param.10), channel_id=1, source_target_pairs={{0,12},{4,8},{8,4},{12,0},{1,13},{5,9},{9,5},{13,1},{2,14},{6,10},... | collective-permute-start | bytes 393224 | tf_op jit(solution)/shard_map/ppermute | solution.py:25
  5.5 13.0 %collective-permute-start.7 = (bf16[32,2048]{1,0:T(8,128)(2,1)}, bf16[32,2048]{1,0:T(8,128)(2,1)S(1)}, u32[]{:S(2)}, u32[]{:S(2)}) collective-permute-start(bf16[32,2048]{1,0:T(8,128)(2,1)} %param.10), channel_id=1, source_target_pairs={{0,8},{4,12},{8,0},{12,4},{1,9},{5,13},{9,1},{13,5},{2,10},{6,14},... | collective-permute-start | bytes 393224 | tf_op jit(solution)/shard_map/ppermute | solution.py:25
  6.7 0.9 copy-start.1
  8.2 4.5 %collective-permute-start = (bf16[4,8,1152]{2,1,0:T(8,128)(2,1)S(1)}, bf16[4,8,1152]{2,1,0:T(8,128)(2,1)S(1)}, u32[]{:S(2)}, u32[]{:S(2)}) collective-permute-start(bf16[4,8,1152]{2,1,0:T(8,128)(2,1)S(1)} %get-tuple-element.36.refs_1_), channel_id=1, source_target_pairs={{0,16},{16,0},{1,17},{17,1},{2,18},{18,2},{3,19},{19,3},{4,20},{20... | collective-permute-start | bytes 221192 | tf_op jit(solution)/shard_map/ppermute | solution.py:25
  12.8 12.2 %collective-permute-start.1 = (bf16[2,8,1152]{2,1,0:T(8,128)(2,1)S(1)}, bf16[2,8,1152]{2,1,0:T(8,128)(2,1)S(1)}, u32[]{:S(2)}, u32[]{:S(2)}) collective-permute-start(bf16[2,8,1152]{2,1,0:T(8,128)(2,1)S(1)} %pad_maximum_fusion.11), channel_id=1, source_target_pairs={{0,4},{4,0},{8,12},{12,8},{1,5},{5,1},{9,13},{13,9},{2,6},{6,2},{1... | collective-permute-start | bytes 110600 | tf_op jit(solution)/shard_map/ppermute | solution.py:25
  14.5 4.1 %collective-permute-start.6 = (bf16[32,2048]{1,0:T(8,128)(2,1)S(1)}, bf16[32,2048]{1,0:T(8,128)(2,1)S(1)}, u32[]{:S(2)}, u32[]{:S(2)}) collective-permute-start(bf16[32,2048]{1,0:T(8,128)(2,1)S(1)} %collective-permute-done.5.refs_2_), channel_id=1, source_target_pairs={{0,16},{16,0},{1,17},{17,1},{2,18},{18,2},{3,19},{19,3},{4,20},{20... | collective-permute-start | bytes 393224 | tf_op jit(solution)/shard_map/ppermute | solution.py:25
  14.8 10.7 %collective-permute-start.2 = (bf16[2,8,1152]{2,1,0:T(8,128)(2,1)S(1)}, bf16[2,8,1152]{2,1,0:T(8,128)(2,1)S(1)}, u32[]{:S(2)}, u32[]{:S(2)}) collective-permute-start(bf16[2,8,1152]{2,1,0:T(8,128)(2,1)S(1)} %pad_maximum_fusion.12), channel_id=1, source_target_pairs={{0,8},{4,12},{8,0},{12,4},{1,9},{5,13},{9,1},{13,5},{2,10},{6,14},... | collective-permute-start | bytes 110600 | tf_op jit(solution)/shard_map/ppermute | solution.py:25
  16.5 8.9 %collective-permute-start.3 = (bf16[2,8,1152]{2,1,0:T(8,128)(2,1)S(1)}, bf16[2,8,1152]{2,1,0:T(8,128)(2,1)S(1)}, u32[]{:S(2)}, u32[]{:S(2)}) collective-permute-start(bf16[2,8,1152]{2,1,0:T(8,128)(2,1)S(1)} %pad_maximum_fusion.13), channel_id=1, source_target_pairs={{0,12},{4,8},{8,4},{12,0},{1,13},{5,9},{9,5},{13,1},{2,14},{6,10},... | collective-permute-start | bytes 110600 | tf_op jit(solution)/shard_map/ppermute | solution.py:25
  18.5 1.3 %collective-permute-start.10 = (bf16[32,2048]{1,0:T(8,128)(2,1)S(1)}, bf16[32,2048]{1,0:T(8,128)(2,1)S(1)}, u32[]{:S(2)}, u32[]{:S(2)}) collective-permute-start(bf16[32,2048]{1,0:T(8,128)(2,1)S(1)} %collective-permute-done.9.refs_6_), channel_id=1, source_target_pairs={{0,16},{16,0},{1,17},{17,1},{2,18},{18,2},{3,19},{19,3},{4,20},{20... | collective-permute-start | bytes 393224 | tf_op jit(solution)/shard_map/ppermute | solution.py:25
  18.5 1.5 %collective-permute-start.8 = (bf16[32,2048]{1,0:T(8,128)(2,1)S(1)}, bf16[32,2048]{1,0:T(8,128)(2,1)S(1)}, u32[]{:S(2)}, u32[]{:S(2)}) collective-permute-start(bf16[32,2048]{1,0:T(8,128)(2,1)S(1)} %collective-permute-done.7.refs_4_), channel_id=1, source_target_pairs={{0,16},{16,0},{1,17},{17,1},{2,18},{18,2},{3,19},{19,3},{4,20},{20... | collective-permute-start | bytes 393224 | tf_op jit(solution)/shard_map/ppermute | solution.py:25
  21.9 9.0 %collective-permute-start.11 = (bf16[64,1024]{1,0:T(8,128)(2,1)S(1)}, bf16[64,1024]{1,0:T(8,128)(2,1)S(1)}, u32[]{:S(2)}, u32[]{:S(2)}) collective-permute-start(bf16[64,1024]{1,0:T(8,128)(2,1)S(1)} %get-tuple-element.40), channel_id=1, source_target_pairs={{0,1},{1,0},{2,3},{3,2},{4,5},{5,4},{6,7},{7,6},{8,9},{9,8},{10,11... | collective-permute-start | bytes 393224 | tf_op jit(solution)/shard_map/ppermute | solution.py:25
  23.4 8.3 %collective-permute-start.12 = (bf16[64,1024]{1,0:T(8,128)(2,1)S(1)}, bf16[64,1024]{1,0:T(8,128)(2,1)S(1)}, u32[]{:S(2)}, u32[]{:S(2)}) collective-permute-start(bf16[64,1024]{1,0:T(8,128)(2,1)S(1)} %get-tuple-element.41), channel_id=1, source_target_pairs={{0,2},{1,3},{2,0},{3,1},{4,6},{5,7},{6,4},{7,5},{8,10},{9,11},{10,... | collective-permute-start | bytes 393224 | tf_op jit(solution)/shard_map/ppermute | solution.py:25
  25.0 6.7 %collective-permute-start.13 = (bf16[64,1024]{1,0:T(8,128)(2,1)S(1)}, bf16[64,1024]{1,0:T(8,128)(2,1)S(1)}, u32[]{:S(2)}, u32[]{:S(2)}) collective-permute-start(bf16[64,1024]{1,0:T(8,128)(2,1)S(1)} %get-tuple-element.42), channel_id=1, source_target_pairs={{0,3},{1,2},{2,1},{3,0},{4,7},{5,6},{6,5},{7,4},{8,11},{9,10},{10,... | collective-permute-start | bytes 393224 | tf_op jit(solution)/shard_map/ppermute | solution.py:25
  32.5 1.3 %collective-permute-start.14 = (bf16[2,16,1024]{2,1,0:T(8,128)(2,1)S(1)}, bf16[2,16,1024]{2,1,0:T(8,128)(2,1)S(1)}, u32[]{:S(2)}, u32[]{:S(2)}) collective-permute-start(bf16[2,16,1024]{2,1,0:T(8,128)(2,1)S(1)} %get-tuple-element.44), channel_id=1, source_target_pairs={{0,16},{16,0},{1,17},{17,1},{2,18},{18,2},{3,19},{19,3},{4,20},{20... | collective-permute-start | bytes 196616 | tf_op jit(solution)/shard_map/ppermute | solution.py:25
  33.9 5.9 %collective-permute-start.15 = (bf16[2,16,1024]{2,1,0:T(8,128)(2,1)S(1)}, bf16[2,16,1024]{2,1,0:T(8,128)(2,1)S(1)}, u32[]{:S(2)}, u32[]{:S(2)}) collective-permute-start(bf16[2,16,1024]{2,1,0:T(8,128)(2,1)S(1)} %pad_maximum_fusion.4.refs_4_), channel_id=1, source_target_pairs={{0,4},{4,0},{8,12},{12,8},{1,5},{5,1},{9,13},{13,9},{2,6},{6,2},{1... | collective-permute-start | bytes 196616 | tf_op jit(solution)/shard_map/ppermute | solution.py:25
  34.8 1.3 %collective-permute-start.16 = (bf16[2,16,1024]{2,1,0:T(8,128)(2,1)S(1)}, bf16[2,16,1024]{2,1,0:T(8,128)(2,1)S(1)}, u32[]{:S(2)}, u32[]{:S(2)}) collective-permute-start(bf16[2,16,1024]{2,1,0:T(8,128)(2,1)S(1)} %get-tuple-element.46), channel_id=1, source_target_pairs={{0,16},{16,0},{1,17},{17,1},{2,18},{18,2},{3,19},{19,3},{4,20},{20... | collective-permute-start | bytes 196616 | tf_op jit(solution)/shard_map/ppermute | solution.py:25
  36.1 10.6 %collective-permute-start.18 = (bf16[2,16,1024]{2,1,0:T(8,128)(2,1)S(1)}, bf16[2,16,1024]{2,1,0:T(8,128)(2,1)S(1)}, u32[]{:S(2)}, u32[]{:S(2)}) collective-permute-start(bf16[2,16,1024]{2,1,0:T(8,128)(2,1)S(1)} %pad_maximum_fusion.6), channel_id=1, source_target_pairs={{0,12},{4,8},{8,4},{12,0},{1,13},{5,9},{9,5},{13,1},{2,14},{6,10},... | collective-permute-start | bytes 196616 | tf_op jit(solution)/shard_map/ppermute | solution.py:25
  38.8 7.9 %collective-permute-start.17 = (bf16[2,16,1024]{2,1,0:T(8,128)(2,1)S(1)}, bf16[2,16,1024]{2,1,0:T(8,128)(2,1)S(1)}, u32[]{:S(2)}, u32[]{:S(2)}) collective-permute-start(bf16[2,16,1024]{2,1,0:T(8,128)(2,1)S(1)} %pad_maximum_fusion.5), channel_id=1, source_target_pairs={{0,8},{4,12},{8,0},{12,4},{1,9},{5,13},{9,1},{13,5},{2,10},{6,14},... | collective-permute-start | bytes 196616 | tf_op jit(solution)/shard_map/ppermute | solution.py:25
  39.7 10.6 %copy-start = (bf16[2,4,8192]{2,1,0:T(4,128)(2,1)S(1)}, bf16[2,4,8192]{2,1,0:T(4,128)(2,1)}, u32[]{:S(2)}) copy-start(bf16[2,4,8192]{2,1,0:T(4,128)(2,1)} %router_ref.3) | copy-start | bytes 393220
  39.7 9.8 %collective-permute-start.21 = (bf16[2,2,16,1024]{3,2,1,0:T(8,128)(2,1)S(1)}, bf16[2,2,16,1024]{3,2,1,0:T(8,128)(2,1)S(1)}, u32[]{:S(2)}, u32[]{:S(2)}) collective-permute-start(bf16[2,2,16,1024]{3,2,1,0:T(8,128)(2,1)S(1)} %pad_maximum_fusion.2.refs_0_), channel_id=1, source_target_pairs={{0,3},{1,2},{2,1},{3,0},{4,7},{5,6},{6,5},{7,4},{8,11},{9,10},{10,... | collective-permute-start | bytes 393224 | tf_op jit(solution)/shard_map/ppermute | solution.py:25
  41.5 8.9 %collective-permute-start.20 = (bf16[2,2,16,1024]{3,2,1,0:T(8,128)(2,1)S(1)}, bf16[2,2,16,1024]{3,2,1,0:T(8,128)(2,1)S(1)}, u32[]{:S(2)}, u32[]{:S(2)}) collective-permute-start(bf16[2,2,16,1024]{3,2,1,0:T(8,128)(2,1)S(1)} %pad_maximum_fusion.2.refs_0_), channel_id=1, source_target_pairs={{0,2},{1,3},{2,0},{3,1},{4,6},{5,7},{6,4},{7,5},{8,10},{9,11},{10,... | collective-permute-start | bytes 393224 | tf_op jit(solution)/shard_map/ppermute | solution.py:25
  42.5 7.8 %collective-permute-start.19 = (bf16[2,2,16,1024]{3,2,1,0:T(8,128)(2,1)S(1)}, bf16[2,2,16,1024]{3,2,1,0:T(8,128)(2,1)S(1)}, u32[]{:S(2)}, u32[]{:S(2)}) collective-permute-start(bf16[2,2,16,1024]{3,2,1,0:T(8,128)(2,1)S(1)} %pad_maximum_fusion.2.refs_0_), channel_id=1, source_target_pairs={{0,1},{1,0},{2,3},{3,2},{4,5},{5,4},{6,7},{7,6},{8,9},{9,8},{10,11... | collective-permute-start | bytes 393224 | tf_op jit(solution)/shard_map/ppermute | solution.py:25
  46.8 11.7 %collective-permute-start.24 = (bf16[2,2,16,1024]{3,2,1,0:T(8,128)(2,1)S(1)}, bf16[2,2,16,1024]{3,2,1,0:T(8,128)(2,1)S(1)}, u32[]{:S(2)}, u32[]{:S(2)}) collective-permute-start(bf16[2,2,16,1024]{3,2,1,0:T(8,128)(2,1)S(1)} %pad_maximum_fusion.3.refs_0_), channel_id=1, source_target_pairs={{0,3},{1,2},{2,1},{3,0},{4,7},{5,6},{6,5},{7,4},{8,11},{9,10},{10,... | collective-permute-start | bytes 393224 | tf_op jit(solution)/shard_map/ppermute | solution.py:25
  48.5 10.0 %collective-permute-start.23 = (bf16[2,2,16,1024]{3,2,1,0:T(8,128)(2,1)S(1)}, bf16[2,2,16,1024]{3,2,1,0:T(8,128)(2,1)S(1)}, u32[]{:S(2)}, u32[]{:S(2)}) collective-permute-start(bf16[2,2,16,1024]{3,2,1,0:T(8,128)(2,1)S(1)} %pad_maximum_fusion.3.refs_0_), channel_id=1, source_target_pairs={{0,2},{1,3},{2,0},{3,1},{4,6},{5,7},{6,4},{7,5},{8,10},{9,11},{10,... | collective-permute-start | bytes 393224 | tf_op jit(solution)/shard_map/ppermute | solution.py:25
  49.5 8.9 %collective-permute-start.22 = (bf16[2,2,16,1024]{3,2,1,0:T(8,128)(2,1)S(1)}, bf16[2,2,16,1024]{3,2,1,0:T(8,128)(2,1)S(1)}, u32[]{:S(2)}, u32[]{:S(2)}) collective-permute-start(bf16[2,2,16,1024]{3,2,1,0:T(8,128)(2,1)S(1)} %pad_maximum_fusion.3.refs_0_), channel_id=1, source_target_pairs={{0,1},{1,0},{2,3},{3,2},{4,5},{5,4},{6,7},{7,6},{8,9},{9,8},{10,11... | collective-permute-start | bytes 393224 | tf_op jit(solution)/shard_map/ppermute | solution.py:25
  75.7 9.0 %collective-permute-start.25 = (bf16[16,5120]{1,0:T(8,128)(2,1)S(1)}, bf16[16,5120]{1,0:T(8,128)(2,1)S(1)}, u32[]{:S(2)}, u32[]{:S(2)}) collective-permute-start(bf16[16,5120]{1,0:T(8,128)(2,1)S(1)} %get-tuple-element.55), channel_id=1, source_target_pairs={{0,1},{1,0},{2,3},{3,2},{4,5},{5,4},{6,7},{7,6},{8,9},{9,8},{10,11... | collective-permute-start | bytes 491528 | tf_op jit(solution)/shard_map/ppermute | solution.py:25
  77.0 9.0 %collective-permute-start.27 = (bf16[16,5120]{1,0:T(8,128)(2,1)S(1)}, bf16[16,5120]{1,0:T(8,128)(2,1)S(1)}, u32[]{:S(2)}, u32[]{:S(2)}) collective-permute-start(bf16[16,5120]{1,0:T(8,128)(2,1)S(1)} %get-tuple-element.57), channel_id=1, source_target_pairs={{0,2},{1,3},{2,0},{3,1},{4,6},{5,7},{6,4},{7,5},{8,10},{9,11},{10,... | collective-permute-start | bytes 491528 | tf_op jit(solution)/shard_map/ppermute | solution.py:25
  78.0 9.1 %collective-permute-start.29 = (bf16[16,5120]{1,0:T(8,128)(2,1)S(1)}, bf16[16,5120]{1,0:T(8,128)(2,1)S(1)}, u32[]{:S(2)}, u32[]{:S(2)}) collective-permute-start(bf16[16,5120]{1,0:T(8,128)(2,1)S(1)} %get-tuple-element.59), channel_id=1, source_target_pairs={{0,3},{1,2},{2,1},{3,0},{4,7},{5,6},{6,5},{7,4},{8,11},{9,10},{10,... | collective-permute-start | bytes 491528 | tf_op jit(solution)/shard_map/ppermute | solution.py:25
  84.8 4.7 %collective-permute-start.26 = (bf16[16,3072]{1,0:T(8,128)(2,1)S(1)}, bf16[16,3072]{1,0:T(8,128)(2,1)S(1)}, u32[]{:S(2)}, u32[]{:S(2)}) collective-permute-start(bf16[16,3072]{1,0:T(8,128)(2,1)S(1)} %fusion.2), channel_id=1, source_target_pairs={{0,1},{1,0},{2,3},{3,2},{4,5},{5,4},{6,7},{7,6},{8,9},{9,8},{10,11... | collective-permute-start | bytes 294920 | tf_op jit(solution)/shard_map/ppermute | solution.py:25
  86.1 4.7 %collective-permute-start.28 = (bf16[16,3072]{1,0:T(8,128)(2,1)S(1)}, bf16[16,3072]{1,0:T(8,128)(2,1)S(1)}, u32[]{:S(2)}, u32[]{:S(2)}) collective-permute-start(bf16[16,3072]{1,0:T(8,128)(2,1)S(1)} %fusion.1), channel_id=1, source_target_pairs={{0,2},{1,3},{2,0},{3,1},{4,6},{5,7},{6,4},{7,5},{8,10},{9,11},{10,... | collective-permute-start | bytes 294920 | tf_op jit(solution)/shard_map/ppermute | solution.py:25
  87.1 5.6 %collective-permute-start.30 = (bf16[16,3072]{1,0:T(8,128)(2,1)S(1)}, bf16[16,3072]{1,0:T(8,128)(2,1)S(1)}, u32[]{:S(2)}, u32[]{:S(2)}) collective-permute-start(bf16[16,3072]{1,0:T(8,128)(2,1)S(1)} %fusion), channel_id=1, source_target_pairs={{0,3},{1,2},{2,1},{3,0},{4,7},{5,6},{6,5},{7,4},{8,11},{9,10},{10,... | collective-permute-start | bytes 294920 | tf_op jit(solution)/shard_map/ppermute | solution.py:25
  93.4 1.4 %collective-permute-start.31 = (bf16[8,8192]{1,0:T(8,128)(2,1)S(1)}, bf16[8,8192]{1,0:T(8,128)(2,1)S(1)}, u32[]{:S(2)}, u32[]{:S(2)}) collective-permute-start(bf16[8,8192]{1,0:T(8,128)(2,1)S(1)} %get-tuple-element.64), channel_id=1, source_target_pairs={{0,16},{16,0},{1,17},{17,1},{2,18},{18,2},{3,19},{19,3},{4,20},{20... | collective-permute-start | bytes 393224 | tf_op jit(solution)/shard_map/ppermute | solution.py:25
  95.0 4.8 %collective-permute-start.32 = (bf16[4,8192]{1,0:T(4,128)(2,1)S(1)}, bf16[4,8192]{1,0:T(4,128)(2,1)S(1)}, u32[]{:S(2)}, u32[]{:S(2)}) collective-permute-start(bf16[4,8192]{1,0:T(4,128)(2,1)S(1)} %pad_maximum_fusion.8), channel_id=1, source_target_pairs={{0,4},{4,0},{8,12},{12,8},{1,5},{5,1},{9,13},{13,9},{2,6},{6,2},{1... | collective-permute-start | bytes 196616 | tf_op jit(solution)/shard_map/ppermute | solution.py:25
  96.0 7.5 %collective-permute-start.33 = (bf16[4,8192]{1,0:T(4,128)(2,1)S(1)}, bf16[4,8192]{1,0:T(4,128)(2,1)S(1)}, u32[]{:S(2)}, u32[]{:S(2)}) collective-permute-start(bf16[4,8192]{1,0:T(4,128)(2,1)S(1)} %pad_maximum_fusion.9), channel_id=1, source_target_pairs={{0,8},{4,12},{8,0},{12,4},{1,9},{5,13},{9,1},{13,5},{2,10},{6,14},... | collective-permute-start | bytes 196616 | tf_op jit(solution)/shard_map/ppermute | solution.py:25
  98.4 6.2 %collective-permute-start.34 = (bf16[4,8192]{1,0:T(4,128)(2,1)S(1)}, bf16[4,8192]{1,0:T(4,128)(2,1)S(1)}, u32[]{:S(2)}, u32[]{:S(2)}) collective-permute-start(bf16[4,8192]{1,0:T(4,128)(2,1)S(1)} %pad_maximum_fusion.10), channel_id=1, source_target_pairs={{0,12},{4,8},{8,4},{12,0},{1,13},{5,9},{9,5},{13,1},{2,14},{6,10},... | collective-permute-start | bytes 196616 | tf_op jit(solution)/shard_map/ppermute | solution.py:25

commit v4 on v3

--- a/solution.py
+++ b/solution.py
@@ -510,7 +510,7 @@
         ),
         name="first",
     )(place, gains, router, *in_vmem([near_block]), *near_all, up_matrix)
-    tile, depth = 256, 4
+    tile, depth = 256, 5
     early = width // cols * 5 // 8 * cols
     held = width // tile // 8 * tile
     sizes = (tp_count, exp_count, split, near_steps, far_steps, width, early)
@@ -530,7 +530,7 @@
             pltpu.SemaphoreType.DMA((depth,)),
             pltpu.SemaphoreType.DMA,
         ],
-        compiler_params=pltpu.CompilerParams(vmem_limit_bytes=(21 if small else 40) * MIB),
+        compiler_params=pltpu.CompilerParams(vmem_limit_bytes=(22 if small else 40) * MIB),
         cost_estimate=pl.CostEstimate(
             flops=4 * rows * half * units, bytes_accessed=4 * half * units, transcendentals=0
         ),

time: 106 us -> 106 us (level)
  no operation moved by 1% of the time
where the time goes in v4:
time: 106 us; the launch traced here: 105 us
  Pallas kernels  47.7 us (45%)
  starting transfers between devices  37.6 us (35%)
  waiting for transfers between devices  14.9 us (14%)
  other arithmetic  3.53 us (3%)
  local copies, waits for them, and re-layouts  1.32 us (1%)
    ppermute x35, starting transfers between devices, swap(): return lax.ppermute(value, axis, [(i, i ^ distance) for i in range(size)])  37.6 us
    pallas_call x1, Pallas kernels, per_device(): pl.pallas_call(functools.partial(second_kernel, sizes), out_shape=[jax.Sh...  17.2 us
    ppermute x35, waiting for transfers between devices, swap(): return lax.ppermute(value, axis, [(i, i ^ distance) for i in range(size)])  14.9 us
    pallas_call x2, Pallas kernels, fetch_up(): pl.pallas_call(functools.partial(fetch_kernel, places, exp_count, cols),...  8.67 us
    pallas_call x1, Pallas kernels, per_device(): pl.pallas_call(functools.partial(first_kernel, (tp_count, exp_count, spli...  8.1 us
    pallas_call x1, Pallas kernels, per_device(): pl.pallas_call(functools.partial(third_kernel, tp_count, early), out_shap...  5.36 us
    pallas_call x1, Pallas kernels, fetch_weight(): pl.pallas_call(weight_kernel, out_shape=[pltpu.VMEM(matrix.shape, matrix....  2.21 us
  transfers between devices with their start and end apart: 35, of which 12 were waited for; matrix products, arithmetic and copies ran while one was open for 4% of the time, Pallas kernels for 27%

profile of v4, /device:TPU:0, one launch (start us, length us, event | category | flops | bytes accessed | tf_op | source)
XLA Modules:
  0.0 105.4 jit_solution(5678447202779370313)
XLA Ops:
  0.0 3.0 %collective-permute-start.5 = (bf16[32,2048]{1,0:T(8,128)(2,1)}, bf16[32,2048]{1,0:T(8,128)(2,1)S(1)}, u32[]{:S(2)}, u32[]{:S(2)}) collective-permute-start(bf16[32,2048]{1,0:T(8,128)(2,1)} %param.10), channel_id=1, source_target_pairs={{0,4},{4,0},{8,12},{12,8},{1,5},{5,1},{9,13},{13,9},{2,6},{6,2},{1... | collective-permute-start | bytes 393224 | tf_op jit(solution)/shard_map/ppermute | solution.py:25
  3.0 2.5 %collective-permute-start.9 = (bf16[32,2048]{1,0:T(8,128)(2,1)}, bf16[32,2048]{1,0:T(8,128)(2,1)S(1)}, u32[]{:S(2)}, u32[]{:S(2)}) collective-permute-start(bf16[32,2048]{1,0:T(8,128)(2,1)} %param.10), channel_id=1, source_target_pairs={{0,12},{4,8},{8,4},{12,0},{1,13},{5,9},{9,5},{13,1},{2,14},{6,10},... | collective-permute-start | bytes 393224 | tf_op jit(solution)/shard_map/ppermute | solution.py:25
  5.5 0.1 collective-permute-start.7
  5.6 0.7 multiply_add_fusion.1
  6.4 0.2 select_reduce_fusion
  6.7 0.9 copy-done.1
  7.7 0.6 piece.1
  8.2 0.3 collective-permute-start
  8.7 0.1 add.93
  8.8 0.7 broadcast_in_dim.9
  9.6 2.2 %fetch_weight.1 = (bf16[2048,1024]{1,0:T(8,128)(2,1)S(1)}, bf16[8,2048]{1,0:T(8,128)(2,1)S(1)}) custom-call(bf16[2048,1024]{1,0:T(8,128)(2,1)} %source_ref.1, s32[3]{0:T(128)S(1)} %pad_add_fusion.place_ref.refs_0_, bf16[4,8,1152]{2,1,0:T(8,128)(2,1)S(1)} %get-tuple-element.36.refs_1_, f32[1,8192]{1,0:T(1,128)S(1)} %bitcast.20, ...), custom_call_target="tpu_custom_call" | custom-call | bytes 4194304 | tf_op jit(solution)/shard_map/fetch_weight/pallas_call | solution.py:99
  11.8 0.9 bitcast_add_fusion.refs_0_
  12.8 1.7 %collective-permute-start.1 = (bf16[2,8,1152]{2,1,0:T(8,128)(2,1)S(1)}, bf16[2,8,1152]{2,1,0:T(8,128)(2,1)S(1)}, u32[]{:S(2)}, u32[]{:S(2)}) collective-permute-start(bf16[2,8,1152]{2,1,0:T(8,128)(2,1)S(1)} %pad_maximum_fusion.11), channel_id=1, source_target_pairs={{0,4},{4,0},{8,12},{12,8},{1,5},{5,1},{9,13},{13,9},{2,6},{6,2},{1... | collective-permute-start | bytes 110600 | tf_op jit(solution)/shard_map/ppermute | solution.py:25
  14.5 0.3 collective-permute-start.6
  14.8 1.8 %collective-permute-start.2 = (bf16[2,8,1152]{2,1,0:T(8,128)(2,1)S(1)}, bf16[2,8,1152]{2,1,0:T(8,128)(2,1)S(1)}, u32[]{:S(2)}, u32[]{:S(2)}) collective-permute-start(bf16[2,8,1152]{2,1,0:T(8,128)(2,1)S(1)} %pad_maximum_fusion.12), channel_id=1, source_target_pairs={{0,8},{4,12},{8,0},{12,4},{1,9},{5,13},{9,1},{13,5},{2,10},{6,14},... | collective-permute-start | bytes 110600 | tf_op jit(solution)/shard_map/ppermute | solution.py:25
  16.5 1.0 collective-permute-start.3
  17.5 1.0 collective-permute-done.7.refs_4_
  18.5 0.5 collective-permute-start.8
  19.1 0.8 collective-permute-done.10.refs_7_
  19.9 0.2 collective-permute-done.8.refs_5_
  20.1 1.8 %project.1 = (bf16[64,1024]{1,0:T(8,128)(2,1)S(1)}, bf16[64,1024]{1,0:T(8,128)(2,1)S(1)}, bf16[64,1024]{1,0:T(8,128)(2,1)S(1)}, bf16[64,1024]{1,0:T(8,128)(2,1)S(1)}) custom-call(s32[3]{0:T(128)S(1)} %pad_add_fusion.place_ref.refs_0_, bf16[32,2048]{1,0:T(8,128)(2,1)S(1)} %bitcast_add_fusion.refs_0_, bf16[32,2048]{1,0:T(8,128)(2,1)S(1)} %collective-permute-done.4.refs_1_, ...), custom_call_target="tpu_custom_call" | custom-call | tf_op jit(solution)/shard_map/project/pallas_call | solution.py:447
  21.9 1.6 %collective-permute-start.11 = (bf16[64,1024]{1,0:T(8,128)(2,1)S(1)}, bf16[64,1024]{1,0:T(8,128)(2,1)S(1)}, u32[]{:S(2)}, u32[]{:S(2)}) collective-permute-start(bf16[64,1024]{1,0:T(8,128)(2,1)S(1)} %get-tuple-element.40), channel_id=1, source_target_pairs={{0,1},{1,0},{2,3},{3,2},{4,5},{5,4},{6,7},{7,6},{8,9},{9,8},{10,11... | collective-permute-start | bytes 393224 | tf_op jit(solution)/shard_map/ppermute | solution.py:25
  23.4 1.5 %collective-permute-start.12 = (bf16[64,1024]{1,0:T(8,128)(2,1)S(1)}, bf16[64,1024]{1,0:T(8,128)(2,1)S(1)}, u32[]{:S(2)}, u32[]{:S(2)}) collective-permute-start(bf16[64,1024]{1,0:T(8,128)(2,1)S(1)} %get-tuple-element.41), channel_id=1, source_target_pairs={{0,2},{1,3},{2,0},{3,1},{4,6},{5,7},{6,4},{7,5},{8,10},{9,11},{10,... | collective-permute-start | bytes 393224 | tf_op jit(solution)/shard_map/ppermute | solution.py:25
  25.0 0.5 collective-permute-start.13
  25.5 0.1 convert_reduce_fusion
  25.6 5.3 %fetch_up.2.refs_4_ = bf16[2048,3072]{1,0:T(8,128)(2,1)S(1)} custom-call(s32[3]{0:T(128)S(1)} %pad_add_fusion.place_ref.refs_0_, bf16[8192,3072]{1,0:T(8,128)(2,1)} %bitcast.26, bf16[64,1024]{1,0:T(8,128)(2,1)S(1)} %get-tuple-element.39.refs_0_, f32[1,8192]{1,0:T(1,128)S(1)} %bitcast.21, bf16[8,16]{1,0:T(8,128)(2,1)S(1)} %compare_convert_fusion.refs_3_.refs_2_.picks_ref), custom_call_target="tpu_custom_call" | custom-call | bytes 12582912 | tf_op jit(solution)/shard_map/fetch_up/pallas_call | solution.py:57
  30.9 0.8 collective-permute-done.12.refs_2_
  31.7 0.8 slot.2
  32.6 1.2 %collective-permute-done.14 = bf16[2,16,1024]{2,1,0:T(8,128)(2,1)S(1)} collective-permute-done((bf16[2,16,1024]{2,1,0:T(8,128)(2,1)S(1)}, bf16[2,16,1024]{2,1,0:T(8,128)(2,1)S(1)}, u32[]{:S(2)}, u32[]{:S(2)}) %collective-permute-start.14) | collective-permute-done | bytes 65568 | tf_op jit(solution)/shard_map/ppermute | solution.py:25
  33.9 0.8 slot.3
  34.8 0.2 collective-permute-start.16
  35.0 1.1 %collective-permute-done.16 = bf16[2,16,1024]{2,1,0:T(8,128)(2,1)S(1)} collective-permute-done((bf16[2,16,1024]{2,1,0:T(8,128)(2,1)S(1)}, bf16[2,16,1024]{2,1,0:T(8,128)(2,1)S(1)}, u32[]{:S(2)}, u32[]{:S(2)}) %collective-permute-start.16) | collective-permute-done | bytes 65568 | tf_op jit(solution)/shard_map/ppermute | solution.py:25
  36.1 2.7 %collective-permute-start.18 = (bf16[2,16,1024]{2,1,0:T(8,128)(2,1)S(1)}, bf16[2,16,1024]{2,1,0:T(8,128)(2,1)S(1)}, u32[]{:S(2)}, u32[]{:S(2)}) collective-permute-start(bf16[2,16,1024]{2,1,0:T(8,128)(2,1)S(1)} %pad_maximum_fusion.6), channel_id=1, source_target_pairs={{0,12},{4,8},{8,4},{12,0},{1,13},{5,9},{9,5},{13,1},{2,14},{6,10},... | collective-permute-start | bytes 196616 | tf_op jit(solution)/shard_map/ppermute | solution.py:25
  38.8 0.9 collective-permute-start.17
  39.7 1.7 %collective-permute-start.21 = (bf16[2,2,16,1024]{3,2,1,0:T(8,128)(2,1)S(1)}, bf16[2,2,16,1024]{3,2,1,0:T(8,128)(2,1)S(1)}, u32[]{:S(2)}, u32[]{:S(2)}) collective-permute-start(bf16[2,2,16,1024]{3,2,1,0:T(8,128)(2,1)S(1)} %pad_maximum_fusion.2.refs_0_), channel_id=1, source_target_pairs={{0,3},{1,2},{2,1},{3,0},{4,7},{5,6},{6,5},{7,4},{8,11},{9,10},{10,... | collective-permute-start | bytes 393224 | tf_op jit(solution)/shard_map/ppermute | solution.py:25
  41.5 1.0 collective-permute-start.20
  42.5 0.8 collective-permute-start.19
  43.3 3.4 %fetch_up.3.up_ref = bf16[1024,3072]{1,0:T(8,128)(2,1)S(1)} custom-call(s32[3]{0:T(128)S(1)} %pad_add_fusion.place_ref.refs_0_, bf16[8192,3072]{1,0:T(8,128)(2,1)} %bitcast.27, bf16[2,2,16,1024]{3,2,1,0:T(8,128)(2,1)S(1)} %pad_maximum_fusion.2.refs_0_), custom_call_target="tpu_custom_call" | custom-call | bytes 6291456 | tf_op jit(solution)/shard_map/fetch_up/pallas_call | solution.py:57
  46.8 1.7 %collective-permute-start.24 = (bf16[2,2,16,1024]{3,2,1,0:T(8,128)(2,1)S(1)}, bf16[2,2,16,1024]{3,2,1,0:T(8,128)(2,1)S(1)}, u32[]{:S(2)}, u32[]{:S(2)}) collective-permute-start(bf16[2,2,16,1024]{3,2,1,0:T(8,128)(2,1)S(1)} %pad_maximum_fusion.3.refs_0_), channel_id=1, source_target_pairs={{0,3},{1,2},{2,1},{3,0},{4,7},{5,6},{6,5},{7,4},{8,11},{9,10},{10,... | collective-permute-start | bytes 393224 | tf_op jit(solution)/shard_map/ppermute | solution.py:25
  48.5 1.0 collective-permute-start.23
  49.5 0.8 collective-permute-start.22
  50.3 8.1 %first.1 = (f32[64,3072]{1,0:T(8,128)S(1)}, f32[64,128]{1,0:T(8,128)S(1)}, f32[16,128]{1,0:T(8,128)S(1)}) custom-call(s32[3]{0:T(128)S(1)} %pad_add_fusion.place_ref.refs_0_, f32[1,8192]{1,0:T(1,128)S(1)} %bitcast.22, bf16[2,4,8192]{2,1,0:T(4,128)(2,1)S(1)} %copy-done, bf16[1024,3072]{1,0:T(8,128)(2,1)S(1)} %fetch_up.3.up_ref, ...), custom_call_target="tpu_custom_call" | custom-call | flops 1610612736 | bytes 25165824 | tf_op jit(solution)/shard_map/first/pallas_call | solution.py:493
  58.5 17.2 %second.1 = (bf16[16,5120]{1,0:T(8,128)(2,1)S(1)}, bf16[16,5120]{1,0:T(8,128)(2,1)S(1)}, bf16[16,5120]{1,0:T(8,128)(2,1)S(1)}, bf16[16,5120]{1,0:T(8,128)(2,1)S(...) custom-call(s32[3]{0:T(128)S(1)} %pad_add_fusion.place_ref.refs_0_, ...), custom_call_target="tpu_custom_call" | custom-call | flops 3221225472 | bytes 50331648 | tf_op jit(solution)/shard_map/second/pallas_call | solution.py:517
  75.7 1.3 %collective-permute-start.25 = (bf16[16,5120]{1,0:T(8,128)(2,1)S(1)}, bf16[16,5120]{1,0:T(8,128)(2,1)S(1)}, u32[]{:S(2)}, u32[]{:S(2)}) collective-permute-start(bf16[16,5120]{1,0:T(8,128)(2,1)S(1)} %get-tuple-element.55), channel_id=1, source_target_pairs={{0,1},{1,0},{2,3},{3,2},{4,5},{5,4},{6,7},{7,6},{8,9},{9,8},{10,11... | collective-permute-start | bytes 491528 | tf_op jit(solution)/shard_map/ppermute | solution.py:25
  77.0 1.0 collective-permute-start.27
  78.0 1.3 %collective-permute-start.29 = (bf16[16,5120]{1,0:T(8,128)(2,1)S(1)}, bf16[16,5120]{1,0:T(8,128)(2,1)S(1)}, u32[]{:S(2)}, u32[]{:S(2)}) collective-permute-start(bf16[16,5120]{1,0:T(8,128)(2,1)S(1)} %get-tuple-element.59), channel_id=1, source_target_pairs={{0,3},{1,2},{2,1},{3,0},{4,7},{5,6},{6,5},{7,4},{8,11},{9,10},{10,... | collective-permute-start | bytes 491528 | tf_op jit(solution)/shard_map/ppermute | solution.py:25
  79.2 5.4 %third.1 = (bf16[16,3072]{1,0:T(8,128)(2,1)S(1)}, bf16[16,3072]{1,0:T(8,128)(2,1)S(1)}, bf16[16,3072]{1,0:T(8,128)(2,1)S(1)}, bf16[16,3072]{1,0:T(8,128)(2,1)S(1)}) custom-call(bf16[64,3072]{1,0:T(8,128)(2,1)S(1)} %get-tuple-element.51.hidden, bf16[3072,1024]{1,0:T(8,128)(2,1)S(1)} %get-tuple-element.52.held_ref, bf16[3072,8192]{1,0:T(8,128)(2,1)} %bitcast.31), custom_call_target="tpu_custom_call" | custom-call | flops 1610612736 | bytes 25165824 | tf_op jit(solution)/shard_map/third/pallas_call | solution.py:542
  84.6 1.3 %collective-permute-start.26 = (bf16[16,3072]{1,0:T(8,128)(2,1)S(1)}, bf16[16,3072]{1,0:T(8,128)(2,1)S(1)}, u32[]{:S(2)}, u32[]{:S(2)}) collective-permute-start(bf16[16,3072]{1,0:T(8,128)(2,1)S(1)} %fusion.2), channel_id=1, source_target_pairs={{0,1},{1,0},{2,3},{3,2},{4,5},{5,4},{6,7},{7,6},{8,9},{9,8},{10,11... | collective-permute-start | bytes 294920 | tf_op jit(solution)/shard_map/ppermute | solution.py:25
  85.9 1.0 collective-permute-start.28
  87.0 1.3 %collective-permute-start.30 = (bf16[16,3072]{1,0:T(8,128)(2,1)S(1)}, bf16[16,3072]{1,0:T(8,128)(2,1)S(1)}, u32[]{:S(2)}, u32[]{:S(2)}) collective-permute-start(bf16[16,3072]{1,0:T(8,128)(2,1)S(1)} %fusion), channel_id=1, source_target_pairs={{0,3},{1,2},{2,1},{3,0},{4,7},{5,6},{6,5},{7,4},{8,11},{9,10},{10,... | collective-permute-start | bytes 294920 | tf_op jit(solution)/shard_map/ppermute | solution.py:25
  88.4 0.7 combine.2
  89.1 0.2 collective-permute-done.26.refs_1_
  89.3 1.3 %collective-permute-done.28.refs_2_ = bf16[16,3072]{1,0:T(8,128)(2,1)S(1)} collective-permute-done((bf16[16,3072]{1,0:T(8,128)(2,1)S(1)}, bf16[16,3072]{1,0:T(8,128)(2,1)S(1)}, u32[]{:S(2)}, u32[]{:S(2)}) %collective-permute-start.28) | collective-permute-done | bytes 98336 | tf_op jit(solution)/shard_map/ppermute | solution.py:25
  90.6 2.0 %collective-permute-done.30.refs_3_ = bf16[16,3072]{1,0:T(8,128)(2,1)S(1)} collective-permute-done((bf16[16,3072]{1,0:T(8,128)(2,1)S(1)}, bf16[16,3072]{1,0:T(8,128)(2,1)S(1)}, u32[]{:S(2)}, u32[]{:S(2)}) %collective-permute-start.30) | collective-permute-done | bytes 98336 | tf_op jit(solution)/shard_map/ppermute | solution.py:25
  92.6 0.6 combine.3
  93.3 0.1 fusion.4
  93.4 1.2 %collective-permute-done.31 = bf16[8,8192]{1,0:T(8,128)(2,1)S(1)} collective-permute-done((bf16[8,8192]{1,0:T(8,128)(2,1)S(1)}, bf16[8,8192]{1,0:T(8,128)(2,1)S(1)}, u32[]{:S(2)}, u32[]{:S(2)}) %collective-permute-start.31) | collective-permute-done | bytes 131104 | tf_op jit(solution)/shard_map/ppermute | solution.py:25
  94.6 0.1 fusion.5
  94.8 1.0 collective-permute-start.32
  95.9 2.4 %collective-permute-start.33 = (bf16[4,8192]{1,0:T(4,128)(2,1)S(1)}, bf16[4,8192]{1,0:T(4,128)(2,1)S(1)}, u32[]{:S(2)}, u32[]{:S(2)}) collective-permute-start(bf16[4,8192]{1,0:T(4,128)(2,1)S(1)} %pad_maximum_fusion.9), channel_id=1, source_target_pairs={{0,8},{4,12},{8,0},{12,4},{1,9},{5,13},{9,1},{13,5},{2,10},{6,14},... | collective-permute-start | bytes 196616 | tf_op jit(solution)/shard_map/ppermute | solution.py:25
  98.3 1.3 %collective-permute-start.34 = (bf16[4,8192]{1,0:T(4,128)(2,1)S(1)}, bf16[4,8192]{1,0:T(4,128)(2,1)S(1)}, u32[]{:S(2)}, u32[]{:S(2)}) collective-permute-start(bf16[4,8192]{1,0:T(4,128)(2,1)S(1)} %pad_maximum_fusion.10), channel_id=1, source_target_pairs={{0,12},{4,8},{8,4},{12,0},{1,13},{5,9},{9,5},{13,1},{2,14},{6,10},... | collective-permute-start | bytes 196616 | tf_op jit(solution)/shard_map/ppermute | solution.py:25
  99.6 3.7 %collective-permute-done.33.refs_2_ = bf16[4,8192]{1,0:T(4,128)(2,1)S(1)} collective-permute-done((bf16[4,8192]{1,0:T(4,128)(2,1)S(1)}, bf16[4,8192]{1,0:T(4,128)(2,1)S(1)}, u32[]{:S(2)}, u32[]{:S(2)}) %collective-permute-start.33) | collective-permute-done | bytes 65568 | tf_op jit(solution)/shard_map/ppermute | solution.py:25
  103.3 1.2 %collective-permute-done.34.refs_3_ = bf16[4,8192]{1,0:T(4,128)(2,1)S(1)} collective-permute-done((bf16[4,8192]{1,0:T(4,128)(2,1)S(1)}, bf16[4,8192]{1,0:T(4,128)(2,1)S(1)}, u32[]{:S(2)}, u32[]{:S(2)}) %collective-permute-start.34) | collective-permute-done | bytes 65568 | tf_op jit(solution)/shard_map/ppermute | solution.py:25
  104.5 0.9 final.1
  (69 shorter events, 1.3 us)
Async XLA Ops:
  0.0 14.5 %collective-permute-start.5 = (bf16[32,2048]{1,0:T(8,128)(2,1)}, bf16[32,2048]{1,0:T(8,128)(2,1)S(1)}, u32[]{:S(2)}, u32[]{:S(2)}) collective-permute-start(bf16[32,2048]{1,0:T(8,128)(2,1)} %param.10), channel_id=1, source_target_pairs={{0,4},{4,0},{8,12},{12,8},{1,5},{5,1},{9,13},{13,9},{2,6},{6,2},{1... | collective-permute-start | bytes 393224 | tf_op jit(solution)/shard_map/ppermute | solution.py:25
  3.0 11.7 %collective-permute-start.4 = (bf16[32,2048]{1,0:T(8,128)(2,1)}, bf16[32,2048]{1,0:T(8,128)(2,1)S(1)}, u32[]{:S(2)}, u32[]{:S(2)}) collective-permute-start(bf16[32,2048]{1,0:T(8,128)(2,1)} %param.10), channel_id=1, source_target_pairs={{0,16},{16,0},{1,17},{17,1},{2,18},{18,2},{3,19},{19,3},{4,20},{20... | collective-permute-start | bytes 393224 | tf_op jit(solution)/shard_map/ppermute | solution.py:25
  3.0 13.5 %collective-permute-start.9 = (bf16[32,2048]{1,0:T(8,128)(2,1)}, bf16[32,2048]{1,0:T(8,128)(2,1)S(1)}, u32[]{:S(2)}, u32[]{:S(2)}) collective-permute-start(bf16[32,2048]{1,0:T(8,128)(2,1)} %param.10), channel_id=1, source_target_pairs={{0,12},{4,8},{8,4},{12,0},{1,13},{5,9},{9,5},{13,1},{2,14},{6,10},... | collective-permute-start | bytes 393224 | tf_op jit(solution)/shard_map/ppermute | solution.py:25
  5.5 13.0 %collective-permute-start.7 = (bf16[32,2048]{1,0:T(8,128)(2,1)}, bf16[32,2048]{1,0:T(8,128)(2,1)S(1)}, u32[]{:S(2)}, u32[]{:S(2)}) collective-permute-start(bf16[32,2048]{1,0:T(8,128)(2,1)} %param.10), channel_id=1, source_target_pairs={{0,8},{4,12},{8,0},{12,4},{1,9},{5,13},{9,1},{13,5},{2,10},{6,14},... | collective-permute-start | bytes 393224 | tf_op jit(solution)/shard_map/ppermute | solution.py:25
  6.7 0.9 copy-start.1
  8.2 4.5 %collective-permute-start = (bf16[4,8,1152]{2,1,0:T(8,128)(2,1)S(1)}, bf16[4,8,1152]{2,1,0:T(8,128)(2,1)S(1)}, u32[]{:S(2)}, u32[]{:S(2)}) collective-permute-start(bf16[4,8,1152]{2,1,0:T(8,128)(2,1)S(1)} %get-tuple-element.36.refs_1_), channel_id=1, source_target_pairs={{0,16},{16,0},{1,17},{17,1},{2,18},{18,2},{3,19},{19,3},{4,20},{20... | collective-permute-start | bytes 221192 | tf_op jit(solution)/shard_map/ppermute | solution.py:25
  12.8 12.2 %collective-permute-start.1 = (bf16[2,8,1152]{2,1,0:T(8,128)(2,1)S(1)}, bf16[2,8,1152]{2,1,0:T(8,128)(2,1)S(1)}, u32[]{:S(2)}, u32[]{:S(2)}) collective-permute-start(bf16[2,8,1152]{2,1,0:T(8,128)(2,1)S(1)} %pad_maximum_fusion.11), channel_id=1, source_target_pairs={{0,4},{4,0},{8,12},{12,8},{1,5},{5,1},{9,13},{13,9},{2,6},{6,2},{1... | collective-permute-start | bytes 110600 | tf_op jit(solution)/shard_map/ppermute | solution.py:25
  14.5 4.1 %collective-permute-start.6 = (bf16[32,2048]{1,0:T(8,128)(2,1)S(1)}, bf16[32,2048]{1,0:T(8,128)(2,1)S(1)}, u32[]{:S(2)}, u32[]{:S(2)}) collective-permute-start(bf16[32,2048]{1,0:T(8,128)(2,1)S(1)} %collective-permute-done.5.refs_2_), channel_id=1, source_target_pairs={{0,16},{16,0},{1,17},{17,1},{2,18},{18,2},{3,19},{19,3},{4,20},{20... | collective-permute-start | bytes 393224 | tf_op jit(solution)/shard_map/ppermute | solution.py:25
  14.8 10.7 %collective-permute-start.2 = (bf16[2,8,1152]{2,1,0:T(8,128)(2,1)S(1)}, bf16[2,8,1152]{2,1,0:T(8,128)(2,1)S(1)}, u32[]{:S(2)}, u32[]{:S(2)}) collective-permute-start(bf16[2,8,1152]{2,1,0:T(8,128)(2,1)S(1)} %pad_maximum_fusion.12), channel_id=1, source_target_pairs={{0,8},{4,12},{8,0},{12,4},{1,9},{5,13},{9,1},{13,5},{2,10},{6,14},... | collective-permute-start | bytes 110600 | tf_op jit(solution)/shard_map/ppermute | solution.py:25
  16.5 8.9 %collective-permute-start.3 = (bf16[2,8,1152]{2,1,0:T(8,128)(2,1)S(1)}, bf16[2,8,1152]{2,1,0:T(8,128)(2,1)S(1)}, u32[]{:S(2)}, u32[]{:S(2)}) collective-permute-start(bf16[2,8,1152]{2,1,0:T(8,128)(2,1)S(1)} %pad_maximum_fusion.13), channel_id=1, source_target_pairs={{0,12},{4,8},{8,4},{12,0},{1,13},{5,9},{9,5},{13,1},{2,14},{6,10},... | collective-permute-start | bytes 110600 | tf_op jit(solution)/shard_map/ppermute | solution.py:25
  18.5 1.3 %collective-permute-start.10 = (bf16[32,2048]{1,0:T(8,128)(2,1)S(1)}, bf16[32,2048]{1,0:T(8,128)(2,1)S(1)}, u32[]{:S(2)}, u32[]{:S(2)}) collective-permute-start(bf16[32,2048]{1,0:T(8,128)(2,1)S(1)} %collective-permute-done.9.refs_6_), channel_id=1, source_target_pairs={{0,16},{16,0},{1,17},{17,1},{2,18},{18,2},{3,19},{19,3},{4,20},{20... | collective-permute-start | bytes 393224 | tf_op jit(solution)/shard_map/ppermute | solution.py:25
  18.5 1.5 %collective-permute-start.8 = (bf16[32,2048]{1,0:T(8,128)(2,1)S(1)}, bf16[32,2048]{1,0:T(8,128)(2,1)S(1)}, u32[]{:S(2)}, u32[]{:S(2)}) collective-permute-start(bf16[32,2048]{1,0:T(8,128)(2,1)S(1)} %collective-permute-done.7.refs_4_), channel_id=1, source_target_pairs={{0,16},{16,0},{1,17},{17,1},{2,18},{18,2},{3,19},{19,3},{4,20},{20... | collective-permute-start | bytes 393224 | tf_op jit(solution)/shard_map/ppermute | solution.py:25
  21.9 9.0 %collective-permute-start.11 = (bf16[64,1024]{1,0:T(8,128)(2,1)S(1)}, bf16[64,1024]{1,0:T(8,128)(2,1)S(1)}, u32[]{:S(2)}, u32[]{:S(2)}) collective-permute-start(bf16[64,1024]{1,0:T(8,128)(2,1)S(1)} %get-tuple-element.40), channel_id=1, source_target_pairs={{0,1},{1,0},{2,3},{3,2},{4,5},{5,4},{6,7},{7,6},{8,9},{9,8},{10,11... | collective-permute-start | bytes 393224 | tf_op jit(solution)/shard_map/ppermute | solution.py:25
  23.4 8.3 %collective-permute-start.12 = (bf16[64,1024]{1,0:T(8,128)(2,1)S(1)}, bf16[64,1024]{1,0:T(8,128)(2,1)S(1)}, u32[]{:S(2)}, u32[]{:S(2)}) collective-permute-start(bf16[64,1024]{1,0:T(8,128)(2,1)S(1)} %get-tuple-element.41), channel_id=1, source_target_pairs={{0,2},{1,3},{2,0},{3,1},{4,6},{5,7},{6,4},{7,5},{8,10},{9,11},{10,... | collective-permute-start | bytes 393224 | tf_op jit(solution)/shard_map/ppermute | solution.py:25
  25.0 6.7 %collective-permute-start.13 = (bf16[64,1024]{1,0:T(8,128)(2,1)S(1)}, bf16[64,1024]{1,0:T(8,128)(2,1)S(1)}, u32[]{:S(2)}, u32[]{:S(2)}) collective-permute-start(bf16[64,1024]{1,0:T(8,128)(2,1)S(1)} %get-tuple-element.42), channel_id=1, source_target_pairs={{0,3},{1,2},{2,1},{3,0},{4,7},{5,6},{6,5},{7,4},{8,11},{9,10},{10,... | collective-permute-start | bytes 393224 | tf_op jit(solution)/shard_map/ppermute | solution.py:25
  32.5 1.3 %collective-permute-start.14 = (bf16[2,16,1024]{2,1,0:T(8,128)(2,1)S(1)}, bf16[2,16,1024]{2,1,0:T(8,128)(2,1)S(1)}, u32[]{:S(2)}, u32[]{:S(2)}) collective-permute-start(bf16[2,16,1024]{2,1,0:T(8,128)(2,1)S(1)} %get-tuple-element.44), channel_id=1, source_target_pairs={{0,16},{16,0},{1,17},{17,1},{2,18},{18,2},{3,19},{19,3},{4,20},{20... | collective-permute-start | bytes 196616 | tf_op jit(solution)/shard_map/ppermute | solution.py:25
  33.9 5.9 %collective-permute-start.15 = (bf16[2,16,1024]{2,1,0:T(8,128)(2,1)S(1)}, bf16[2,16,1024]{2,1,0:T(8,128)(2,1)S(1)}, u32[]{:S(2)}, u32[]{:S(2)}) collective-permute-start(bf16[2,16,1024]{2,1,0:T(8,128)(2,1)S(1)} %pad_maximum_fusion.4.refs_4_), channel_id=1, source_target_pairs={{0,4},{4,0},{8,12},{12,8},{1,5},{5,1},{9,13},{13,9},{2,6},{6,2},{1... | collective-permute-start | bytes 196616 | tf_op jit(solution)/shard_map/ppermute | solution.py:25
  34.8 1.3 %collective-permute-start.16 = (bf16[2,16,1024]{2,1,0:T(8,128)(2,1)S(1)}, bf16[2,16,1024]{2,1,0:T(8,128)(2,1)S(1)}, u32[]{:S(2)}, u32[]{:S(2)}) collective-permute-start(bf16[2,16,1024]{2,1,0:T(8,128)(2,1)S(1)} %get-tuple-element.46), channel_id=1, source_target_pairs={{0,16},{16,0},{1,17},{17,1},{2,18},{18,2},{3,19},{19,3},{4,20},{20... | collective-permute-start | bytes 196616 | tf_op jit(solution)/shard_map/ppermute | solution.py:25
  36.1 10.6 %collective-permute-start.18 = (bf16[2,16,1024]{2,1,0:T(8,128)(2,1)S(1)}, bf16[2,16,1024]{2,1,0:T(8,128)(2,1)S(1)}, u32[]{:S(2)}, u32[]{:S(2)}) collective-permute-start(bf16[2,16,1024]{2,1,0:T(8,128)(2,1)S(1)} %pad_maximum_fusion.6), channel_id=1, source_target_pairs={{0,12},{4,8},{8,4},{12,0},{1,13},{5,9},{9,5},{13,1},{2,14},{6,10},... | collective-permute-start | bytes 196616 | tf_op jit(solution)/shard_map/ppermute | solution.py:25
  38.8 7.9 %collective-permute-start.17 = (bf16[2,16,1024]{2,1,0:T(8,128)(2,1)S(1)}, bf16[2,16,1024]{2,1,0:T(8,128)(2,1)S(1)}, u32[]{:S(2)}, u32[]{:S(2)}) collective-permute-start(bf16[2,16,1024]{2,1,0:T(8,128)(2,1)S(1)} %pad_maximum_fusion.5), channel_id=1, source_target_pairs={{0,8},{4,12},{8,0},{12,4},{1,9},{5,13},{9,1},{13,5},{2,10},{6,14},... | collective-permute-start | bytes 196616 | tf_op jit(solution)/shard_map/ppermute | solution.py:25
  39.7 10.6 %copy-start = (bf16[2,4,8192]{2,1,0:T(4,128)(2,1)S(1)}, bf16[2,4,8192]{2,1,0:T(4,128)(2,1)}, u32[]{:S(2)}) copy-start(bf16[2,4,8192]{2,1,0:T(4,128)(2,1)} %router_ref.3) | copy-start | bytes 393220
  39.7 9.8 %collective-permute-start.21 = (bf16[2,2,16,1024]{3,2,1,0:T(8,128)(2,1)S(1)}, bf16[2,2,16,1024]{3,2,1,0:T(8,128)(2,1)S(1)}, u32[]{:S(2)}, u32[]{:S(2)}) collective-permute-start(bf16[2,2,16,1024]{3,2,1,0:T(8,128)(2,1)S(1)} %pad_maximum_fusion.2.refs_0_), channel_id=1, source_target_pairs={{0,3},{1,2},{2,1},{3,0},{4,7},{5,6},{6,5},{7,4},{8,11},{9,10},{10,... | collective-permute-start | bytes 393224 | tf_op jit(solution)/shard_map/ppermute | solution.py:25
  41.5 8.9 %collective-permute-start.20 = (bf16[2,2,16,1024]{3,2,1,0:T(8,128)(2,1)S(1)}, bf16[2,2,16,1024]{3,2,1,0:T(8,128)(2,1)S(1)}, u32[]{:S(2)}, u32[]{:S(2)}) collective-permute-start(bf16[2,2,16,1024]{3,2,1,0:T(8,128)(2,1)S(1)} %pad_maximum_fusion.2.refs_0_), channel_id=1, source_target_pairs={{0,2},{1,3},{2,0},{3,1},{4,6},{5,7},{6,4},{7,5},{8,10},{9,11},{10,... | collective-permute-start | bytes 393224 | tf_op jit(solution)/shard_map/ppermute | solution.py:25
  42.5 7.8 %collective-permute-start.19 = (bf16[2,2,16,1024]{3,2,1,0:T(8,128)(2,1)S(1)}, bf16[2,2,16,1024]{3,2,1,0:T(8,128)(2,1)S(1)}, u32[]{:S(2)}, u32[]{:S(2)}) collective-permute-start(bf16[2,2,16,1024]{3,2,1,0:T(8,128)(2,1)S(1)} %pad_maximum_fusion.2.refs_0_), channel_id=1, source_target_pairs={{0,1},{1,0},{2,3},{3,2},{4,5},{5,4},{6,7},{7,6},{8,9},{9,8},{10,11... | collective-permute-start | bytes 393224 | tf_op jit(solution)/shard_map/ppermute | solution.py:25
  46.8 11.7 %collective-permute-start.24 = (bf16[2,2,16,1024]{3,2,1,0:T(8,128)(2,1)S(1)}, bf16[2,2,16,1024]{3,2,1,0:T(8,128)(2,1)S(1)}, u32[]{:S(2)}, u32[]{:S(2)}) collective-permute-start(bf16[2,2,16,1024]{3,2,1,0:T(8,128)(2,1)S(1)} %pad_maximum_fusion.3.refs_0_), channel_id=1, source_target_pairs={{0,3},{1,2},{2,1},{3,0},{4,7},{5,6},{6,5},{7,4},{8,11},{9,10},{10,... | collective-permute-start | bytes 393224 | tf_op jit(solution)/shard_map/ppermute | solution.py:25
  48.5 10.0 %collective-permute-start.23 = (bf16[2,2,16,1024]{3,2,1,0:T(8,128)(2,1)S(1)}, bf16[2,2,16,1024]{3,2,1,0:T(8,128)(2,1)S(1)}, u32[]{:S(2)}, u32[]{:S(2)}) collective-permute-start(bf16[2,2,16,1024]{3,2,1,0:T(8,128)(2,1)S(1)} %pad_maximum_fusion.3.refs_0_), channel_id=1, source_target_pairs={{0,2},{1,3},{2,0},{3,1},{4,6},{5,7},{6,4},{7,5},{8,10},{9,11},{10,... | collective-permute-start | bytes 393224 | tf_op jit(solution)/shard_map/ppermute | solution.py:25
  49.5 8.9 %collective-permute-start.22 = (bf16[2,2,16,1024]{3,2,1,0:T(8,128)(2,1)S(1)}, bf16[2,2,16,1024]{3,2,1,0:T(8,128)(2,1)S(1)}, u32[]{:S(2)}, u32[]{:S(2)}) collective-permute-start(bf16[2,2,16,1024]{3,2,1,0:T(8,128)(2,1)S(1)} %pad_maximum_fusion.3.refs_0_), channel_id=1, source_target_pairs={{0,1},{1,0},{2,3},{3,2},{4,5},{5,4},{6,7},{7,6},{8,9},{9,8},{10,11... | collective-permute-start | bytes 393224 | tf_op jit(solution)/shard_map/ppermute | solution.py:25
  75.7 8.9 %collective-permute-start.25 = (bf16[16,5120]{1,0:T(8,128)(2,1)S(1)}, bf16[16,5120]{1,0:T(8,128)(2,1)S(1)}, u32[]{:S(2)}, u32[]{:S(2)}) collective-permute-start(bf16[16,5120]{1,0:T(8,128)(2,1)S(1)} %get-tuple-element.55), channel_id=1, source_target_pairs={{0,1},{1,0},{2,3},{3,2},{4,5},{5,4},{6,7},{7,6},{8,9},{9,8},{10,11... | collective-permute-start | bytes 491528 | tf_op jit(solution)/shard_map/ppermute | solution.py:25
  77.0 9.0 %collective-permute-start.27 = (bf16[16,5120]{1,0:T(8,128)(2,1)S(1)}, bf16[16,5120]{1,0:T(8,128)(2,1)S(1)}, u32[]{:S(2)}, u32[]{:S(2)}) collective-permute-start(bf16[16,5120]{1,0:T(8,128)(2,1)S(1)} %get-tuple-element.57), channel_id=1, source_target_pairs={{0,2},{1,3},{2,0},{3,1},{4,6},{5,7},{6,4},{7,5},{8,10},{9,11},{10,... | collective-permute-start | bytes 491528 | tf_op jit(solution)/shard_map/ppermute | solution.py:25
  78.0 9.0 %collective-permute-start.29 = (bf16[16,5120]{1,0:T(8,128)(2,1)S(1)}, bf16[16,5120]{1,0:T(8,128)(2,1)S(1)}, u32[]{:S(2)}, u32[]{:S(2)}) collective-permute-start(bf16[16,5120]{1,0:T(8,128)(2,1)S(1)} %get-tuple-element.59), channel_id=1, source_target_pairs={{0,3},{1,2},{2,1},{3,0},{4,7},{5,6},{6,5},{7,4},{8,11},{9,10},{10,... | collective-permute-start | bytes 491528 | tf_op jit(solution)/shard_map/ppermute | solution.py:25
  84.6 4.7 %collective-permute-start.26 = (bf16[16,3072]{1,0:T(8,128)(2,1)S(1)}, bf16[16,3072]{1,0:T(8,128)(2,1)S(1)}, u32[]{:S(2)}, u32[]{:S(2)}) collective-permute-start(bf16[16,3072]{1,0:T(8,128)(2,1)S(1)} %fusion.2), channel_id=1, source_target_pairs={{0,1},{1,0},{2,3},{3,2},{4,5},{5,4},{6,7},{7,6},{8,9},{9,8},{10,11... | collective-permute-start | bytes 294920 | tf_op jit(solution)/shard_map/ppermute | solution.py:25
  85.9 4.7 %collective-permute-start.28 = (bf16[16,3072]{1,0:T(8,128)(2,1)S(1)}, bf16[16,3072]{1,0:T(8,128)(2,1)S(1)}, u32[]{:S(2)}, u32[]{:S(2)}) collective-permute-start(bf16[16,3072]{1,0:T(8,128)(2,1)S(1)} %fusion.1), channel_id=1, source_target_pairs={{0,2},{1,3},{2,0},{3,1},{4,6},{5,7},{6,4},{7,5},{8,10},{9,11},{10,... | collective-permute-start | bytes 294920 | tf_op jit(solution)/shard_map/ppermute | solution.py:25
  87.0 5.6 %collective-permute-start.30 = (bf16[16,3072]{1,0:T(8,128)(2,1)S(1)}, bf16[16,3072]{1,0:T(8,128)(2,1)S(1)}, u32[]{:S(2)}, u32[]{:S(2)}) collective-permute-start(bf16[16,3072]{1,0:T(8,128)(2,1)S(1)} %fusion), channel_id=1, source_target_pairs={{0,3},{1,2},{2,1},{3,0},{4,7},{5,6},{6,5},{7,4},{8,11},{9,10},{10,... | collective-permute-start | bytes 294920 | tf_op jit(solution)/shard_map/ppermute | solution.py:25
  93.2 1.4 %collective-permute-start.31 = (bf16[8,8192]{1,0:T(8,128)(2,1)S(1)}, bf16[8,8192]{1,0:T(8,128)(2,1)S(1)}, u32[]{:S(2)}, u32[]{:S(2)}) collective-permute-start(bf16[8,8192]{1,0:T(8,128)(2,1)S(1)} %get-tuple-element.64), channel_id=1, source_target_pairs={{0,16},{16,0},{1,17},{17,1},{2,18},{18,2},{3,19},{19,3},{4,20},{20... | collective-permute-start | bytes 393224 | tf_op jit(solution)/shard_map/ppermute | solution.py:25
  94.8 4.8 %collective-permute-start.32 = (bf16[4,8192]{1,0:T(4,128)(2,1)S(1)}, bf16[4,8192]{1,0:T(4,128)(2,1)S(1)}, u32[]{:S(2)}, u32[]{:S(2)}) collective-permute-start(bf16[4,8192]{1,0:T(4,128)(2,1)S(1)} %pad_maximum_fusion.8), channel_id=1, source_target_pairs={{0,4},{4,0},{8,12},{12,8},{1,5},{5,1},{9,13},{13,9},{2,6},{6,2},{1... | collective-permute-start | bytes 196616 | tf_op jit(solution)/shard_map/ppermute | solution.py:25
  95.9 7.5 %collective-permute-start.33 = (bf16[4,8192]{1,0:T(4,128)(2,1)S(1)}, bf16[4,8192]{1,0:T(4,128)(2,1)S(1)}, u32[]{:S(2)}, u32[]{:S(2)}) collective-permute-start(bf16[4,8192]{1,0:T(4,128)(2,1)S(1)} %pad_maximum_fusion.9), channel_id=1, source_target_pairs={{0,8},{4,12},{8,0},{12,4},{1,9},{5,13},{9,1},{13,5},{2,10},{6,14},... | collective-permute-start | bytes 196616 | tf_op jit(solution)/shard_map/ppermute | solution.py:25
  98.3 6.2 %collective-permute-start.34 = (bf16[4,8192]{1,0:T(4,128)(2,1)S(1)}, bf16[4,8192]{1,0:T(4,128)(2,1)S(1)}, u32[]{:S(2)}, u32[]{:S(2)}) collective-permute-start(bf16[4,8192]{1,0:T(4,128)(2,1)S(1)} %pad_maximum_fusion.10), channel_id=1, source_target_pairs={{0,12},{4,8},{8,4},{12,0},{1,13},{5,9},{9,5},{13,1},{2,14},{6,10},... | collective-permute-start | bytes 196616 | tf_op jit(solution)/shard_map/ppermute | solution.py:25
